TPU v7x, 128 devices: a whole 4x4x4 slice. The times are simulated.
128 devices in a mesh: rec: 4 (over y), tm: 32 (over z, x, core).
Axes of the slice: x: 4, y: 4, z: 4, core: 2. Of those that a mesh axis runs over, the one named last changes fastest.
Arguments:
- frames: bfloat16 [4, 12288, 768], P('rec', 'tm'), may hold values from -6 to 6
- cotangent: bfloat16 [4, 12288, 768], P('rec', 'tm'), may hold values from -6 to 6
- routes: int32 [4, 12288, 1], P('rec', 'tm'), may hold values from 0 to 127; in each aligned block of 384 rows (0 to 383, 384 to 767, ..., all dimensions but the last counted through in order) at most 4 rows name the same one
- lengths: int32 [4], P('rec'), may hold values from 3072 to 12288, as said below
- conv_weight: float32 [31, 768], replicated, may hold values from -0.875 to 0.875
- norm_gain: float32 [768], replicated, may hold values from 0.25 to 1.75
- expert_in: bfloat16 [128, 768, 3072], P(('rec', 'tm')), may hold values from -0.21875 to 0.21875
- expert_out: bfloat16 [128, 3072, 768], P(('rec', 'tm')), may hold values from -0.109375 to 0.109375
Outputs:
- output: bfloat16 [4, 12288, 768], P('rec', 'tm')
- grad_frames: bfloat16 [4, 12288, 768], P('rec', 'tm')
- grad_conv: float32 [31, 768], replicated
- grad_gain: float32 [768], replicated
- grad_in: bfloat16 [128, 768, 3072], P(('rec', 'tm'))
- grad_out: bfloat16 [128, 3072, 768], P(('rec', 'tm'))
Inputs may be any that keep to these rules, and one draw needn't show every extreme that they name: `routes`: in the rows of one device no expert is named by more than 4 frames. `lengths`: some recording has all 12288 frames valid and another has exactly 3072.
All inputs are finite; a program needn't handle non-finite values.
Results may differ from a plain program's by a relative error of at most 0.006.
Values may be sent and summed in bfloat16 or wider, within the bound.
No kernel may reach another device: no remote copies, remote signals or barrier semaphores. Data moves between devices by JAX's collectives and lax.ppermute only.
A program may use at most 128 MiB of HBM per device.

v0:
```python
import math

import jax
import jax.numpy as jnp
from jax import lax
from jax.sharding import PartitionSpec as P


def extended(cells, sides, width):
    for axis, dim in sides:
        count = lax.axis_size(axis)
        ends = count - 1
        head = lax.slice_in_dim(cells, 0, width, axis=dim)
        tail = lax.slice_in_dim(cells, cells.shape[dim] - width, cells.shape[dim], axis=dim)
        cells = jnp.concatenate(
            [
                lax.ppermute(tail, axis, [(i, (i + 1) % count) for i in range(ends)]),
                cells,
                lax.ppermute(head, axis, [((i + 1) % count, i) for i in range(ends)]),
            ],
            axis=dim,
        )
    return cells


def depthwise(padded, weight, count):
    total = jnp.zeros((count, padded.shape[-1]), jnp.float32)
    for offset in range(weight.shape[0]):
        total = total + weight[offset] * padded[offset : offset + count].astype(jnp.float32)
    return total


def local(frames, cotangent, routes, lengths, conv_weight, norm_gain, expert_in, expert_out):
    frame_rows = frames.shape[1]
    width = frames.shape[2]
    taps_count = conv_weight.shape[0]
    reach = (taps_count - 1) // 2
    n_rec = lax.axis_size("rec")
    n_tm = lax.axis_size("tm")
    devices = n_rec * n_tm
    exp_dev = expert_in.shape[0]
    n_exp = exp_dev * devices
    capacity = max(2, 3 * frame_rows // (2 * n_exp))
    position = lax.axis_index("tm") * frame_rows + jnp.arange(frame_rows, dtype=jnp.int32)
    in_range = (position < lengths[0]).astype(jnp.float32)[:, None]
    masked = frames[0] * in_range.astype(jnp.bfloat16)
    padded = extended(masked, (("tm", 0),), reach)
    conv_out = masked.astype(jnp.float32) + depthwise(padded, conv_weight, frame_rows)
    inv_rms = lax.rsqrt(jnp.mean(conv_out * conv_out, axis=-1, keepdims=True) + 1e-05)
    normed = conv_out * inv_rms
    hidden_in = (normed * norm_gain).astype(jnp.bfloat16)
    grad_rows = cotangent[0] * in_range.astype(jnp.bfloat16)
    expert_ids = routes[0, :, 0]
    onehot = (expert_ids[:, None] == jnp.arange(n_exp, dtype=jnp.int32)[None, :]).astype(jnp.int32)
    slot_index = jnp.sum((jnp.cumsum(onehot, axis=0) - 1) * onehot, axis=1)
    target = expert_ids * capacity + slot_index
    buffer_in = jnp.zeros((n_exp * capacity, width), jnp.bfloat16).at[target].set(hidden_in)
    buffer_grad = jnp.zeros((n_exp * capacity, width), jnp.bfloat16).at[target].set(grad_rows)
    recv_in, recv_grad = (
        lax.all_to_all(
            buffer_in.reshape(n_exp, capacity, width),
            ("rec", "tm"),
            split_axis=0,
            concat_axis=0,
            tiled=True,
        ),
        lax.all_to_all(
            buffer_grad.reshape(n_exp, capacity, width),
            ("rec", "tm"),
            split_axis=0,
            concat_axis=0,
            tiled=True,
        ),
    )
    recv_in = recv_in.reshape(devices, exp_dev, capacity, width)
    recv_grad = recv_grad.reshape(devices, exp_dev, capacity, width)
    pre_act = jnp.einsum("secd,edh->sech", recv_in, expert_in, preferred_element_type=jnp.float32)
    hidden_act = jax.nn.silu(pre_act).astype(jnp.bfloat16)
    result = jnp.einsum(
        "sech,ehd->secd", hidden_act, expert_out, preferred_element_type=jnp.float32
    ).astype(jnp.bfloat16)
    d_act = jnp.einsum("secd,ehd->sech", recv_grad, expert_out, preferred_element_type=jnp.float32)
    sigmoid = jax.nn.sigmoid(pre_act)
    d_pre = (d_act * sigmoid * (1.0 + pre_act * (1.0 - sigmoid))).astype(jnp.bfloat16)
    grad_out = jnp.einsum(
        "sech,secd->ehd", hidden_act, recv_grad, preferred_element_type=jnp.float32
    ).astype(jnp.bfloat16)
    grad_in = jnp.einsum(
        "secd,sech->edh", recv_in, d_pre, preferred_element_type=jnp.float32
    ).astype(jnp.bfloat16)
    d_rows = jnp.einsum(
        "sech,edh->secd", d_pre, expert_in, preferred_element_type=jnp.float32
    ).astype(jnp.bfloat16)
    back_rows, back_grad = (
        lax.all_to_all(
            result.reshape(devices * exp_dev, capacity, width),
            ("rec", "tm"),
            split_axis=0,
            concat_axis=0,
            tiled=True,
        ),
        lax.all_to_all(
            d_rows.reshape(devices * exp_dev, capacity, width),
            ("rec", "tm"),
            split_axis=0,
            concat_axis=0,
            tiled=True,
        ),
    )
    frame_out = back_rows.reshape(n_exp * capacity, width)[target]
    d_hidden = back_grad.reshape(n_exp * capacity, width)[target].astype(jnp.float32)
    output = (conv_out + in_range * frame_out.astype(jnp.float32)).astype(jnp.bfloat16)
    d_normed = d_hidden * norm_gain
    d_conv = cotangent[0].astype(jnp.float32) + inv_rms * (
        d_normed - normed * jnp.mean(d_normed * normed, axis=-1, keepdims=True)
    )
    gain_term = jnp.sum(d_hidden * normed, axis=0)
    taps = []
    for offset in range(taps_count):
        taps.append(
            jnp.sum(d_conv * padded[offset : offset + frame_rows].astype(jnp.float32), axis=0)
        )
    conv_term = jnp.stack(taps)
    d_padded = extended(d_conv, (("tm", 0),), reach)
    d_masked = d_conv + depthwise(d_padded, conv_weight[::-1], frame_rows)
    grad_frames = (in_range * d_masked).astype(jnp.bfloat16)
    conv_total, gain_total = lax.psum((conv_term, gain_term), ("rec", "tm"))
    scale = 1.0 / math.sqrt(n_rec * n_tm * frame_rows)
    return (
        output[None],
        grad_frames[None],
        scale * conv_total,
        scale * gain_total,
        grad_in,
        grad_out,
    )


def solution(mesh):
    placed = (
        P("rec", "tm", None),
        P("rec", "tm", None),
        P("rec", "tm", None),
        P("rec"),
        P(),
        P(),
        P(("rec", "tm"), None, None),
        P(("rec", "tm"), None, None),
    )
    return jax.shard_map(
        local,
        mesh=mesh,
        in_specs=placed,
        out_specs=(
            P("rec", "tm", None),
            P("rec", "tm", None),
            P(),
            P(),
            P(("rec", "tm"), None, None),
            P(("rec", "tm"), None, None),
        ),
        check_vma=False,
    )
```

profile of v0, /device:TPU:1, one launch (start us, length us, event | category | flops | bytes accessed | tf_op | source)
XLA Modules:
  0.0 306.3 jit_solution(15176398160787911903)
XLA Ops:
  7.2 0.0 copy-start.7
  7.2 0.0 copy-start.69
  7.9 1.2 bitcast_multiply_fusion.5
  9.1 4.5 %collective-permute-start = (bf16[15,768]{1,0:T(8,128)(2,1)S(1)}, bf16[15,768]{1,0:T(8,128)(2,1)S(1)}, u32[]{:S(2)}, u32[]{:S(2)}) collective-permute-start(bf16[15,768]{1,0:T(8,128)(2,1)S(1)} %get-tuple-element.76), channel_id=1, source_target_pairs={{0,1},{1,2},{2,3},{3,4},{4,5},{5,6},{6,7},{7,8},{8,9},{9,10},{10,1... | collective-permute-start | bytes 69128 | tf_op jit(solution)/shard_map/ppermute | solution.py:17
  13.6 1.9 collective-permute-start.1
  15.5 0.0 copy-done.7
  15.5 0.2 slice_reduce_fusion.30
  15.9 0.1 slice_reduce_fusion.29
  16.1 0.1 copy.25
  16.3 0.2 fusion.228
  16.5 0.1 add_add_fusion
  16.6 0.0 copy-start.8
  16.6 0.2 fusion.230
  16.9 0.0 collective-permute-done
  16.9 1.9 collective-permute-done.1
  18.8 5.9 %multiply_reduce_fusion = (f32[384]{0:T(512)S(1)}, f32[384,768]{1,0:T(8,128)S(1)}) fusion(bf16[15,768]{1,0:T(8,128)(2,1)S(1)} %collective-permute-done.1, bf16[384,768]{1,0:T(8,128)(2,1)S(1)} %bitcast_multiply_fusion.5, f32[768]{0:T(1024)S(1)} %get-tuple-element.68, f32[768]{0:T(1024)S(1)} %get-tuple-element.69, f32[768]{0:T(1024)S(1)} %get-tuple-element.40, ...), kind=kLoop, calls=%fused_computation.338 | loop fusion | flops 54558336 | bytes 1912320 | tf_op jit(solution)/shard_map/reduce_sum | solution.py:49
  24.6 0.0 copy-done.9
  24.6 0.0 copy-done.11
  25.0 2.5 scatter_custom_fusion
  27.4 1.1 reshape.133
  28.5 11.8 %all-to-all-start = ((bf16[128,4,768]{2,1,0:T(4,128)(2,1)}), bf16[128,4,768]{2,1,0:T(4,128)(2,1)S(1)}, u32[]{:S(2)}, u32[]{:S(2)}) async-start(bf16[128,4,768]{2,1,0:T(4,128)(2,1)} %reshape.133), calls=%async_computation | async-start | bytes 1572864 | tf_op jit(solution)/shard_map/all_to_all | solution.py:60
  40.4 3.2 %scatter_custom_fusion.1 = bf16[512,768]{1,0:T(8,128)(2,1)} fusion(s32[384]{0:T(512)S(1)} %fusion.233, bf16[1,384,768]{2,1,0:T(8,128)(2,1)S(1)} %copy-done.1, bf16[]{:T(256)} %constant.14.clone.1, bf16[384]{0:T(512)(128)(2,1)S(1)} %fusion.234), kind=kCustom, calls=%fused_computation.374 | custom fusion | flops 294912 | bytes 1377282 | tf_op jit(solution)/shard_map/scatter | solution.py:58
  43.5 2.4 reshape.138
  45.9 11.0 %all-to-all-done = bf16[128,4,768]{2,1,0:T(4,128)(2,1)S(1)} async-done(((bf16[128,4,768]{2,1,0:T(4,128)(2,1)}), bf16[128,4,768]{2,1,0:T(4,128)(2,1)S(1)}, u32[]{:S(2)}, u32[]{:S(2)}) %all-to-all-start) | async-done | bytes 786464 | tf_op jit(solution)/shard_map/all_to_all | solution.py:60
  56.9 5.3 %all-to-all-start.2 = ((bf16[128,4,768]{2,1,0:T(4,128)(2,1)}), bf16[128,4,768]{2,1,0:T(4,128)(2,1)}, u32[]{:S(2)}, u32[]{:S(2)}) async-start(bf16[128,4,768]{2,1,0:T(4,128)(2,1)} %reshape.138), calls=%async_computation.2 | async-start | bytes 1572864 | tf_op jit(solution)/shard_map/all_to_all | solution.py:67
  62.2 1.6 copy.31
  63.8 6.9 %fusion.12 = f32[128,4,3072]{2,0,1:T(8,128)} fusion(bf16[128,4,768]{0,2,1:T(8,128)(2,1)S(1)} %copy.31, bf16[1,768,3072]{2,1,0:T(8,128)(2,1)} %param.14), kind=kOutput, calls=%fused_computation.50 | convolution fusion | flops 2415919104 | bytes 11796480 | tf_op jit(solution)/shard_map/secd,edh->sech/dot_general | solution.py:77
  70.7 7.8 %all-to-all-done.2 = bf16[128,4,768]{2,1,0:T(4,128)(2,1)} async-done(((bf16[128,4,768]{2,1,0:T(4,128)(2,1)}), bf16[128,4,768]{2,1,0:T(4,128)(2,1)}, u32[]{:S(2)}, u32[]{:S(2)}) %all-to-all-start.2) | async-done | bytes 786464 | tf_op jit(solution)/shard_map/all_to_all | solution.py:67
  78.6 8.1 %fusion.16 = bf16[128,4,3072]{2,0,1:T(8,128)(2,1)S(1)} fusion(f32[128,4,3072]{2,0,1:T(8,128)} %fusion.12, bf16[1,3072,768]{2,1,0:T(8,128)(2,1)} %param.15, bf16[128,4,768]{2,1,0:T(4,128)(2,1)} %all-to-all-done.2), kind=kOutput, calls=%fused_computation.54 | convolution fusion | flops 2430074880 | bytes 14942208 | tf_op jit(solution)/shard_map/secd,ehd->sech/dot_general | solution.py:82
  86.6 0.0 copy-start.70
  86.6 6.1 %fusion.23 = bf16[128,4,768]{2,0,1:T(8,128)(2,1)S(1)} fusion(bf16[128,4,3072]{2,0,1:T(8,128)(2,1)S(1)} %fusion.16, bf16[1,768,3072]{2,1,0:T(8,128)(2,1)} %param.14), kind=kOutput, calls=%fused_computation.152 | convolution fusion | flops 2416312320 | bytes 8650752 | tf_op jit(solution)/shard_map/sech,edh->secd/dot_general | solution.py:91
  92.8 1.5 copy.30
  94.3 5.3 %all-to-all-start.3 = ((bf16[128,4,768]{2,1,0:T(4,128)(2,1)}), bf16[128,4,768]{2,1,0:T(4,128)(2,1)}, u32[]{:S(2)}, u32[]{:S(2)}) async-start(bf16[128,4,768]{2,1,0:T(4,128)(2,1)} %copy.30), calls=%async_computation.3 | async-start | bytes 1572864 | tf_op jit(solution)/shard_map/all_to_all | solution.py:102
  99.5 7.6 %fusion.26 = bf16[128,4,768]{2,0,1:T(8,128)(2,1)S(1)} fusion(bf16[1,3072,768]{2,1,0:T(8,128)(2,1)} %param.15, f32[128,4,3072]{2,0,1:T(8,128)} %fusion.12), kind=kOutput, calls=%fused_computation.153 | convolution fusion | flops 2424176640 | bytes 11796480 | tf_op jit(solution)/shard_map/sech,ehd->secd/dot_general | solution.py:79
  107.1 1.6 copy.28
  108.7 7.2 %all-to-all-done.3 = bf16[128,4,768]{2,1,0:T(4,128)(2,1)} async-done(((bf16[128,4,768]{2,1,0:T(4,128)(2,1)}), bf16[128,4,768]{2,1,0:T(4,128)(2,1)}, u32[]{:S(2)}, u32[]{:S(2)}) %all-to-all-start.3) | async-done | bytes 786464 | tf_op jit(solution)/shard_map/all_to_all | solution.py:102
  115.9 5.5 %all-to-all-start.1 = ((bf16[128,4,768]{2,1,0:T(4,128)(2,1)}), bf16[128,4,768]{2,1,0:T(4,128)(2,1)}, u32[]{:S(2)}, u32[]{:S(2)}) async-start(bf16[128,4,768]{2,1,0:T(4,128)(2,1)} %copy.28), calls=%async_computation.1 | async-start | bytes 1572864 | tf_op jit(solution)/shard_map/all_to_all | solution.py:95
  121.4 0.0 all-reduce.2.cloned.1.call-start
  121.5 0.0 copy-start.71
  121.5 8.1 %fusion.15 = bf16[1,3072,768]{2,1,0:T(8,128)(2,1)} fusion(f32[128,4,3072]{2,0,1:T(8,128)} %fusion.12, bf16[128,4,768]{2,1,0:T(4,128)(2,1)} %all-to-all-done.2), kind=kOutput, calls=%fused_computation.53 | convolution fusion | flops 2426142720 | bytes 11796480 | tf_op jit(solution)/shard_map/sech,secd->ehd/dot_general | solution.py:85
  129.6 4.2 %fusion.14 = bf16[1,768,3072]{2,1,0:T(8,128)(2,1)} fusion(bf16[128,4,768]{0,2,1:T(8,128)(2,1)S(1)} %copy.31, bf16[128,4,3072]{2,0,1:T(8,128)(2,1)S(1)} %copy-done.71), kind=kOutput, calls=%fused_computation.52 | convolution fusion | flops 2418278400 | bytes 8650752 | tf_op jit(solution)/shard_map/secd,sech->edh/dot_general | solution.py:88
  133.9 1.6 reshape.140
  135.4 2.2 gather_fusion.1
  137.6 0.2 all-to-all-done.1
  137.8 1.6 reshape.137
  139.4 2.6 gather_fusion
  142.0 0.0 copy-start.6
  142.1 3.1 %fusion.94 = (f32[768]{0:T(1024)}, f32[384]{0:T(512)S(1)}, bf16[1,384,768]{2,1,0:T(8,128)(2,1)}) fusion(bf16[384,768]{1,0:T(8,128)(2,1)S(1)} %gather_fusion.1, f32[384,768]{1,0:T(8,128)S(1)} %get-tuple-element.72, f32[384]{0:T(512)S(1)} %add_rsqrt_fusion, f32[768]{0:T(1024)S(1)} %copy-done.8, bf16[384,768]{1,0:T(8,128)(2,1)} %gather_fusion, f32[384]{0:T(512)S(1)} %fusion.232), kind=kLoop, calls=%fused_computation.217 | loop fusion | flops 3242880 | bytes 2959872 | tf_op jit(solution)/shard_map/reduce_sum | solution.py:117
  145.2 5.4 %fusion.93 = (f32[768]{0:T(1024)S(1)}, f32[768]{0:T(1024)S(1)}, f32[768]{0:T(1024)S(1)}, f32[768]{0:T(1024)S(1)}, f32[768]{0:T(1024)S(1)}, /*index=5*/f32[768]{0...) fusion(bf16[15,768]{1,0:T(8,128)(2,1)S(1)} %copy-done.6, ...), kind=kLoop, calls=%fused_computation.216 | loop fusion | flops 18277632 | bytes 4185600 | tf_op jit(solution)/shard_map/reduce_sum | solution.py:121
  150.6 1.4 fusion.92
  152.1 1.5 fusion.73
  153.6 0.0 copy-start.68
  154.0 1.1 fusion.64
  155.3 2.6 stack.127
  157.9 0.0 all-reduce.2.cloned.1.call-update
  157.9 3.3 %collective-permute-start.2 = (f32[15,768]{1,0:T(8,128)S(1)}, f32[15,768]{1,0:T(8,128)S(1)}, u32[]{:S(2)}, u32[]{:S(2)}) collective-permute-start(f32[15,768]{1,0:T(8,128)S(1)} %get-tuple-element.73), channel_id=1, source_target_pairs={{0,1},{1,2},{2,3},{3,4},{4,5},{5,6},{6,7},{7,8},{8,9},{9,10},{10,1... | collective-permute-start | bytes 138248 | tf_op jit(solution)/shard_map/ppermute | solution.py:17
  161.2 1.9 collective-permute-start.3
  163.2 68.4 %psum.15 = f32[768]{0:T(1024)S(1)} all-reduce(f32[768]{0:T(1024)S(1)} %copy-done.68), channel_id=1, replica_groups=mesh['rec'=4,'tm'=32] {'rec','tm'}, use_global_device_ids=true, to_apply=%region_40.41 | all-reduce | flops 768 | bytes 6144 | tf_op jit(solution)/shard_map/psum | solution.py:127
  231.6 0.6 broadcast_multiply_fusion.1
  232.2 0.0 collective-permute-done.2
  232.2 0.0 collective-permute-done.3
  232.5 9.2 %fusion.224 = bf16[1,384,768]{2,1,0:T(8,128)(2,1)} fusion(f32[384,768]{1,0:T(8,128)S(1)} %get-tuple-element.70, f32[15,768]{1,0:T(8,128)S(1)} %collective-permute-done.3, f32[768]{0:T(1024)S(1)} %get-tuple-element.39, f32[768]{0:T(1024)S(1)} %copy-done.42, f32[768]{0:T(1024)S(1)} %copy-done.60, f32[768]{0:T(1024)S(1)} %copy-done.58, f32[768]{0:T(1024)S(1)} %copy-done.56, ...), kind=kLoop, calls=%fused_computation.378 | loop fusion | flops 27721728 | bytes 1958400 | tf_op jit(solution)/shard_map/broadcast_in_dim | solution.py:131
  241.7 56.2 %all-reduce.2.cloned.1.call-done = f32[31,768]{1,0:T(8,128)} async-done(((f32[31,768]{1,0:T(8,128)}), f32[31,768]{1,0:T(8,128)}) %all-reduce.2.cloned.1.call-update) | async-done | bytes 95248 | tf_op jit(solution)/shard_map/psum | solution.py:127
  297.9 1.5 broadcast_multiply_fusion
  (177 shorter events, 0.6 us)
Async XLA Ops:
  7.2 8.8 %copy-start.69 = (s32[1,384,1]{1,2,0:T(1,128)S(1)}, s32[1,384,1]{1,2,0:T(1,128)}, u32[]{:S(2)}) copy-start(s32[1,384,1]{1,2,0:T(1,128)} %param.10) | copy-start | bytes 4612
  9.1 7.8 %collective-permute-start = (bf16[15,768]{1,0:T(8,128)(2,1)S(1)}, bf16[15,768]{1,0:T(8,128)(2,1)S(1)}, u32[]{:S(2)}, u32[]{:S(2)}) collective-permute-start(bf16[15,768]{1,0:T(8,128)(2,1)S(1)} %get-tuple-element.76), channel_id=1, source_target_pairs={{0,1},{1,2},{2,3},{3,4},{4,5},{5,6},{6,7},{7,8},{8,9},{9,10},{10,1... | collective-permute-start | bytes 69128 | tf_op jit(solution)/shard_map/ppermute | solution.py:17
  13.6 5.1 %collective-permute-start.1 = (bf16[15,768]{1,0:T(8,128)(2,1)S(1)}, bf16[15,768]{1,0:T(8,128)(2,1)S(1)}, u32[]{:S(2)}, u32[]{:S(2)}) collective-permute-start(bf16[15,768]{1,0:T(8,128)(2,1)S(1)} %get-tuple-element.77), channel_id=1, source_target_pairs={{1,0},{2,1},{3,2},{4,3},{5,4},{6,5},{7,6},{8,7},{9,8},{10,9},{11,1... | collective-permute-start | bytes 69128 | tf_op jit(solution)/shard_map/ppermute | solution.py:19
  15.7 8.9 %copy-start.9 = (f32[768]{0:T(1024)}, f32[768]{0:T(1024)S(1)}, u32[]{:S(2)}) copy-start(f32[768]{0:T(1024)S(1)} %get-tuple-element.42) | copy-start | bytes 9220
  15.7 8.9 %copy-start.11 = (f32[768]{0:T(1024)}, f32[768]{0:T(1024)S(1)}, u32[]{:S(2)}) copy-start(f32[768]{0:T(1024)S(1)} %get-tuple-element.43) | copy-start | bytes 9220
  15.7 8.9 %copy-start.13 = (f32[768]{0:T(1024)}, f32[768]{0:T(1024)S(1)}, u32[]{:S(2)}) copy-start(f32[768]{0:T(1024)S(1)} %get-tuple-element.44) | copy-start | bytes 9220
  15.7 8.9 %copy-start.15 = (f32[768]{0:T(1024)}, f32[768]{0:T(1024)S(1)}, u32[]{:S(2)}) copy-start(f32[768]{0:T(1024)S(1)} %get-tuple-element.45) | copy-start | bytes 9220
  15.8 8.9 %copy-start.17 = (f32[768]{0:T(1024)}, f32[768]{0:T(1024)S(1)}, u32[]{:S(2)}) copy-start(f32[768]{0:T(1024)S(1)} %get-tuple-element.46) | copy-start | bytes 9220
  15.8 8.9 %copy-start.19 = (f32[768]{0:T(1024)}, f32[768]{0:T(1024)S(1)}, u32[]{:S(2)}) copy-start(f32[768]{0:T(1024)S(1)} %get-tuple-element.47) | copy-start | bytes 9220
  15.8 8.9 %copy-start.21 = (f32[768]{0:T(1024)}, f32[768]{0:T(1024)S(1)}, u32[]{:S(2)}) copy-start(f32[768]{0:T(1024)S(1)} %get-tuple-element.48) | copy-start | bytes 9220
  15.8 8.9 %copy-start.23 = (f32[768]{0:T(1024)}, f32[768]{0:T(1024)S(1)}, u32[]{:S(2)}) copy-start(f32[768]{0:T(1024)S(1)} %get-tuple-element.49) | copy-start | bytes 9220
  15.8 8.9 %copy-start.25 = (f32[768]{0:T(1024)}, f32[768]{0:T(1024)S(1)}, u32[]{:S(2)}) copy-start(f32[768]{0:T(1024)S(1)} %get-tuple-element.50) | copy-start | bytes 9220
  15.8 8.9 %copy-start.27 = (f32[768]{0:T(1024)}, f32[768]{0:T(1024)S(1)}, u32[]{:S(2)}) copy-start(f32[768]{0:T(1024)S(1)} %get-tuple-element.51) | copy-start | bytes 9220
  15.8 8.9 %copy-start.29 = (f32[768]{0:T(1024)}, f32[768]{0:T(1024)S(1)}, u32[]{:S(2)}) copy-start(f32[768]{0:T(1024)S(1)} %get-tuple-element.52) | copy-start | bytes 9220
  15.8 8.9 %copy-start.31 = (f32[768]{0:T(1024)}, f32[768]{0:T(1024)S(1)}, u32[]{:S(2)}) copy-start(f32[768]{0:T(1024)S(1)} %get-tuple-element.53) | copy-start | bytes 9220
  15.8 8.9 %copy-start.33 = (f32[768]{0:T(1024)}, f32[768]{0:T(1024)S(1)}, u32[]{:S(2)}) copy-start(f32[768]{0:T(1024)S(1)} %get-tuple-element.54) | copy-start | bytes 9220
  15.8 8.9 %copy-start.35 = (f32[768]{0:T(1024)}, f32[768]{0:T(1024)S(1)}, u32[]{:S(2)}) copy-start(f32[768]{0:T(1024)S(1)} %get-tuple-element.55) | copy-start | bytes 9220
  15.9 8.9 %copy-start.37 = (f32[768]{0:T(1024)}, f32[768]{0:T(1024)S(1)}, u32[]{:S(2)}) copy-start(f32[768]{0:T(1024)S(1)} %get-tuple-element.56) | copy-start | bytes 9220
  15.9 8.9 %copy-start.39 = (f32[768]{0:T(1024)}, f32[768]{0:T(1024)S(1)}, u32[]{:S(2)}) copy-start(f32[768]{0:T(1024)S(1)} %get-tuple-element.57) | copy-start | bytes 9220
  16.0 8.8 %copy-start.41 = (f32[768]{0:T(1024)}, f32[768]{0:T(1024)S(1)}, u32[]{:S(2)}) copy-start(f32[768]{0:T(1024)S(1)} %get-tuple-element.58) | copy-start | bytes 9220
  16.0 8.8 %copy-start.43 = (f32[768]{0:T(1024)}, f32[768]{0:T(1024)S(1)}, u32[]{:S(2)}) copy-start(f32[768]{0:T(1024)S(1)} %get-tuple-element.59) | copy-start | bytes 9220
  16.0 8.8 %copy-start.45 = (f32[768]{0:T(1024)}, f32[768]{0:T(1024)S(1)}, u32[]{:S(2)}) copy-start(f32[768]{0:T(1024)S(1)} %get-tuple-element.60) | copy-start | bytes 9220
  16.0 8.8 %copy-start.47 = (f32[768]{0:T(1024)}, f32[768]{0:T(1024)S(1)}, u32[]{:S(2)}) copy-start(f32[768]{0:T(1024)S(1)} %get-tuple-element.61) | copy-start | bytes 9220
  16.0 8.8 %copy-start.49 = (f32[768]{0:T(1024)}, f32[768]{0:T(1024)S(1)}, u32[]{:S(2)}) copy-start(f32[768]{0:T(1024)S(1)} %get-tuple-element.62) | copy-start | bytes 9220
  25.0 117.1 %copy-start.65 = (f32[384]{0:T(512)}, f32[384]{0:T(512)S(1)}, u32[]{:S(2)}) copy-start(f32[384]{0:T(512)S(1)} %add_rsqrt_fusion) | copy-start | bytes 4612
  28.5 11.8 %copy-start.1 = (bf16[1,384,768]{2,1,0:T(8,128)(2,1)S(1)}, bf16[1,384,768]{2,1,0:T(8,128)(2,1)}, u32[]{:S(2)}) copy-start(bf16[1,384,768]{2,1,0:T(8,128)(2,1)} %param.9) | copy-start | bytes 1769476
  28.5 28.4 %all-to-all-start = ((bf16[128,4,768]{2,1,0:T(4,128)(2,1)}), bf16[128,4,768]{2,1,0:T(4,128)(2,1)S(1)}, u32[]{:S(2)}, u32[]{:S(2)}) async-start(bf16[128,4,768]{2,1,0:T(4,128)(2,1)} %reshape.133), calls=%async_computation | async-start | bytes 1572864 | tf_op jit(solution)/shard_map/all_to_all | solution.py:60
  56.9 21.7 %all-to-all-start.2 = ((bf16[128,4,768]{2,1,0:T(4,128)(2,1)}), bf16[128,4,768]{2,1,0:T(4,128)(2,1)}, u32[]{:S(2)}, u32[]{:S(2)}) async-start(bf16[128,4,768]{2,1,0:T(4,128)(2,1)} %reshape.138), calls=%async_computation.2 | async-start | bytes 1572864 | tf_op jit(solution)/shard_map/all_to_all | solution.py:67
  62.2 79.8 %copy-start.66 = (f32[384]{0:T(512)}, f32[384]{0:T(512)S(1)}, u32[]{:S(2)}) copy-start(f32[384]{0:T(512)S(1)} %fusion.232) | copy-start | bytes 4612
  94.3 21.7 %all-to-all-start.3 = ((bf16[128,4,768]{2,1,0:T(4,128)(2,1)}), bf16[128,4,768]{2,1,0:T(4,128)(2,1)}, u32[]{:S(2)}, u32[]{:S(2)}) async-start(bf16[128,4,768]{2,1,0:T(4,128)(2,1)} %copy.30), calls=%async_computation.3 | async-start | bytes 1572864 | tf_op jit(solution)/shard_map/all_to_all | solution.py:102
  115.9 21.9 %all-to-all-start.1 = ((bf16[128,4,768]{2,1,0:T(4,128)(2,1)}), bf16[128,4,768]{2,1,0:T(4,128)(2,1)}, u32[]{:S(2)}, u32[]{:S(2)}) async-start(bf16[128,4,768]{2,1,0:T(4,128)(2,1)} %copy.28), calls=%async_computation.1 | async-start | bytes 1572864 | tf_op jit(solution)/shard_map/all_to_all | solution.py:95
  121.4 176.4 %all-reduce.2.cloned.1.call-start = ((), (), s32[]{:S(2)}) async-start(), calls=%async_computation.4 | async-start | bytes 196608 | tf_op jit(solution)/shard_map/psum | solution.py:127
  153.6 9.5 %copy-start.68 = (f32[768]{0:T(1024)S(1)}, f32[768]{0:T(1024)}, u32[]{:S(2)}) copy-start(f32[768]{0:T(1024)} %get-tuple-element.36) | copy-start | bytes 9220
  153.6 78.6 %copy-start.10 = (f32[768]{0:T(1024)S(1)}, f32[768]{0:T(1024)}, u32[]{:S(2)}) copy-start(f32[768]{0:T(1024)} %copy-done.9) | copy-start | bytes 9220
  153.7 78.6 %copy-start.12 = (f32[768]{0:T(1024)S(1)}, f32[768]{0:T(1024)}, u32[]{:S(2)}) copy-start(f32[768]{0:T(1024)} %copy-done.11) | copy-start | bytes 9220
  153.7 78.6 %copy-start.14 = (f32[768]{0:T(1024)S(1)}, f32[768]{0:T(1024)}, u32[]{:S(2)}) copy-start(f32[768]{0:T(1024)} %copy-done.13) | copy-start | bytes 9220
  153.7 78.6 %copy-start.16 = (f32[768]{0:T(1024)S(1)}, f32[768]{0:T(1024)}, u32[]{:S(2)}) copy-start(f32[768]{0:T(1024)} %copy-done.15) | copy-start | bytes 9220
  153.7 78.6 %copy-start.18 = (f32[768]{0:T(1024)S(1)}, f32[768]{0:T(1024)}, u32[]{:S(2)}) copy-start(f32[768]{0:T(1024)} %copy-done.17) | copy-start | bytes 9220
  153.7 78.6 %copy-start.20 = (f32[768]{0:T(1024)S(1)}, f32[768]{0:T(1024)}, u32[]{:S(2)}) copy-start(f32[768]{0:T(1024)} %copy-done.19) | copy-start | bytes 9220
  153.7 78.6 %copy-start.22 = (f32[768]{0:T(1024)S(1)}, f32[768]{0:T(1024)}, u32[]{:S(2)}) copy-start(f32[768]{0:T(1024)} %copy-done.21) | copy-start | bytes 9220
  153.7 78.6 %copy-start.24 = (f32[768]{0:T(1024)S(1)}, f32[768]{0:T(1024)}, u32[]{:S(2)}) copy-start(f32[768]{0:T(1024)} %copy-done.23) | copy-start | bytes 9220
  153.7 78.6 %copy-start.26 = (f32[768]{0:T(1024)S(1)}, f32[768]{0:T(1024)}, u32[]{:S(2)}) copy-start(f32[768]{0:T(1024)} %copy-done.25) | copy-start | bytes 9220
  153.7 78.6 %copy-start.28 = (f32[768]{0:T(1024)S(1)}, f32[768]{0:T(1024)}, u32[]{:S(2)}) copy-start(f32[768]{0:T(1024)} %copy-done.27) | copy-start | bytes 9220
  153.7 78.6 %copy-start.30 = (f32[768]{0:T(1024)S(1)}, f32[768]{0:T(1024)}, u32[]{:S(2)}) copy-start(f32[768]{0:T(1024)} %copy-done.29) | copy-start | bytes 9220
  153.8 78.6 %copy-start.32 = (f32[768]{0:T(1024)S(1)}, f32[768]{0:T(1024)}, u32[]{:S(2)}) copy-start(f32[768]{0:T(1024)} %copy-done.31) | copy-start | bytes 9220
  153.8 78.6 %copy-start.34 = (f32[768]{0:T(1024)S(1)}, f32[768]{0:T(1024)}, u32[]{:S(2)}) copy-start(f32[768]{0:T(1024)} %copy-done.33) | copy-start | bytes 9220
  153.8 78.6 %copy-start.36 = (f32[768]{0:T(1024)S(1)}, f32[768]{0:T(1024)}, u32[]{:S(2)}) copy-start(f32[768]{0:T(1024)} %copy-done.35) | copy-start | bytes 9220
  153.8 78.6 %copy-start.38 = (f32[768]{0:T(1024)S(1)}, f32[768]{0:T(1024)}, u32[]{:S(2)}) copy-start(f32[768]{0:T(1024)} %copy-done.37) | copy-start | bytes 9220
  153.8 78.6 %copy-start.40 = (f32[768]{0:T(1024)S(1)}, f32[768]{0:T(1024)}, u32[]{:S(2)}) copy-start(f32[768]{0:T(1024)} %copy-done.39) | copy-start | bytes 9220
  153.8 78.6 %copy-start.42 = (f32[768]{0:T(1024)S(1)}, f32[768]{0:T(1024)}, u32[]{:S(2)}) copy-start(f32[768]{0:T(1024)} %copy-done.41) | copy-start | bytes 9220
  153.8 78.6 %copy-start.44 = (f32[768]{0:T(1024)S(1)}, f32[768]{0:T(1024)}, u32[]{:S(2)}) copy-start(f32[768]{0:T(1024)} %copy-done.43) | copy-start | bytes 9220
  153.8 78.6 %copy-start.46 = (f32[768]{0:T(1024)S(1)}, f32[768]{0:T(1024)}, u32[]{:S(2)}) copy-start(f32[768]{0:T(1024)} %copy-done.45) | copy-start | bytes 9220
  153.8 78.6 %copy-start.48 = (f32[768]{0:T(1024)S(1)}, f32[768]{0:T(1024)}, u32[]{:S(2)}) copy-start(f32[768]{0:T(1024)} %copy-done.47) | copy-start | bytes 9220
  153.8 78.6 %copy-start.50 = (f32[768]{0:T(1024)S(1)}, f32[768]{0:T(1024)}, u32[]{:S(2)}) copy-start(f32[768]{0:T(1024)} %copy-done.49) | copy-start | bytes 9220
  153.9 78.6 %copy-start.52 = (f32[768]{0:T(1024)S(1)}, f32[768]{0:T(1024)}, u32[]{:S(2)}) copy-start(f32[768]{0:T(1024)} %copy-done.51) | copy-start | bytes 9220
  153.9 78.6 %copy-start.54 = (f32[768]{0:T(1024)S(1)}, f32[768]{0:T(1024)}, u32[]{:S(2)}) copy-start(f32[768]{0:T(1024)} %copy-done.53) | copy-start | bytes 9220
  153.9 78.6 %copy-start.56 = (f32[768]{0:T(1024)S(1)}, f32[768]{0:T(1024)}, u32[]{:S(2)}) copy-start(f32[768]{0:T(1024)} %copy-done.55) | copy-start | bytes 9220
  153.9 78.6 %copy-start.58 = (f32[768]{0:T(1024)S(1)}, f32[768]{0:T(1024)}, u32[]{:S(2)}) copy-start(f32[768]{0:T(1024)} %copy-done.57) | copy-start | bytes 9220
  153.9 78.6 %copy-start.60 = (f32[768]{0:T(1024)S(1)}, f32[768]{0:T(1024)}, u32[]{:S(2)}) copy-start(f32[768]{0:T(1024)} %copy-done.59) | copy-start | bytes 9220
  153.9 78.6 %copy-start.62 = (f32[768]{0:T(1024)S(1)}, f32[768]{0:T(1024)}, u32[]{:S(2)}) copy-start(f32[768]{0:T(1024)} %copy-done.61) | copy-start | bytes 9220
  153.9 78.6 %copy-start.64 = (f32[768]{0:T(1024)S(1)}, f32[768]{0:T(1024)}, u32[]{:S(2)}) copy-start(f32[768]{0:T(1024)} %copy-done.63) | copy-start | bytes 9220
  153.9 78.6 %copy-start.67 = (f32[384]{0:T(512)S(1)}, f32[384]{0:T(512)}, u32[]{:S(2)}) copy-start(f32[384]{0:T(512)} %copy-done.66) | copy-start | bytes 4612
  157.9 74.3 %collective-permute-start.2 = (f32[15,768]{1,0:T(8,128)S(1)}, f32[15,768]{1,0:T(8,128)S(1)}, u32[]{:S(2)}, u32[]{:S(2)}) collective-permute-start(f32[15,768]{1,0:T(8,128)S(1)} %get-tuple-element.73), channel_id=1, source_target_pairs={{0,1},{1,2},{2,3},{3,4},{4,5},{5,6},{6,7},{7,8},{8,9},{9,10},{10,1... | collective-permute-start | bytes 138248 | tf_op jit(solution)/shard_map/ppermute | solution.py:17
  161.2 71.0 %collective-permute-start.3 = (f32[15,768]{1,0:T(8,128)S(1)}, f32[15,768]{1,0:T(8,128)S(1)}, u32[]{:S(2)}, u32[]{:S(2)}) collective-permute-start(f32[15,768]{1,0:T(8,128)S(1)} %get-tuple-element.74), channel_id=1, source_target_pairs={{1,0},{2,1},{3,2},{4,3},{5,4},{6,5},{7,6},{8,7},{9,8},{10,9},{11,1... | collective-permute-start | bytes 138248 | tf_op jit(solution)/shard_map/ppermute | solution.py:19
  (17 other events, 120.0 us)
Sparse Core Ops, SparseCore 0:
  158.0 139.8 all-reduce.1
where the time goes:
time: 307 us; the launch traced here: 306 us
  waiting for transfers between devices  84.4 us (27%)
  blocking collectives  68.4 us (22%)
  matrix products  41 us (13%)
  starting transfers between devices  39.7 us (13%)
  other arithmetic  37.1 us (12%)
  local copies, waits for them, and re-layouts  19.4 us (6%)
  between operations  16.3 us (5%)
    psum x1, blocking collectives, local(): conv_total, gain_total = lax.psum((conv_term, gain_term), ('rec', 'tm'))  68.4 us
    psum x1, waiting for transfers between devices, local(): conv_total, gain_total = lax.psum((conv_term, gain_term), ('rec', 'tm'))  56.2 us
    all_to_all x1, starting transfers between devices, local(): lax.all_to_all(buffer_in.reshape(n_exp, capacity, width), ('rec', 'tm'),...  11.8 us
    all_to_all x1, waiting for transfers between devices, local(): lax.all_to_all(buffer_in.reshape(n_exp, capacity, width), ('rec', 'tm'),...  11 us
    reduce_sum x4, other arithmetic, local(): jnp.sum(d_conv * padded[offset:offset + frame_rows].astype(jnp.float32),...  9.35 us
    broadcast_in_dim x1, other arithmetic, local(): grad_frames[None]  9.22 us
    dot_general x1, matrix products, local(): jnp.einsum('sech,secd->ehd', hidden_act, recv_grad, preferred_element_typ...  8.13 us
    dot_general x1, matrix products, local(): jnp.einsum('secd,ehd->sech', recv_grad, expert_out, preferred_element_typ...  8.06 us
  transfers between devices with their start and end apart: 9, of which 6 were waited for; matrix products, arithmetic and copies ran while one was open for 16% of the time, Pallas kernels for 0%

commit v1 on v0

v1 whole, which is shorter than its diff:
```python
import math

import jax
import jax.numpy as jnp
from jax import lax
from jax.experimental import pallas as pl
from jax.experimental.pallas import tpu as pltpu
from jax.sharding import PartitionSpec as P

LANES = 128
EDGE = 16
ROWS = 64
SLOTS = 4
PAIR = 2 * SLOTS
VMEM = pl.BlockSpec(memory_space=pltpu.VMEM)
SMEM = pl.BlockSpec(memory_space=pltpu.SMEM)
BIG = pltpu.CompilerParams(vmem_limit_bytes=48 * 1024 * 1024)


def f32(x):
    return x.astype(jnp.float32)


def bf16(x):
    return x.astype(jnp.bfloat16)


def dot(a, b, dims=((1,), (0,))):
    return lax.dot_general(a, b, (dims, ((), ())), preferred_element_type=jnp.float32)


def iota(shape, axis):
    return lax.broadcasted_iota(jnp.int32, shape, axis)


def cost(flops, nbytes):
    return pl.CostEstimate(flops=flops, bytes_accessed=nbytes, transcendentals=0)


def pre_kernel(
    nv_ref, col_ref, row_ref, x_ref, left_ref, right_ref, cot_ref, w_ref, gain_ref,
    send_ref, conv_ref, inv_ref, pad_ref,
    stack, taps, squares,
):
    count, width = x_ref.shape
    chunks = width // LANES
    reach = (w_ref.shape[0] - 1) // 2
    valid = nv_ref[0]
    edge = iota((EDGE, LANES), 0)
    inside = iota((count, LANES), 0) < valid
    for c in range(chunks):
        lanes = slice(c * LANES, (c + 1) * LANES)
        pad_ref[c, 0:EDGE, :] = jnp.where(edge - EDGE < valid, f32(left_ref[:, lanes]), 0.0)
        pad_ref[c, EDGE : EDGE + count, :] = jnp.where(inside, f32(x_ref[:, lanes]), 0.0)
        pad_ref[c, EDGE + count :, :] = jnp.where(edge + count < valid, f32(right_ref[:, lanes]), 0.0)
        taps[c, 0 : w_ref.shape[0], :] = w_ref[:, lanes]
        stack[count:, lanes] = bf16(jnp.where(inside, f32(cot_ref[:, lanes]), 0.0))
    squares[...] = jnp.zeros_like(squares)

    @pl.loop(0, chunks)
    def _(c):
        for start in range(0, count, ROWS):
            total = jnp.zeros((ROWS, LANES), jnp.float32)
            for k in range(w_ref.shape[0]):
                at = start + k + EDGE - reach
                total = total + taps[c, k : k + 1, :] * pad_ref[c, at : at + ROWS, :]
            total = pad_ref[c, EDGE + start : EDGE + start + ROWS, :] + total
            conv_ref[c, start : start + ROWS, :] = total
            squares[start : start + ROWS, :] += total * total

    inv = lax.rsqrt(jnp.sum(squares[...], axis=-1, keepdims=True) * (1.0 / width) + 1e-05)
    inv = jnp.broadcast_to(inv, (count, LANES))
    inv_ref[...] = inv
    for c in range(chunks):
        lanes = slice(c * LANES, (c + 1) * LANES)
        stack[0:count, lanes] = bf16(conv_ref[c] * inv * gain_ref[:, lanes])

    earlier = (col_ref[...] == row_ref[...]) & (iota((count, count), 0) < iota((count, count), 1))
    slot = jnp.sum(jnp.where(earlier, 1.0, 0.0), axis=0, keepdims=True).astype(jnp.int32)
    key = row_ref[...] * PAIR + slot
    key = jnp.concatenate([key, key + SLOTS], axis=1)
    block = 256
    for start in range(0, send_ref.shape[0], block):
        pick = bf16(jnp.where(iota((block, 2 * count), 0) + start == key, 1.0, 0.0))
        send_ref[start : start + block, :] = bf16(dot(pick, stack[...]))


def expert_kernel(recv_ref, win_ref, wout_ref, back_ref, x_ref, g_ref, act_ref, dpre_ref):
    rows, width = x_ref.shape
    hidden = win_ref.shape[1]
    half, whole = 128, 256
    i, r = iota((half, whole), 0), iota((half, whole), 1)
    place = (i // SLOTS) * PAIR + i % SLOTS
    pick_x = bf16(jnp.where(r == place, 1.0, 0.0))
    pick_g = bf16(jnp.where(r == place + SLOTS, 1.0, 0.0))
    for n in range(rows // half):
        part = recv_ref[n * whole : (n + 1) * whole, :]
        x_ref[n * half : (n + 1) * half, :] = bf16(dot(pick_x, part))
        g_ref[n * half : (n + 1) * half, :] = bf16(dot(pick_g, part))
    result = jnp.zeros((rows, width), jnp.float32)
    d_rows = jnp.zeros((rows, width), jnp.float32)
    tile = 512
    for start in range(0, hidden, tile):
        cols = slice(start, start + tile)
        pre = dot(x_ref[...], win_ref[:, cols])
        d_act = dot(g_ref[...], wout_ref[cols, :], ((1,), (1,)))
        gate = jax.nn.sigmoid(pre)
        act = bf16(pre * gate)
        d_pre = bf16(d_act * gate * (1.0 + pre * (1.0 - gate)))
        act_ref[:, cols] = act
        dpre_ref[:, cols] = d_pre
        result = result + dot(act, wout_ref[cols, :])
        d_rows = d_rows + dot(d_pre, win_ref[:, cols], ((1,), (1,)))
    result, d_rows = bf16(result), bf16(d_rows)
    q, j = iota((whole, half), 0), iota((whole, half), 1)
    home = (j // SLOTS) * PAIR + j % SLOTS
    put_x = bf16(jnp.where(q == home, 1.0, 0.0))
    put_g = bf16(jnp.where(q == home + SLOTS, 1.0, 0.0))
    for n in range(rows // half):
        part = slice(n * half, (n + 1) * half)
        back_ref[n * whole : (n + 1) * whole, :] = bf16(
            dot(put_x, result[part, :]) + dot(put_g, d_rows[part, :])
        )


def grads_kernel(x_ref, g_ref, act_ref, dpre_ref, gin_ref, gout_ref):
    gin_ref[0] = bf16(dot(x_ref[...], dpre_ref[...], ((0,), (0,))))
    gout_ref[0] = bf16(dot(act_ref[...], g_ref[...], ((0,), (0,))))


def post_kernel(
    nv_ref, col_ref, row_ref, recv_ref, conv_ref, inv_ref, pad_ref, cot_ref, gain_ref,
    out_ref, dconv_ref, head_ref, tail_ref, sums_ref,
    back, dhid, means,
):
    count, width = cot_ref.shape
    chunks = width // LANES
    kernel = sums_ref.shape[0] - 1
    reach = (kernel - 1) // 2
    earlier = (col_ref[...] == row_ref[...]) & (iota((count, count), 1) < iota((count, count), 0))
    slot = jnp.sum(jnp.where(earlier, 1.0, 0.0), axis=1, keepdims=True).astype(jnp.int32)
    key = col_ref[...] * PAIR + slot
    seats = iota((count, recv_ref.shape[0]), 1)
    dhid[...] = dot(bf16(jnp.where(seats == key + SLOTS, 1.0, 0.0)), recv_ref[...])
    back[...] = dot(bf16(jnp.where(seats == key, 1.0, 0.0)), recv_ref[...])
    inside = iota((count, LANES), 0) < nv_ref[0]
    inv = inv_ref[...]
    means[...] = jnp.zeros_like(means)
    for c in range(chunks):
        lanes = slice(c * LANES, (c + 1) * LANES)
        normed = conv_ref[c] * inv
        d_hidden = dhid[:, lanes]
        means[...] += d_hidden * gain_ref[:, lanes] * normed
        sums_ref[kernel : kernel + 1, lanes] = jnp.sum(d_hidden * normed, axis=0, keepdims=True)
        out_ref[:, lanes] = bf16(conv_ref[c] + jnp.where(inside, back[:, lanes], 0.0))
    mean = jnp.sum(means[...], axis=-1, keepdims=True) * (1.0 / width)
    mean = jnp.broadcast_to(mean, (count, LANES))
    for c in range(chunks):
        lanes = slice(c * LANES, (c + 1) * LANES)
        d_conv = f32(cot_ref[:, lanes]) + inv * (
            dhid[:, lanes] * gain_ref[:, lanes] - conv_ref[c] * inv * mean
        )
        dconv_ref[c] = d_conv
        head_ref[c] = d_conv[0:EDGE, :]
        tail_ref[c] = d_conv[count - EDGE :, :]
    for c in range(chunks):
        lanes = slice(c * LANES, (c + 1) * LANES)
        totals = [jnp.zeros((8, LANES), jnp.float32) for _ in range(kernel)]
        for start in range(0, count, ROWS):
            part = dconv_ref[c, start : start + ROWS, :]
            for k in range(kernel):
                at = start + k + EDGE - reach
                product = part * pad_ref[c, at : at + ROWS, :]
                totals[k] = totals[k] + jnp.sum(product.reshape(ROWS // 8, 8, LANES), axis=0)
        for k in range(kernel):
            sums_ref[k : k + 1, lanes] = jnp.sum(totals[k], axis=0, keepdims=True)


def back_kernel(nv_ref, dconv_ref, left_ref, right_ref, w_ref, grad_ref, pad, taps):
    chunks, count, _ = dconv_ref.shape
    kernel = w_ref.shape[0]
    reach = (kernel - 1) // 2
    for c in range(chunks):
        pad[c, 0:EDGE, :] = left_ref[c]
        pad[c, EDGE : EDGE + count, :] = dconv_ref[c]
        pad[c, EDGE + count :, :] = right_ref[c]
    valid = nv_ref[0]
    for c in range(chunks):
        lanes = slice(c * LANES, (c + 1) * LANES)
        for start in range(0, count, ROWS):
            total = jnp.zeros((ROWS, LANES), jnp.float32)
            for k in range(kernel):
                at = start + EDGE + reach - k
                total = total + w_ref[k : k + 1, lanes] * pad[c, at : at + ROWS, :]
            total = pad[c, EDGE + start : EDGE + start + ROWS, :] + total
            keep = iota((ROWS, LANES), 0) + start < valid
            grad_ref[start : start + ROWS, lanes] = bf16(jnp.where(keep, total, 0.0))


def ring_sum(part, axis, pairs_of):
    one, two, three = (lax.ppermute(part, axis, pairs_of(flip)) for flip in (1, 2, 3))
    return (part + one) + (two + three)


def total_over_all(sums):
    rows = sums.shape[0] // 2
    n_tm = lax.axis_size("tm")
    core = lax.axis_index("tm") % 2
    swap = [(i, i ^ 1) for i in range(n_tm)]
    mine = lax.dynamic_slice_in_dim(sums, core * rows, rows, 0)
    other = lax.dynamic_slice_in_dim(sums, (1 - core) * rows, rows, 0)
    part = mine + lax.ppermute(other, "tm", swap)
    part = ring_sum(part, "tm", lambda f: [(i, i ^ (2 * f)) for i in range(n_tm)])
    part = ring_sum(part, "rec", lambda f: [(i, i ^ f) for i in range(4)])
    part = ring_sum(part, "tm", lambda f: [(i, i ^ (8 * f)) for i in range(n_tm)])
    part = part * (1.0 / math.sqrt(lax.axis_size("rec") * n_tm * 384))
    fellow = lax.ppermute(part, "tm", swap)
    low = jnp.where(core == 0, part, fellow)
    high = jnp.where(core == 0, fellow, part)
    return jnp.concatenate([low, high], axis=0)


def shifted(tail, head):
    n = lax.axis_size("tm")
    left = lax.ppermute(tail, "tm", [(i, i + 1) for i in range(n - 1)])
    right = lax.ppermute(head, "tm", [(i + 1, i) for i in range(n - 1)])
    return left, right


def local(frames, cotangent, routes, lengths, conv_weight, norm_gain, expert_in, expert_out):
    count, width = frames.shape[1:]
    kernel = conv_weight.shape[0]
    chunks = width // LANES
    devices = lax.axis_size("rec") * lax.axis_size("tm")
    hidden = expert_in.shape[2]
    rows = devices * SLOTS
    x, cot = frames[0], cotangent[0]
    win, wout = expert_in[0], expert_out[0]
    gain = norm_gain[None, :]
    valid = lengths - lax.axis_index("tm") * count
    col, row = routes[0], routes[0].reshape(1, count)
    left, right = shifted(x[count - EDGE :], x[:EDGE])
    shape = jax.ShapeDtypeStruct
    wide = shape((chunks, count, LANES), jnp.float32)
    send, conv, inv, pad = pl.pallas_call(
        pre_kernel,
        out_shape=[
            shape((2 * rows, width), jnp.bfloat16),
            wide,
            shape((count, LANES), jnp.float32),
            shape((chunks, count + 2 * EDGE, LANES), jnp.float32),
        ],
        in_specs=[SMEM] + [VMEM] * 8,
        out_specs=[VMEM] * 4,
        scratch_shapes=[
            pltpu.VMEM((2 * count, width), jnp.bfloat16),
            pltpu.VMEM((chunks, 32, LANES), jnp.float32),
            pltpu.VMEM((count, LANES), jnp.float32),
        ],
        compiler_params=BIG,
        cost_estimate=cost(10**9, 10**7),
        name="pre",
    )(valid, col, row, x, left, right, cot, conv_weight, gain)
    recv = lax.all_to_all(send, ("rec", "tm"), split_axis=0, concat_axis=0, tiled=True)
    back, rows_x, rows_g, act, d_pre = pl.pallas_call(
        expert_kernel,
        out_shape=[
            shape((2 * rows, width), jnp.bfloat16),
            shape((rows, width), jnp.bfloat16),
            shape((rows, width), jnp.bfloat16),
            shape((rows, hidden), jnp.bfloat16),
            shape((rows, hidden), jnp.bfloat16),
        ],
        in_specs=[VMEM] * 3,
        out_specs=[VMEM] * 5,
        compiler_params=BIG,
        cost_estimate=cost(8 * rows * width * hidden, 2 * 10**7),
        name="experts",
    )(recv, win, wout)
    home = lax.all_to_all(back, ("rec", "tm"), split_axis=0, concat_axis=0, tiled=True)
    tile = 512
    grad_in, grad_out = pl.pallas_call(
        grads_kernel,
        grid=(hidden // tile,),
        out_shape=[
            shape((1, width, hidden), jnp.bfloat16),
            shape((1, hidden, width), jnp.bfloat16),
        ],
        in_specs=[
            pl.BlockSpec((rows, width), lambda i: (0, 0)),
            pl.BlockSpec((rows, width), lambda i: (0, 0)),
            pl.BlockSpec((rows, tile), lambda i: (0, i)),
            pl.BlockSpec((rows, tile), lambda i: (0, i)),
        ],
        out_specs=[
            pl.BlockSpec((1, width, tile), lambda i: (0, 0, i)),
            pl.BlockSpec((1, tile, width), lambda i: (0, i, 0)),
        ],
        compiler_params=BIG,
        cost_estimate=cost(4 * rows * width * hidden, 2 * 10**7),
        name="weight_grads",
    )(rows_x, rows_g, act, d_pre)
    output, d_conv, head, tail, sums = pl.pallas_call(
        post_kernel,
        out_shape=[
            shape((count, width), jnp.bfloat16),
            wide,
            shape((chunks, EDGE, LANES), jnp.float32),
            shape((chunks, EDGE, LANES), jnp.float32),
            shape((kernel + 1, width), jnp.float32),
        ],
        in_specs=[SMEM] + [VMEM] * 8,
        out_specs=[VMEM] * 5,
        scratch_shapes=[
            pltpu.VMEM((count, width), jnp.float32),
            pltpu.VMEM((count, width), jnp.float32),
            pltpu.VMEM((count, LANES), jnp.float32),
        ],
        compiler_params=BIG,
        cost_estimate=cost(10**9, 10**7),
        name="post",
    )(valid, col, row, home, conv, inv, pad, cot, gain)
    left, right = shifted(tail, head)
    grad_frames = pl.pallas_call(
        back_kernel,
        out_shape=shape((count, width), jnp.bfloat16),
        in_specs=[SMEM] + [VMEM] * 4,
        out_specs=VMEM,
        scratch_shapes=[
            pltpu.VMEM((chunks, count + 2 * EDGE, LANES), jnp.float32),
            pltpu.VMEM((chunks, 32, LANES), jnp.float32),
        ],
        compiler_params=BIG,
        cost_estimate=cost(10**9, 10**7),
        name="conv_back",
    )(valid, d_conv, left, right, conv_weight)
    total = total_over_all(sums)
    return (
        output[None],
        grad_frames[None],
        total[:kernel],
        total[kernel],
        grad_in,
        grad_out,
    )


def solution(mesh):
    placed = (
        P("rec", "tm", None),
        P("rec", "tm", None),
        P("rec", "tm", None),
        P("rec"),
        P(),
        P(),
        P(("rec", "tm"), None, None),
        P(("rec", "tm"), None, None),
    )
    return jax.shard_map(
        local,
        mesh=mesh,
        in_specs=placed,
        out_specs=(
            P("rec", "tm", None),
            P("rec", "tm", None),
            P(),
            P(),
            P(("rec", "tm"), None, None),
            P(("rec", "tm"), None, None),
        ),
        check_vma=False,
    )
```

time: 307 us -> 162 us (0.53)
  waiting for transfers between devices: 84.4 us -> 33 us
  Pallas kernels: 0 us -> 42.8 us
  matrix products: 41 us -> 0 us
  other arithmetic: 37.1 us -> 0.7 us
  blocking collectives: 68.4 us -> 36.5 us
  between operations: 16.3 us -> 1.5 us
  starting transfers between devices: 39.7 us -> 31.8 us
  local copies, waits for them, and re-layouts: 19.4 us -> 14.8 us
    psum x1 -> x0, blocking collectives: 68.4 us -> none  [local(): conv_total, gain_total = lax.psum((conv_term, gain_term), ('rec', 'tm'))]
    psum x1 -> x0, waiting for transfers between devices: 56.2 us -> none  [local(): conv_total, gain_total = lax.psum((conv_term, gain_term), ('rec', 'tm'))]
    pallas_call x0 -> x5, Pallas kernels: none -> 42.8 us  [the longest x1 17.2 us: local(): pl.pallas_call(expert_kernel, out_shape=[shape((2 * rows, width), jnp.bfl...]
    dot_general x6 -> x0, matrix products: 41 us -> none  [the longest x1 8.13 us: local(): jnp.einsum('sech,secd->ehd', hidden_act, recv_grad, preferred_element_typ...]
    all_to_all x0 -> x1, blocking collectives: none -> 36.5 us  [local(): lax.all_to_all(send, ('rec', 'tm'), split_axis=0, concat_axis=0, tiled=True)]
    all_to_all x4 -> x1, starting transfers between devices: 27.9 us -> 5.49 us  [local(): lax.all_to_all(back, ('rec', 'tm'), split_axis=0, concat_axis=0, tiled=True)]
    reduce_sum x7 -> x0, other arithmetic: 18.6 us -> none  [the longest x4 9.35 us: local(): jnp.sum(d_conv * padded[offset:offset + frame_rows].astype(jnp.float32),...]
    ppermute x4 -> x15, starting transfers between devices: 11.7 us -> 26.4 us  [the longest x9 9.95 us: ring_sum(): lax.ppermute(part, axis, pairs_of(flip))]
  transfers between devices with their start and end apart: 9 -> 16, of which waited for: 6 -> 9; matrix products, arithmetic and copies ran while one was open for 16% -> 1% of each run, Pallas kernels for 0% -> 8%
where the time goes in v1:
time: 162 us; the launch traced here: 161 us
  Pallas kernels  42.8 us (26%)
  blocking collectives  36.5 us (23%)
  waiting for transfers between devices  33 us (20%)
  starting transfers between devices  31.8 us (20%)
  local copies, waits for them, and re-layouts  14.8 us (9%)
    all_to_all x1, blocking collectives, local(): lax.all_to_all(send, ('rec', 'tm'), split_axis=0, concat_axis=0, tiled=True)  36.5 us
    all_to_all x1, waiting for transfers between devices, local(): lax.all_to_all(back, ('rec', 'tm'), split_axis=0, concat_axis=0, tiled=True)  24.7 us
    pallas_call x1, Pallas kernels, local(): pl.pallas_call(expert_kernel, out_shape=[shape((2 * rows, width), jnp.bfl...  17.2 us
    unnamed x36, local copies, waits for them, and re-layouts  12 us
    ppermute x9, starting transfers between devices, ring_sum(): lax.ppermute(part, axis, pairs_of(flip))  9.95 us
    ppermute x2, starting transfers between devices, shifted(): left = lax.ppermute(tail, 'tm', [(i, i + 1) for i in range(n - 1)])  9.9 us
    pallas_call x1, Pallas kernels, local(): pl.pallas_call(grads_kernel, grid=(hidden // tile,), out_shape=[shape((1,...  9.01 us
    pallas_call x1, Pallas kernels, local(): pl.pallas_call(post_kernel, out_shape=[shape((count, width), jnp.bfloat16...  8.73 us
  transfers between devices with their start and end apart: 16, of which 9 were waited for; matrix products, arithmetic and copies ran while one was open for 1% of the time, Pallas kernels for 8%

profile of v1, /device:TPU:1, one launch (start us, length us, event | category | flops | bytes accessed | tf_op | source)
XLA Modules:
  0.0 161.2 jit_solution(13121324475457610066)
XLA Ops:
  0.6 0.8 slice_bitcast_fusion
  1.4 3.3 %collective-permute-start.1 = (bf16[16,768]{1,0:T(8,128)(2,1)S(1)}, bf16[16,768]{1,0:T(8,128)(2,1)S(1)}, u32[]{:S(2)}, u32[]{:S(2)}) collective-permute-start(bf16[16,768]{1,0:T(8,128)(2,1)S(1)} %get-tuple-element.38), channel_id=1, source_target_pairs={{1,0},{2,1},{3,2},{4,3},{5,4},{6,5},{7,6},{8,7},{9,8},{10,9},{11,1... | collective-permute-start | bytes 73736 | tf_op jit(solution)/shard_map/ppermute | solution.py:226
  4.7 3.1 %collective-permute-start = (bf16[16,768]{1,0:T(8,128)(2,1)S(1)}, bf16[16,768]{1,0:T(8,128)(2,1)S(1)}, u32[]{:S(2)}, u32[]{:S(2)}) collective-permute-start(bf16[16,768]{1,0:T(8,128)(2,1)S(1)} %get-tuple-element.39), channel_id=1, source_target_pairs={{0,1},{1,2},{2,3},{3,4},{4,5},{5,6},{6,7},{7,8},{8,9},{9,10},{10,1... | collective-permute-start | bytes 73736 | tf_op jit(solution)/shard_map/ppermute | solution.py:225
  8.5 0.7 broadcast_in_dim.9.gain_ref
  9.2 0.8 copy.15.col_ref
  10.0 0.0 collective-permute-done.1.right_ref
  10.0 0.0 collective-permute-done.left_ref
  10.0 0.0 copy-start
  10.0 1.1 copy-done
  11.1 0.0 copy-start.2
  11.1 0.7 copy-done.2
  11.8 0.0 copy-start.4
  11.8 1.1 copy-done.4
  12.8 0.9 copy-done.7
  13.7 4.5 %pre.1 = (bf16[1024,768]{1,0:T(8,128)(2,1)S(1)}, f32[6,384,128]{2,1,0:T(8,128)S(1)}, f32[384,128]{1,0:T(8,128)S(1)}, f32[6,416,128]{2,1,0:T(8,128)S(1)}) custom-call(s32[1]{0:T(128)S(6)} %sub.10.nv_ref, s32[384,1]{1,0:T(8,128)S(1)} %copy.15.col_ref, s32[1,384]{1,0:T(1,128)S(1)} %bitcast.22, bf16[384,768]{1,0:T(8,128)(2,1)S(1)} %bitcast.24, ...), custom_call_target="tpu_custom_call" | custom-call | flops 1000000000 | bytes 10000000 | tf_op jit(solution)/shard_map/pre/pallas_call | solution.py:245
  18.2 36.5 %all_to_all.22 = bf16[128,8,768]{2,1,0:T(8,128)(2,1)S(1)} all-to-all(bf16[128,8,768]{2,1,0:T(8,128)(2,1)S(1)} %bitcast.17), channel_id=1, replica_groups=mesh['rec'=4,'tm'=32] {'rec','tm'}, dimensions={0} | all-to-all | bytes 3145728 | tf_op jit(solution)/shard_map/all_to_all | solution.py:264
  54.7 17.2 %experts.1 = (bf16[1024,768]{1,0:T(8,128)(2,1)}, bf16[512,768]{1,0:T(8,128)(2,1)S(1)}, bf16[512,768]{1,0:T(8,128)(2,1)S(1)}, bf16[512,3072]{1,0:T(8,128)(2,1)}, bf16[512,3072]{1,0:T(8,128)(2,1)}) custom-call(bf16[1024,768]{1,0:T(8,128)(2,1)S(1)} %bitcast.18, bf16[768,3072]{1,0:T(8,128)(2,1)} %bitcast.25, bf16[3072,768]{1,0:T(8,128)(2,1)} %bitcast.26), custom_call_target="tpu_custom_call" | custom-call | flops 9663676416 | bytes 20000000 | tf_op jit(solution)/shard_map/experts/pallas_call | solution.py:265
  71.9 0.9 copy-done.14
  72.8 0.9 copy-done.16
  73.7 5.5 %all-to-all-start.1 = ((bf16[128,8,768]{2,1,0:T(8,128)(2,1)}), bf16[128,8,768]{2,1,0:T(8,128)(2,1)}, u32[]{:S(2)}, u32[]{:S(2)}) async-start(bf16[128,8,768]{2,1,0:T(8,128)(2,1)} %bitcast.11), calls=%async_computation.1 | async-start | bytes 3145728 | tf_op jit(solution)/shard_map/all_to_all | solution.py:280
  79.2 24.7 %all-to-all-done.1 = bf16[128,8,768]{2,1,0:T(8,128)(2,1)} async-done(((bf16[128,8,768]{2,1,0:T(8,128)(2,1)}), bf16[128,8,768]{2,1,0:T(8,128)(2,1)}, u32[]{:S(2)}, u32[]{:S(2)}) %all-to-all-start.1) | async-done | bytes 1572896 | tf_op jit(solution)/shard_map/all_to_all | solution.py:280
  104.0 0.0 copy-done.1
  104.0 0.0 copy-done.3
  104.0 8.7 %post.1 = (bf16[384,768]{1,0:T(8,128)(2,1)}, f32[6,384,128]{2,1,0:T(8,128)S(1)}, f32[6,16,128]{2,1,0:T(8,128)S(1)}, f32[6,16,128]{2,1,0:T(8,128)S(1)}, f32[32,768]{1,0:T(8,128)S(1)}) custom-call(s32[1]{0:T(128)S(6)} %sub.10.nv_ref, s32[384,1]{1,0:T(8,128)S(1)} %copy.15.col_ref, s32[1,384]{1,0:T(1,128)S(1)} %bitcast.23, bf16[1024,768]{1,0:T(8,128)(2,1)} %bitcast.12.recv_ref, ...), custom_call_target="tpu_custom_call" | custom-call | flops 1000000000 | bytes 10000000 | tf_op jit(solution)/shard_map/post/pallas_call | solution.py:303
  112.7 1.0 copy-done.5
  113.7 0.6 copy-done.9
  114.4 0.6 copy-done.11
  115.0 0.9 collective-permute-start.4
  115.9 0.9 collective-permute-done.4
  116.8 0.4 collective-permute-start.7
  117.2 1.7 %collective-permute-start.6 = (f32[16,768]{1,0:T(8,128)S(1)}, f32[16,768]{1,0:T(8,128)S(1)}, u32[]{:S(2)}, u32[]{:S(2)}) collective-permute-start(f32[16,768]{1,0:T(8,128)S(1)} %dynamic-slice_add_fusion), channel_id=1, source_target_pairs={{0,4},{1,5},{2,6},{3,7},{4,0},{5,1},{6,2},{7,3},{8,12},{9,13},{10,... | collective-permute-start | bytes 147464 | tf_op jit(solution)/shard_map/ppermute | solution.py:201
  118.9 1.2 collective-permute-start.5
  120.1 0.9 collective-permute-done.7
  121.0 0.7 collective-permute-done.6
  121.7 0.7 collective-permute-done.5
  122.4 0.6 collective-permute-start.10
  123.0 1.1 collective-permute-start.9
  124.1 1.6 %collective-permute-start.8 = (f32[16,768]{1,0:T(8,128)S(1)}, f32[16,768]{1,0:T(8,128)S(1)}, u32[]{:S(2)}, u32[]{:S(2)}) collective-permute-start(f32[16,768]{1,0:T(8,128)S(1)} %add_add_fusion.1), channel_id=1, source_target_pairs={{0,32},{32,0},{64,96},{96,64},{1,33},{33,1},{65,97},{97,65},{2,34}... | collective-permute-start | bytes 147464 | tf_op jit(solution)/shard_map/ppermute | solution.py:201
  125.7 0.9 collective-permute-done.10
  126.6 0.8 collective-permute-done.9
  127.4 0.3 collective-permute-done.8
  127.7 0.1 collective-permute-start.13
  127.8 1.8 %collective-permute-start.12 = (f32[16,768]{1,0:T(8,128)S(1)}, f32[16,768]{1,0:T(8,128)S(1)}, u32[]{:S(2)}, u32[]{:S(2)}) collective-permute-start(f32[16,768]{1,0:T(8,128)S(1)} %add_add_fusion), channel_id=1, source_target_pairs={{0,16},{1,17},{2,18},{3,19},{4,20},{5,21},{6,22},{7,23},{8,24},{9,... | collective-permute-start | bytes 147464 | tf_op jit(solution)/shard_map/ppermute | solution.py:201
  129.7 1.4 collective-permute-start.11
  131.1 1.9 %copy-done.13 = bf16[512,3072]{1,0:T(8,128)(2,1)S(1)} copy-done((bf16[512,3072]{1,0:T(8,128)(2,1)S(1)}, bf16[512,3072]{1,0:T(8,128)(2,1)}, u32[]{:S(2)}) %copy-start.13) | copy-done | bytes 3145752
  133.0 1.1 copy-done.15
  134.1 1.1 copy-done.17
  135.2 9.0 %weight_grads.1 = (bf16[1,768,3072]{2,1,0:T(8,128)(2,1)}, bf16[1,3072,768]{2,1,0:T(8,128)(2,1)}) custom-call(bf16[512,768]{1,0:T(8,128)(2,1)S(1)} %copy-done.15, bf16[512,768]{1,0:T(8,128)(2,1)S(1)} %copy-done.17, bf16[512,3072]{1,0:T(8,128)(2,1)S(1)} %copy-done.13, bf16[512,3072]{1,0:T(8,128)(2,1)} %get-tuple-element.35.dpre_ref), custom_call_target="tpu_custom_call" | custom-call | flops 4831838208 | bytes 20000000 | tf_op jit(solution)/shard_map/weight_grads/pallas_call | solution.py:282
  144.3 0.0 copy-done.12
  144.3 6.8 %collective-permute-start.2 = (f32[6,16,128]{2,1,0:T(8,128)S(1)}, f32[6,16,128]{2,1,0:T(8,128)S(1)}, u32[]{:S(2)}, u32[]{:S(2)}) collective-permute-start(f32[6,16,128]{2,1,0:T(8,128)S(1)} %copy-done.12), channel_id=1, source_target_pairs={{0,1},{1,2},{2,3},{3,4},{4,5},{5,6},{6,7},{7,8},{8,9},{9,10},{10,1... | collective-permute-start | bytes 147464 | tf_op jit(solution)/shard_map/ppermute | solution.py:225
  151.1 0.0 copy-done.10
  151.1 1.9 %collective-permute-start.3 = (f32[6,16,128]{2,1,0:T(8,128)S(1)}, f32[6,16,128]{2,1,0:T(8,128)S(1)}, u32[]{:S(2)}, u32[]{:S(2)}) collective-permute-start(f32[6,16,128]{2,1,0:T(8,128)S(1)} %copy-done.10), channel_id=1, source_target_pairs={{1,0},{2,1},{3,2},{4,3},{5,4},{6,5},{7,6},{8,7},{9,8},{10,9},{11,1... | collective-permute-start | bytes 147464 | tf_op jit(solution)/shard_map/ppermute | solution.py:226
  153.0 0.0 collective-permute-done.13
  153.0 0.0 collective-permute-done.12
  153.0 0.0 collective-permute-done.11
  153.1 0.3 collective-permute-start.14
  153.4 0.0 collective-permute-done.2.left_ref
  153.4 3.1 %collective-permute-done.3.right_ref = f32[6,16,128]{2,1,0:T(8,128)S(1)} collective-permute-done((f32[6,16,128]{2,1,0:T(8,128)S(1)}, f32[6,16,128]{2,1,0:T(8,128)S(1)}, u32[]{:S(2)}, u32[]{:S(2)}) %collective-permute-start.3) | collective-permute-done | bytes 49184 | tf_op jit(solution)/shard_map/ppermute | solution.py:226
  156.5 0.0 copy-done.6
  156.5 0.0 copy-done.8
  156.5 3.4 %conv_back.1 = bf16[384,768]{1,0:T(8,128)(2,1)} custom-call(s32[1]{0:T(128)S(6)} %sub.10.nv_ref, f32[6,384,128]{2,1,0:T(8,128)S(1)} %copy-done.6, f32[6,16,128]{2,1,0:T(8,128)S(1)} %collective-permute-done.2.left_ref, f32[6,16,128]{2,1,0:T(8,128)S(1)} %collective-permute-done.3.right_ref, f32[31,768]{1,0:T(8,128)S(1)} %copy-done.8), custom_call_target="tpu_custom_call" | custom-call | flops 1000000000 | bytes 10000000 | tf_op jit(solution)/shard_map/conv_back/pallas_call | solution.py:324
  159.9 0.0 collective-permute-done.14
  159.9 0.6 slice_reduce_fusion
  160.5 0.6 pad_maximum_fusion
  (21 shorter events, 0.1 us)
Async XLA Ops:
  1.4 8.6 %collective-permute-start.1 = (bf16[16,768]{1,0:T(8,128)(2,1)S(1)}, bf16[16,768]{1,0:T(8,128)(2,1)S(1)}, u32[]{:S(2)}, u32[]{:S(2)}) collective-permute-start(bf16[16,768]{1,0:T(8,128)(2,1)S(1)} %get-tuple-element.38), channel_id=1, source_target_pairs={{1,0},{2,1},{3,2},{4,3},{5,4},{6,5},{7,6},{8,7},{9,8},{10,9},{11,1... | collective-permute-start | bytes 73736 | tf_op jit(solution)/shard_map/ppermute | solution.py:226
  4.7 5.3 %collective-permute-start = (bf16[16,768]{1,0:T(8,128)(2,1)S(1)}, bf16[16,768]{1,0:T(8,128)(2,1)S(1)}, u32[]{:S(2)}, u32[]{:S(2)}) collective-permute-start(bf16[16,768]{1,0:T(8,128)(2,1)S(1)} %get-tuple-element.39), channel_id=1, source_target_pairs={{0,1},{1,2},{2,3},{3,4},{4,5},{5,6},{6,7},{7,8},{8,9},{9,10},{10,1... | collective-permute-start | bytes 73736 | tf_op jit(solution)/shard_map/ppermute | solution.py:225
  10.0 1.1 copy-start
  11.1 0.7 copy-start.2
  11.8 1.1 copy-start.4
  12.8 0.9 copy-start.7
  71.9 0.9 copy-start.14
  72.8 0.9 copy-start.16
  73.7 30.3 %copy-start.1 = (bf16[1,384,768]{2,1,0:T(8,128)(2,1)S(1)}, bf16[1,384,768]{2,1,0:T(8,128)(2,1)}, u32[]{:S(2)}) copy-start(bf16[1,384,768]{2,1,0:T(8,128)(2,1)} %param.9) | copy-start | bytes 1769476
  73.7 30.3 %copy-start.3 = (s32[1,384,1]{1,2,0:T(1,128)S(1)}, s32[1,384,1]{1,2,0:T(1,128)}, u32[]{:S(2)}) copy-start(s32[1,384,1]{1,2,0:T(1,128)} %param.10) | copy-start | bytes 4612
  73.7 30.2 %all-to-all-start.1 = ((bf16[128,8,768]{2,1,0:T(8,128)(2,1)}), bf16[128,8,768]{2,1,0:T(8,128)(2,1)}, u32[]{:S(2)}, u32[]{:S(2)}) async-start(bf16[128,8,768]{2,1,0:T(8,128)(2,1)} %bitcast.11), calls=%async_computation.1 | async-start | bytes 3145728 | tf_op jit(solution)/shard_map/all_to_all | solution.py:280
  112.7 1.0 copy-start.5
  113.7 0.6 copy-start.9
  114.4 0.6 copy-start.11
  115.0 1.8 %collective-permute-start.4 = (f32[16,768]{1,0:T(8,128)S(1)}, f32[16,768]{1,0:T(8,128)S(1)}, u32[]{:S(2)}, u32[]{:S(2)}) collective-permute-start(f32[16,768]{1,0:T(8,128)S(1)} %constant_dynamic-slice_fusion), channel_id=1, source_target_pairs={{0,1},{1,0},{2,3},{3,2},{4,5},{5,4},{6,7},{7,6},{8,9},{9,8},{10,11... | collective-permute-start | bytes 147464 | tf_op jit(solution)/shard_map/ppermute | solution.py:212
  116.8 4.2 %collective-permute-start.7 = (f32[16,768]{1,0:T(8,128)S(1)}, f32[16,768]{1,0:T(8,128)S(1)}, u32[]{:S(2)}, u32[]{:S(2)}) collective-permute-start(f32[16,768]{1,0:T(8,128)S(1)} %dynamic-slice_add_fusion), channel_id=1, source_target_pairs={{0,6},{1,7},{2,4},{3,5},{4,2},{5,3},{6,0},{7,1},{8,14},{9,15},{10,... | collective-permute-start | bytes 147464 | tf_op jit(solution)/shard_map/ppermute | solution.py:201
  117.2 4.5 %collective-permute-start.6 = (f32[16,768]{1,0:T(8,128)S(1)}, f32[16,768]{1,0:T(8,128)S(1)}, u32[]{:S(2)}, u32[]{:S(2)}) collective-permute-start(f32[16,768]{1,0:T(8,128)S(1)} %dynamic-slice_add_fusion), channel_id=1, source_target_pairs={{0,4},{1,5},{2,6},{3,7},{4,0},{5,1},{6,2},{7,3},{8,12},{9,13},{10,... | collective-permute-start | bytes 147464 | tf_op jit(solution)/shard_map/ppermute | solution.py:201
  118.9 3.5 %collective-permute-start.5 = (f32[16,768]{1,0:T(8,128)S(1)}, f32[16,768]{1,0:T(8,128)S(1)}, u32[]{:S(2)}, u32[]{:S(2)}) collective-permute-start(f32[16,768]{1,0:T(8,128)S(1)} %dynamic-slice_add_fusion), channel_id=1, source_target_pairs={{0,2},{1,3},{2,0},{3,1},{4,6},{5,7},{6,4},{7,5},{8,10},{9,11},{10,... | collective-permute-start | bytes 147464 | tf_op jit(solution)/shard_map/ppermute | solution.py:201
  122.4 4.2 %collective-permute-start.10 = (f32[16,768]{1,0:T(8,128)S(1)}, f32[16,768]{1,0:T(8,128)S(1)}, u32[]{:S(2)}, u32[]{:S(2)}) collective-permute-start(f32[16,768]{1,0:T(8,128)S(1)} %add_add_fusion.1), channel_id=1, source_target_pairs={{0,96},{32,64},{64,32},{96,0},{1,97},{33,65},{65,33},{97,1},{2,98}... | collective-permute-start | bytes 147464 | tf_op jit(solution)/shard_map/ppermute | solution.py:201
  123.0 4.4 %collective-permute-start.9 = (f32[16,768]{1,0:T(8,128)S(1)}, f32[16,768]{1,0:T(8,128)S(1)}, u32[]{:S(2)}, u32[]{:S(2)}) collective-permute-start(f32[16,768]{1,0:T(8,128)S(1)} %add_add_fusion.1), channel_id=1, source_target_pairs={{0,64},{32,96},{64,0},{96,32},{1,65},{33,97},{65,1},{97,33},{2,66}... | collective-permute-start | bytes 147464 | tf_op jit(solution)/shard_map/ppermute | solution.py:201
  124.1 3.6 %collective-permute-start.8 = (f32[16,768]{1,0:T(8,128)S(1)}, f32[16,768]{1,0:T(8,128)S(1)}, u32[]{:S(2)}, u32[]{:S(2)}) collective-permute-start(f32[16,768]{1,0:T(8,128)S(1)} %add_add_fusion.1), channel_id=1, source_target_pairs={{0,32},{32,0},{64,96},{96,64},{1,33},{33,1},{65,97},{97,65},{2,34}... | collective-permute-start | bytes 147464 | tf_op jit(solution)/shard_map/ppermute | solution.py:201
  127.7 25.3 %collective-permute-start.13 = (f32[16,768]{1,0:T(8,128)S(1)}, f32[16,768]{1,0:T(8,128)S(1)}, u32[]{:S(2)}, u32[]{:S(2)}) collective-permute-start(f32[16,768]{1,0:T(8,128)S(1)} %add_add_fusion), channel_id=1, source_target_pairs={{0,24},{1,25},{2,26},{3,27},{4,28},{5,29},{6,30},{7,31},{8,16},{9,... | collective-permute-start | bytes 147464 | tf_op jit(solution)/shard_map/ppermute | solution.py:201
  127.8 25.2 %collective-permute-start.12 = (f32[16,768]{1,0:T(8,128)S(1)}, f32[16,768]{1,0:T(8,128)S(1)}, u32[]{:S(2)}, u32[]{:S(2)}) collective-permute-start(f32[16,768]{1,0:T(8,128)S(1)} %add_add_fusion), channel_id=1, source_target_pairs={{0,16},{1,17},{2,18},{3,19},{4,20},{5,21},{6,22},{7,23},{8,24},{9,... | collective-permute-start | bytes 147464 | tf_op jit(solution)/shard_map/ppermute | solution.py:201
  129.7 23.3 %collective-permute-start.11 = (f32[16,768]{1,0:T(8,128)S(1)}, f32[16,768]{1,0:T(8,128)S(1)}, u32[]{:S(2)}, u32[]{:S(2)}) collective-permute-start(f32[16,768]{1,0:T(8,128)S(1)} %add_add_fusion), channel_id=1, source_target_pairs={{0,8},{1,9},{2,10},{3,11},{4,12},{5,13},{6,14},{7,15},{8,0},{9,1},... | collective-permute-start | bytes 147464 | tf_op jit(solution)/shard_map/ppermute | solution.py:201
  131.1 1.9 %copy-start.13 = (bf16[512,3072]{1,0:T(8,128)(2,1)S(1)}, bf16[512,3072]{1,0:T(8,128)(2,1)}, u32[]{:S(2)}) copy-start(bf16[512,3072]{1,0:T(8,128)(2,1)} %get-tuple-element.34.act_ref) | copy-start | bytes 9437188
  133.0 1.1 copy-start.15
  134.1 1.1 copy-start.17
  135.2 9.0 %copy-start.12 = (f32[6,16,128]{2,1,0:T(8,128)S(1)}, f32[6,16,128]{2,1,0:T(8,128)}, u32[]{:S(2)}) copy-start(f32[6,16,128]{2,1,0:T(8,128)} %copy-done.11) | copy-start | bytes 147460
  135.2 15.8 %copy-start.10 = (f32[6,16,128]{2,1,0:T(8,128)S(1)}, f32[6,16,128]{2,1,0:T(8,128)}, u32[]{:S(2)}) copy-start(f32[6,16,128]{2,1,0:T(8,128)} %copy-done.9) | copy-start | bytes 147460
  135.2 21.3 %copy-start.6 = (f32[6,384,128]{2,1,0:T(8,128)S(1)}, f32[6,384,128]{2,1,0:T(8,128)}, u32[]{:S(2)}) copy-start(f32[6,384,128]{2,1,0:T(8,128)} %copy-done.5) | copy-start | bytes 3538948
  135.2 21.3 %copy-start.8 = (f32[31,768]{1,0:T(8,128)S(1)}, f32[31,768]{1,0:T(8,128)}, u32[]{:S(2)}) copy-start(f32[31,768]{1,0:T(8,128)} %w_ref.3) | copy-start | bytes 285700
  144.3 9.2 %collective-permute-start.2 = (f32[6,16,128]{2,1,0:T(8,128)S(1)}, f32[6,16,128]{2,1,0:T(8,128)S(1)}, u32[]{:S(2)}, u32[]{:S(2)}) collective-permute-start(f32[6,16,128]{2,1,0:T(8,128)S(1)} %copy-done.12), channel_id=1, source_target_pairs={{0,1},{1,2},{2,3},{3,4},{4,5},{5,6},{6,7},{7,8},{8,9},{9,10},{10,1... | collective-permute-start | bytes 147464 | tf_op jit(solution)/shard_map/ppermute | solution.py:225
  151.1 5.4 %collective-permute-start.3 = (f32[6,16,128]{2,1,0:T(8,128)S(1)}, f32[6,16,128]{2,1,0:T(8,128)S(1)}, u32[]{:S(2)}, u32[]{:S(2)}) collective-permute-start(f32[6,16,128]{2,1,0:T(8,128)S(1)} %copy-done.10), channel_id=1, source_target_pairs={{1,0},{2,1},{3,2},{4,3},{5,4},{6,5},{7,6},{8,7},{9,8},{10,9},{11,1... | collective-permute-start | bytes 147464 | tf_op jit(solution)/shard_map/ppermute | solution.py:226
  153.1 6.8 %collective-permute-start.14 = (f32[16,768]{1,0:T(8,128)S(1)}, f32[16,768]{1,0:T(8,128)S(1)}, u32[]{:S(2)}, u32[]{:S(2)}) collective-permute-start(f32[16,768]{1,0:T(8,128)S(1)} %add_multiply_fusion), channel_id=1, source_target_pairs={{0,1},{1,0},{2,3},{3,2},{4,5},{5,4},{6,7},{7,6},{8,9},{9,8},{10,11... | collective-permute-start | bytes 147464 | tf_op jit(solution)/shard_map/ppermute | solution.py:217

commit v2 on v1

v2 whole, which is shorter than its diff:
```python
import functools
import math

import jax
import jax.numpy as jnp
from jax import lax
from jax.experimental import pallas as pl
from jax.experimental.pallas import tpu as pltpu
from jax.sharding import PartitionSpec as P

LANES = 128
EDGE = 16
ROWS = 64
SLOTS = 4
PAIR = 2 * SLOTS
VMEM = pl.BlockSpec(memory_space=pltpu.VMEM)
SMEM = pl.BlockSpec(memory_space=pltpu.SMEM)
ANY = pl.BlockSpec(memory_space=pl.ANY)
HBM = pl.BlockSpec(memory_space=pltpu.HBM)


def f32(x):
    return x.astype(jnp.float32)


def bf16(x):
    return x.astype(jnp.bfloat16)


def dot(a, b, dims=((1,), (0,))):
    return lax.dot_general(a, b, (dims, ((), ())), preferred_element_type=jnp.float32)


def iota(shape, axis):
    return lax.broadcasted_iota(jnp.int32, shape, axis)


def limit(mebibytes):
    return pltpu.CompilerParams(vmem_limit_bytes=mebibytes * 1024 * 1024)


def hbm(x):
    return pltpu.with_memory_space_constraint(x, pltpu.HBM)


def cost(flops, nbytes):
    return pl.CostEstimate(flops=flops, bytes_accessed=nbytes, transcendentals=0)


def pre_kernel(
    nv_ref, row_hbm, x_hbm, cot_hbm, w_hbm, gain_hbm,
    conv_ref, pad_ref, squares_ref, pick_ref, send_ref, taps_ref,
    row_ref, x_ref, cot_ref, w_ref, gain_ref, grads, sems,
):
    count, width = x_ref.shape
    chunks = width // LANES
    kernel = w_ref.shape[0]
    reach = (kernel - 1) // 2
    copies = [
        pltpu.make_async_copy(src, dst, sems.at[i])
        for i, (src, dst) in enumerate(
            (
                (x_hbm, x_ref), (w_hbm, w_ref), (gain_hbm, gain_ref),
                (row_hbm, row_ref), (cot_hbm, cot_ref),
            )
        )
    ]
    for copy in copies:
        copy.start()
    valid = nv_ref[0]
    inside = iota((count, LANES), 0) < valid
    squares_ref[...] = jnp.zeros_like(squares_ref)
    for copy in copies[:3]:
        copy.wait()
    for c in range(chunks):
        lanes = slice(c * LANES, (c + 1) * LANES)
        pad_ref[c, 0:EDGE, :] = jnp.zeros((EDGE, LANES), jnp.float32)
        pad_ref[c, EDGE : EDGE + count, :] = jnp.where(inside, f32(x_ref[:, lanes]), 0.0)
        pad_ref[c, EDGE + count :, :] = jnp.zeros((EDGE, LANES), jnp.float32)
        taps_ref[c, 0:kernel, :] = w_ref[:, lanes]
        taps_ref[c, kernel : kernel + 1, :] = gain_ref[lanes][None, :]

    @pl.loop(0, chunks)
    def _(c):
        for start in range(0, count, ROWS):
            total = jnp.zeros((ROWS, LANES), jnp.float32)
            for k in range(kernel):
                at = start + k + EDGE - reach
                total = total + taps_ref[c, k : k + 1, :] * pad_ref[c, at : at + ROWS, :]
            total = pad_ref[c, EDGE + start : EDGE + start + ROWS, :] + total
            conv_ref[c, start : start + ROWS, :] = total
            if 0 < start < count - ROWS:
                squares_ref[start : start + ROWS, :] += total * total
            else:
                low = EDGE if start == 0 else 0
                high = ROWS if start == 0 else ROWS - EDGE
                inner = total[low:high, :]
                squares_ref[start + low : start + high, :] += inner * inner

    for copy in copies[3:]:
        copy.wait()
    row = row_ref[...]
    experts = send_ref.shape[0] // PAIR
    named = jnp.where(iota((experts, count), 0) == row, 1.0, 0.0)
    before = bf16(jnp.where(iota((count, count), 0) < iota((count, count), 1), 1.0, 0.0))
    slot = jnp.sum(named * dot(bf16(named), before), axis=0, keepdims=True)
    key = row * PAIR + slot.astype(jnp.int32)
    for c in range(chunks):
        lanes = slice(c * LANES, (c + 1) * LANES)
        grads[:, lanes] = bf16(jnp.where(inside, f32(cot_ref[:, lanes]), 0.0))
    block = 256
    for start in range(0, send_ref.shape[0], block):
        seat = iota((block, count), 0) + start
        pick_ref[start : start + block, :] = bf16(jnp.where(seat == key, 1.0, 0.0))
        pick = bf16(jnp.where(seat == key + SLOTS, 1.0, 0.0))
        send_ref[start : start + block, :] = bf16(dot(pick, grads[...]))


def send_kernel(
    nv_ref, left_ref, right_ref, conv_in, pad_in, squares_ref, pick_ref, grads_ref, taps_ref,
    conv_ref, pad_ref, send_ref, inv_ref,
    rows, squares,
):
    chunks, count, _ = conv_in.shape
    width = chunks * LANES
    kernel = taps_ref.shape[1] - 1
    reach = (kernel - 1) // 2
    valid = nv_ref[0]
    edge = iota((EDGE, LANES), 0)
    squares[...] = squares_ref[...]
    for c in range(chunks):
        lanes = slice(c * LANES, (c + 1) * LANES)
        pad_ref[c, 0:EDGE, :] = jnp.where(edge - EDGE < valid, f32(left_ref[:, lanes]), 0.0)
        pad_ref[c, EDGE : EDGE + count, :] = pad_in[c, EDGE : EDGE + count, :]
        pad_ref[c, EDGE + count :, :] = jnp.where(edge + count < valid, f32(right_ref[:, lanes]), 0.0)
        conv_ref[c, EDGE : count - EDGE, :] = conv_in[c, EDGE : count - EDGE, :]
        for start in (0, count - EDGE):
            total = jnp.zeros((EDGE, LANES), jnp.float32)
            for k in range(kernel):
                at = start + k + EDGE - reach
                total = total + taps_ref[c, k : k + 1, :] * pad_ref[c, at : at + EDGE, :]
            total = pad_ref[c, EDGE + start : EDGE + start + EDGE, :] + total
            conv_ref[c, start : start + EDGE, :] = total
            squares[start : start + EDGE, :] += total * total
    inv = lax.rsqrt(jnp.sum(squares[...], axis=-1, keepdims=True) * (1.0 / width) + 1e-05)
    inv = jnp.broadcast_to(inv, (count, LANES))
    inv_ref[...] = inv
    for c in range(chunks):
        lanes = slice(c * LANES, (c + 1) * LANES)
        rows[:, lanes] = bf16(conv_ref[c] * inv * taps_ref[c, kernel : kernel + 1, :])
    block = 256
    for start in range(0, send_ref.shape[0], block):
        part = slice(start, start + block)
        send_ref[part, :] = bf16(dot(pick_ref[part, :], rows[...]) + f32(grads_ref[part, :]))


def picks():
    half, whole = 128, 256
    i, r = iota((half, whole), 0), iota((half, whole), 1)
    place = (i // SLOTS) * PAIR + i % SLOTS
    return bf16(jnp.where(r == place, 1.0, 0.0)), bf16(jnp.where(r == place + SLOTS, 1.0, 0.0))


def unpack(recv_ref, x_ref, g_ref, copies=None):
    pick_x, pick_g = picks()
    half, whole = pick_x.shape
    for n in range(x_ref.shape[0] // half):
        if copies:
            copies[n].wait()
        part = recv_ref[n * whole : (n + 1) * whole, :]
        x_ref[n * half : (n + 1) * half, :] = bf16(dot(pick_x, part))
        g_ref[n * half : (n + 1) * half, :] = bf16(dot(pick_g, part))


TILE = 512


def expert_kernel(
    recv_hbm, win_hbm, wout_hbm,
    back_hbm, act_hbm, dpre_hbm,
    recv_ref, win_ref, wout_ref, x_ref, g_ref, act_ref, dpre_ref, result, d_rows,
    row_sems, in_sems, out_sems,
):
    rows = x_ref.shape[0]
    hidden = win_ref.shape[1]
    tiles = hidden // TILE
    half, whole = 128, 256
    groups = rows // half
    arrivals, returns, loads, stores = [], [], [], []
    for n in range(groups):
        part = pl.ds(n * whole, whole)
        arrivals.append(pltpu.make_async_copy(recv_hbm.at[part, :], recv_ref.at[part, :], row_sems.at[0, n]))
        returns.append(pltpu.make_async_copy(recv_ref.at[part, :], back_hbm.at[part, :], row_sems.at[1, n]))
        arrivals[n].start()
    for n in range(tiles):
        cols = pl.ds(n * TILE, TILE)
        loads.append((
            pltpu.make_async_copy(win_hbm.at[:, cols], win_ref.at[:, cols], in_sems.at[0, n]),
            pltpu.make_async_copy(wout_hbm.at[cols, :], wout_ref.at[cols, :], in_sems.at[1, n]),
        ))
        stores.append((
            pltpu.make_async_copy(act_ref.at[:, cols], act_hbm.at[:, cols], out_sems.at[0, n]),
            pltpu.make_async_copy(dpre_ref.at[:, cols], dpre_hbm.at[:, cols], out_sems.at[1, n]),
        ))
        for copy in loads[n]:
            copy.start()
    unpack(recv_ref, x_ref, g_ref, arrivals)

    def front(n):
        cols = slice(n * TILE, (n + 1) * TILE)
        for copy in loads[n]:
            copy.wait()
        return (
            dot(x_ref[...], win_ref[:, cols]),
            dot(g_ref[...], wout_ref[cols, :], ((1,), (1,))),
        )

    ready = front(0)
    for n in range(tiles):
        cols = slice(n * TILE, (n + 1) * TILE)
        pre, d_act = ready
        if n + 1 < tiles:
            ready = front(n + 1)
        gate = 0.5 * jnp.tanh(0.5 * pre) + 0.5
        value = pre * gate
        act = bf16(value)
        d_pre = bf16(d_act * (gate + value * (1.0 - gate)))
        act_ref[:, cols] = act
        dpre_ref[:, cols] = d_pre
        for copy in stores[n]:
            copy.start()
        forward = dot(act, wout_ref[cols, :])
        backward = dot(d_pre, win_ref[:, cols], ((1,), (1,)))
        if n:
            forward, backward = forward + result[...], backward + d_rows[...]
        result[...] = forward
        d_rows[...] = backward
    q, j = iota((whole, half), 0), iota((whole, half), 1)
    home = (j // SLOTS) * PAIR + j % SLOTS
    put_x = bf16(jnp.where(q == home, 1.0, 0.0))
    put_g = bf16(jnp.where(q == home + SLOTS, 1.0, 0.0))
    for n in range(groups):
        part = slice(n * half, (n + 1) * half)
        recv_ref[n * whole : (n + 1) * whole, :] = bf16(
            dot(put_x, bf16(result[part, :])) + dot(put_g, bf16(d_rows[part, :]))
        )
        returns[n].start()
    for pair in stores:
        for copy in pair:
            copy.wait()
    for copy in returns:
        copy.wait()


def grads_kernel(recv_ref, act_ref, dpre_ref, gin_ref, gout_ref, done_ref, x_ref, g_ref):
    @pl.when(pl.program_id(0) == 0)
    def _():
        unpack(recv_ref, x_ref, g_ref)

    gin_ref[0] = bf16(dot(x_ref[...], dpre_ref[...], ((0,), (0,))))
    gout_ref[0] = bf16(dot(act_ref[...], g_ref[...], ((0,), (0,))))
    done_ref[...] = jnp.zeros_like(done_ref)


def post_kernel(
    nv_ref, row_hbm, recv_hbm, cot_hbm, inv_hbm, conv_hbm, taps_hbm, pad_hbm, done_ref,
    out_ref, dconv_ref, head_ref, tail_ref, mine_ref, other_ref,
    row_ref, recv_ref, cot_ref, inv_ref, conv_ref, taps_ref, pad_ref,
    back, dhid, means, sums_ref, sems,
):
    copies = [
        pltpu.make_async_copy(src, dst, sems.at[i])
        for i, (src, dst) in enumerate(
            (
                (row_hbm, row_ref), (recv_hbm, recv_ref), (cot_hbm, cot_ref), (inv_hbm, inv_ref),
                (conv_hbm, conv_ref), (taps_hbm, taps_ref), (pad_hbm, pad_ref),
            )
        )
    ]
    for copy in copies:
        copy.start()
    count, width = cot_ref.shape
    chunks = width // LANES
    kernel = sums_ref.shape[0] - 1
    reach = (kernel - 1) // 2
    here, there = iota((count, count), 0), iota((count, count), 1)
    copies[0].wait()
    row = row_ref[...]
    col = jnp.sum(jnp.where(here == there, f32(row), 0.0), axis=1, keepdims=True).astype(jnp.int32)
    earlier = (col == row) & (there < here)
    slot = jnp.sum(jnp.where(earlier, 1.0, 0.0), axis=1, keepdims=True).astype(jnp.int32)
    key = col * PAIR + slot
    seats = iota((count, recv_ref.shape[0]), 1)
    pick_grad = bf16(jnp.where(seats == key + SLOTS, 1.0, 0.0))
    pick_out = bf16(jnp.where(seats == key, 1.0, 0.0))
    copies[1].wait()
    dhid[...] = dot(pick_grad, recv_ref[...])
    back[...] = dot(pick_out, recv_ref[...])
    for copy in copies[2:]:
        copy.wait()
    inside = iota((count, LANES), 0) < nv_ref[0]
    inv = inv_ref[...]
    means[...] = jnp.zeros_like(means)
    for c in range(chunks):
        lanes = slice(c * LANES, (c + 1) * LANES)
        normed = conv_ref[c] * inv
        d_hidden = dhid[:, lanes]
        means[...] += d_hidden * taps_ref[c, kernel : kernel + 1, :] * normed
        sums_ref[kernel : kernel + 1, lanes] = jnp.sum(d_hidden * normed, axis=0, keepdims=True)
        out_ref[:, lanes] = bf16(conv_ref[c] + jnp.where(inside, back[:, lanes], 0.0))
    mean = jnp.sum(means[...], axis=-1, keepdims=True) * (1.0 / width)
    mean = jnp.broadcast_to(mean, (count, LANES))
    for c in range(chunks):
        lanes = slice(c * LANES, (c + 1) * LANES)
        d_conv = f32(cot_ref[:, lanes]) + inv * (
            dhid[:, lanes] * taps_ref[c, kernel : kernel + 1, :] - conv_ref[c] * inv * mean
        )
        dconv_ref[c] = d_conv
        head_ref[c] = d_conv[0:EDGE, :]
        tail_ref[c] = d_conv[count - EDGE :, :]
    for c in range(chunks):
        lanes = slice(c * LANES, (c + 1) * LANES)
        totals = [jnp.zeros((8, LANES), jnp.float32) for _ in range(kernel)]
        for start in range(0, count, ROWS):
            part = dconv_ref[c, start : start + ROWS, :]
            for k in range(kernel):
                at = start + k + EDGE - reach
                product = part * pad_ref[c, at : at + ROWS, :]
                totals[k] = totals[k] + jnp.sum(product.reshape(ROWS // 8, 8, LANES), axis=0)
        for k in range(kernel):
            sums_ref[k : k + 1, lanes] = jnp.sum(totals[k], axis=0, keepdims=True)
    core = nv_ref[1]
    rows = mine_ref.shape[0]
    low, high = sums_ref[0:rows, :], sums_ref[rows:, :]
    mine_ref[...] = jnp.where(core == 0, low, high)
    other_ref[...] = jnp.where(core == 0, high, low)


def back_kernel(first, nv_ref, dconv_ref, left_ref, right_ref, taps_ref, tie_ref, grad_ref, low, high):
    _, count, _ = dconv_ref.shape
    kernel = taps_ref.shape[1] - 1
    reach = (kernel - 1) // 2
    valid = nv_ref[0]
    for i in range(grad_ref.shape[1] // LANES):
        c = first + i
        lanes = slice(i * LANES, (i + 1) * LANES)
        low[i, 0:EDGE, :] = left_ref[c]
        low[i, EDGE:, :] = dconv_ref[c, 0 : ROWS + EDGE, :]
        high[i, 0 : ROWS + EDGE, :] = dconv_ref[c, count - ROWS - EDGE :, :]
        high[i, ROWS + EDGE :, :] = right_ref[c]
        for start in range(0, count, ROWS):
            if start == 0:
                window, shift, at = low, EDGE, i
            elif start == count - ROWS:
                window, shift, at = high, EDGE - start, i
            else:
                window, shift, at = dconv_ref, 0, c
            total = jnp.zeros((ROWS, LANES), jnp.float32)
            for k in range(kernel):
                begin = start + shift + reach - k
                total = total + taps_ref[c, k : k + 1, :] * window[at, begin : begin + ROWS, :]
            total = window[at, start + shift : start + shift + ROWS, :] + total
            keep = iota((ROWS, LANES), 0) + start < valid
            grad_ref[start : start + ROWS, lanes] = bf16(jnp.where(keep, total, 0.0))


def add_kernel(tie_ref, own_ref, one_ref, two_ref, three_ref, out_ref):
    out_ref[...] = (own_ref[...] + one_ref[...]) + (two_ref[...] + three_ref[...])


def finish_kernel(scale, nv_ref, part_ref, fellow_ref, *refs):
    pieces, (taps_ref, gain_ref, grad_ref) = refs[:-3], refs[-3:]
    core = nv_ref[1]
    rows = part_ref.shape[0]
    part, fellow = part_ref[...] * scale, fellow_ref[...] * scale
    low = jnp.where(core == 0, part, fellow)
    high = jnp.where(core == 0, fellow, part)
    taps_ref[0:rows, :] = low
    taps_ref[rows:, :] = high[0 : rows - 1, :]
    gain_ref[...] = high[rows - 1, :]
    width = pieces[0].shape[1]
    for n, piece in enumerate(pieces):
        grad_ref[:, n * width : (n + 1) * width] = piece[...]


def shifted(tail, head):
    n = lax.axis_size("tm")
    left = lax.ppermute(tail, "tm", [(i, i + 1) for i in range(n - 1)])
    right = lax.ppermute(head, "tm", [(i + 1, i) for i in range(n - 1)])
    return left, right


def local(frames, cotangent, routes, lengths, conv_weight, norm_gain, expert_in, expert_out):
    count, width = frames.shape[1:]
    kernel = conv_weight.shape[0]
    chunks = width // LANES
    devices = lax.axis_size("rec") * lax.axis_size("tm")
    hidden = expert_in.shape[2]
    rows = devices * SLOTS
    x, cot = hbm(frames[0]), hbm(cotangent[0])
    win, wout = hbm(expert_in[0]), hbm(expert_out[0])
    place = lax.axis_index("tm")
    scalars = jnp.stack([lengths[0] - place * count, place % 2])
    row = hbm(routes[0].reshape(1, count))
    conv_weight, norm_gain = hbm(conv_weight), hbm(norm_gain)
    shape = jax.ShapeDtypeStruct
    wide = shape((chunks, count, LANES), jnp.float32)
    padded = shape((chunks, count + 2 * EDGE, LANES), jnp.float32)
    lane = shape((count, LANES), jnp.float32)
    buffer = shape((2 * rows, width), jnp.bfloat16)
    half = shape(((kernel + 1) // 2, width), jnp.float32)
    left, right = shifted(frames[0, count - EDGE :], frames[0, :EDGE])
    conv, pad, squares, pick, grads, taps = pl.pallas_call(
        pre_kernel,
        out_shape=[
            wide, padded, lane, shape((2 * rows, count), jnp.bfloat16), buffer,
            shape((chunks, 32, LANES), jnp.float32),
        ],
        in_specs=[SMEM] + [HBM] * 5,
        out_specs=[VMEM] * 6,
        scratch_shapes=[
            pltpu.VMEM((1, count), jnp.int32),
            pltpu.VMEM((count, width), jnp.bfloat16),
            pltpu.VMEM((count, width), jnp.bfloat16),
            pltpu.VMEM((kernel, width), jnp.float32),
            pltpu.VMEM((width,), jnp.float32),
            pltpu.VMEM((count, width), jnp.bfloat16),
            pltpu.SemaphoreType.DMA((5,)),
        ],
        compiler_params=limit(20),
        cost_estimate=cost(6 * 10**9, 2 * 10**7),
        name="pre",
    )(scalars, row, x, cot, conv_weight, norm_gain)
    conv, pad, send, inv = pl.pallas_call(
        send_kernel,
        out_shape=[wide, padded, buffer, lane],
        in_specs=[SMEM] + [VMEM] * 8,
        out_specs=[VMEM] * 4,
        scratch_shapes=[
            pltpu.VMEM((count, width), jnp.bfloat16),
            pltpu.VMEM((count, LANES), jnp.float32),
        ],
        compiler_params=limit(20),
        cost_estimate=cost(10**9, 10**7),
        name="send",
    )(scalars, left, right, conv, pad, squares, pick, grads, taps)
    recv = lax.all_to_all(send, ("rec", "tm"), split_axis=0, concat_axis=0, tiled=True)
    wide_rows = shape((rows, hidden), jnp.bfloat16)
    back, act, d_pre = pl.pallas_call(
        expert_kernel,
        out_shape=[pltpu.HBM(v.shape, v.dtype) for v in (buffer, wide_rows, wide_rows)],
        in_specs=[HBM] * 3,
        out_specs=[HBM] * 3,
        scratch_shapes=[
            pltpu.VMEM((2 * rows, width), jnp.bfloat16),
            pltpu.VMEM((width, hidden), jnp.bfloat16),
            pltpu.VMEM((hidden, width), jnp.bfloat16),
            pltpu.VMEM((rows, width), jnp.bfloat16),
            pltpu.VMEM((rows, width), jnp.bfloat16),
            pltpu.VMEM((rows, hidden), jnp.bfloat16),
            pltpu.VMEM((rows, hidden), jnp.bfloat16),
            pltpu.VMEM((rows, width), jnp.float32),
            pltpu.VMEM((rows, width), jnp.float32),
            pltpu.SemaphoreType.DMA((2, rows // 128)),
            pltpu.SemaphoreType.DMA((2, hidden // TILE)),
            pltpu.SemaphoreType.DMA((2, hidden // TILE)),
        ],
        compiler_params=limit(40),
        cost_estimate=cost(8 * rows * width * hidden, 2 * 10**7),
        name="experts",
    )(hbm(recv), win, wout)
    home = lax.all_to_all(back, ("rec", "tm"), split_axis=0, concat_axis=0, tiled=True)
    grad_in, grad_out, done = pl.pallas_call(
        grads_kernel,
        grid=(hidden // TILE,),
        out_shape=[
            shape((1, width, hidden), jnp.bfloat16),
            shape((1, hidden, width), jnp.bfloat16),
            shape((8, LANES), jnp.float32),
        ],
        in_specs=[
            pl.BlockSpec((2 * rows, width), lambda i: (0, 0)),
            pl.BlockSpec((rows, TILE), lambda i: (0, i)),
            pl.BlockSpec((rows, TILE), lambda i: (0, i)),
        ],
        out_specs=[
            pl.BlockSpec((1, width, TILE), lambda i: (0, 0, i)),
            pl.BlockSpec((1, TILE, width), lambda i: (0, i, 0)),
            pl.BlockSpec((8, LANES), lambda i: (0, 0)),
        ],
        scratch_shapes=[
            pltpu.VMEM((rows, width), jnp.bfloat16),
            pltpu.VMEM((rows, width), jnp.bfloat16),
        ],
        compiler_params=limit(24),
        cost_estimate=cost(4 * rows * width * hidden, 2 * 10**7),
        name="weight_grads",
    )(hbm(recv), hbm(act), hbm(d_pre))
    edges = shape((chunks, EDGE, LANES), jnp.float32)
    output, d_conv, head, tail, mine, other = pl.pallas_call(
        post_kernel,
        out_shape=[shape((count, width), jnp.bfloat16), wide, edges, edges, half, half],
        in_specs=[SMEM] + [HBM] * 7 + [ANY],
        out_specs=[VMEM] * 6,
        scratch_shapes=[
            pltpu.VMEM((1, count), jnp.int32),
            pltpu.VMEM((2 * rows, width), jnp.bfloat16),
            pltpu.VMEM((count, width), jnp.bfloat16),
            pltpu.VMEM((count, LANES), jnp.float32),
            pltpu.VMEM(wide.shape, jnp.float32),
            pltpu.VMEM((chunks, 32, LANES), jnp.float32),
            pltpu.VMEM(padded.shape, jnp.float32),
            pltpu.VMEM((count, width), jnp.float32),
            pltpu.VMEM((count, width), jnp.float32),
            pltpu.VMEM((count, LANES), jnp.float32),
            pltpu.VMEM((kernel + 1, width), jnp.float32),
            pltpu.SemaphoreType.DMA((7,)),
        ],
        compiler_params=limit(24),
        cost_estimate=cost(10**9, 10**7),
        name="post",
    )(scalars, row, hbm(home), cot, hbm(inv), hbm(conv), hbm(taps), hbm(pad), done)
    left, right = shifted(tail, head)

    def back_part(first, tie):
        return pl.pallas_call(
            functools.partial(back_kernel, first),
            out_shape=shape((count, 2 * LANES), jnp.bfloat16),
            in_specs=[SMEM] + [VMEM] * 4 + [ANY],
            out_specs=VMEM,
            scratch_shapes=[
                pltpu.VMEM((2, ROWS + 2 * EDGE, LANES), jnp.float32),
                pltpu.VMEM((2, ROWS + 2 * EDGE, LANES), jnp.float32),
            ],
            compiler_params=limit(8),
            cost_estimate=cost(10**9, 4 * 10**6),
            name="conv_back",
        )(scalars, d_conv, left, right, taps, tie)

    def add(part, others, tie):
        return pl.pallas_call(
            add_kernel,
            out_shape=half,
            in_specs=[ANY] + [VMEM] * 4,
            out_specs=VMEM,
            compiler_params=limit(4),
            name="ring_add",
        )(tie, part, *others)

    n_rec, n_tm = lax.axis_size("rec"), lax.axis_size("tm")
    swap = [(i, i ^ 1) for i in range(n_tm)]
    part = mine + lax.ppermute(other, "tm", swap)
    pieces = []
    for axis, size, step in (("tm", n_tm, 2), ("rec", n_rec, 1), ("tm", n_tm, 8)):
        others = [
            lax.ppermute(part, axis, [(i, i ^ (step * flip)) for i in range(size)])
            for flip in (1, 2, 3)
        ]
        pieces.append(back_part(2 * len(pieces), part))
        part = add(part, others, pieces[-1])
    fellow = lax.ppermute(part, "tm", swap)
    grad_conv, grad_gain, grad_frames = pl.pallas_call(
        functools.partial(finish_kernel, 1.0 / math.sqrt(n_rec * n_tm * count)),
        out_shape=[
            shape((kernel, width), jnp.float32),
            shape((width,), jnp.float32),
            shape((count, width), jnp.bfloat16),
        ],
        in_specs=[SMEM] + [VMEM] * 5,
        out_specs=[VMEM] * 3,
        compiler_params=limit(8),
        name="finish",
    )(scalars, part, fellow, *pieces)
    return output[None], grad_frames[None], grad_conv, grad_gain, grad_in, grad_out


def solution(mesh):
    placed = (
        P("rec", "tm", None),
        P("rec", "tm", None),
        P("rec", "tm", None),
        P("rec"),
        P(),
        P(),
        P(("rec", "tm"), None, None),
        P(("rec", "tm"), None, None),
    )
    return jax.shard_map(
        local,
        mesh=mesh,
        in_specs=placed,
        out_specs=(
            P("rec", "tm", None),
            P("rec", "tm", None),
            P(),
            P(),
            P(("rec", "tm"), None, None),
            P(("rec", "tm"), None, None),
        ),
        check_vma=False,
    )
```

time: 162 us -> 141 us (0.87)
  waiting for transfers between devices: 33 us -> 18.3 us
  local copies, waits for them, and re-layouts: 14.8 us -> 1.97 us
  Pallas kernels: 42.8 us -> 49.4 us
    unnamed x36 -> x12, local copies, waits for them, and re-layouts: 12 us -> 1.21 us
    all_to_all x1, waiting for transfers between devices: 24.7 us -> 14.3 us  [local(): lax.all_to_all(back, ('rec', 'tm'), split_axis=0, concat_axis=0, tiled=True)]
    pallas_call x4 -> x11, Pallas kernels: 34.1 us -> 42.3 us  [the longest x1 18 us: local(): pl.pallas_call(expert_kernel, out_shape=[pltpu.HBM(v.shape, v.dtype) for...]
    ppermute x11, starting transfers between devices: 11.2 us -> 17.1 us  [the longest x9 9.99 us: local(): lax.ppermute(part, axis, [(i, i ^ step * flip) for i in range(size)])]
    ppermute x2, starting transfers between devices: 9.9 us -> 5.21 us  [shifted(): left = lax.ppermute(tail, 'tm', [(i, i + 1) for i in range(n - 1)])]
    ppermute x2, waiting for transfers between devices: 3.06 us -> 0.01 us  [shifted(): right = lax.ppermute(head, 'tm', [(i + 1, i) for i in range(n - 1)])]
  transfers between devices with their start and end apart: 16 -> 16, of which waited for: 9 -> 6; matrix products, arithmetic and copies ran while one was open for 1% -> 0% of each run, Pallas kernels for 8% -> 15%
where the time goes in v2:
time: 141 us; the launch traced here: 140 us
  Pallas kernels  49.4 us (35%)
  blocking collectives  36.6 us (26%)
  starting transfers between devices  32.3 us (23%)
  waiting for transfers between devices  18.3 us (13%)
  local copies, waits for them, and re-layouts  1.97 us (1%)
  between operations  1.51 us (1%)
    all_to_all x1, blocking collectives, local(): lax.all_to_all(send, ('rec', 'tm'), split_axis=0, concat_axis=0, tiled=True)  36.6 us
    pallas_call x1, Pallas kernels, local(): pl.pallas_call(expert_kernel, out_shape=[pltpu.HBM(v.shape, v.dtype) for...  18 us
    all_to_all x1, waiting for transfers between devices, local(): lax.all_to_all(back, ('rec', 'tm'), split_axis=0, concat_axis=0, tiled=True)  14.3 us
    pallas_call x1, Pallas kernels, local(): pl.pallas_call(grads_kernel, grid=(hidden // TILE,), out_shape=[shape((1,...  10.7 us
    ppermute x9, starting transfers between devices, local(): lax.ppermute(part, axis, [(i, i ^ step * flip) for i in range(size)])  9.99 us
    pallas_call x1, Pallas kernels, local(): pl.pallas_call(post_kernel, out_shape=[shape((count, width), jnp.bfloat16...  7.15 us
    ppermute x1, starting transfers between devices, local(): fellow = lax.ppermute(part, 'tm', swap)  6.16 us
    pallas_call x1, Pallas kernels, local(): pl.pallas_call(pre_kernel, out_shape=[wide, padded, lane, shape((2 * rows...  5.77 us
  transfers between devices with their start and end apart: 16, of which 6 were waited for; matrix products, arithmetic and copies ran while one was open for 0% of the time, Pallas kernels for 15%

profile of v2, /device:TPU:1, one launch (start us, length us, event | category | flops | bytes accessed | tf_op | source)
XLA Modules:
  0.0 140.1 jit_solution(6156168224883750915)
XLA Ops:
  0.6 0.8 slice_bitcast_fusion
  1.4 3.3 %collective-permute-start.1 = (bf16[16,768]{1,0:T(8,128)(2,1)S(1)}, bf16[16,768]{1,0:T(8,128)(2,1)S(1)}, u32[]{:S(2)}, u32[]{:S(2)}) collective-permute-start(bf16[16,768]{1,0:T(8,128)(2,1)S(1)} %get-tuple-element.56), channel_id=1, source_target_pairs={{1,0},{2,1},{3,2},{4,3},{5,4},{6,5},{7,6},{8,7},{9,8},{10,9},{11,1... | collective-permute-start | bytes 73736 | tf_op jit(solution)/shard_map/ppermute | solution.py:389
  4.7 3.1 %collective-permute-start = (bf16[16,768]{1,0:T(8,128)(2,1)S(1)}, bf16[16,768]{1,0:T(8,128)(2,1)S(1)}, u32[]{:S(2)}, u32[]{:S(2)}) collective-permute-start(bf16[16,768]{1,0:T(8,128)(2,1)S(1)} %get-tuple-element.57), channel_id=1, source_target_pairs={{0,1},{1,2},{2,3},{3,4},{4,5},{5,6},{6,7},{7,8},{8,9},{9,10},{10,1... | collective-permute-start | bytes 73736 | tf_op jit(solution)/shard_map/ppermute | solution.py:388
  8.5 0.1 pad_add_fusion.nv_ref
  8.6 5.8 %pre.1 = (f32[6,384,128]{2,1,0:T(8,128)S(1)}, f32[6,416,128]{2,1,0:T(8,128)S(1)}, f32[384,128]{1,0:T(8,128)S(1)}, bf16[1024,384]{1,0:T(8,128)(2,1)S(1)}, bf16[10...) custom-call(s32[2]{0:T(128)S(1)} %pad_add_fusion.nv_ref, s32[1,384]{1,0:T(1,128)} %bitcast.27, ...), custom_call_target="tpu_custom_call" | custom-call | flops 6000000000 | bytes 20000000 | tf_op jit(solution)/shard_map/pre/pallas_call | solution.py:413
  14.3 0.0 copy-start.2
  14.4 0.0 collective-permute-done.1.right_ref
  14.4 0.0 collective-permute-done.left_ref
  14.4 2.0 %send.1 = (f32[6,384,128]{2,1,0:T(8,128)S(1)}, f32[6,416,128]{2,1,0:T(8,128)S(1)}, bf16[1024,768]{1,0:T(8,128)(2,1)S(1)}, f32[384,128]{1,0:T(8,128)S(1)}) custom-call(s32[2]{0:T(128)S(1)} %pad_add_fusion.nv_ref, bf16[16,768]{1,0:T(8,128)(2,1)S(1)} %collective-permute-done.left_ref, bf16[16,768]{1,0:T(8,128)(2,1)S(1)} %collective-permute-done.1.right_ref, ...), custom_call_target="tpu_custom_call" | custom-call | flops 1000000000 | bytes 10000000 | tf_op jit(solution)/shard_map/send/pallas_call | solution.py:434
  16.4 0.0 copy-done.2
  16.4 0.0 copy-start
  16.4 0.0 copy-start.1
  16.4 0.0 copy-start.4
  16.4 36.6 %all_to_all.22 = bf16[128,8,768]{2,1,0:T(8,128)(2,1)} all-to-all(bf16[128,8,768]{2,1,0:T(8,128)(2,1)S(1)} %bitcast.19), channel_id=1, replica_groups=mesh['rec'=4,'tm'=32] {'rec','tm'}, dimensions={0} | all-to-all | bytes 3145728 | tf_op jit(solution)/shard_map/all_to_all | solution.py:447
  53.0 0.0 copy-done
  53.0 0.0 copy-done.1
  53.0 0.0 copy-done.4
  53.0 18.0 %experts.1 = (bf16[1024,768]{1,0:T(8,128)(2,1)}, bf16[512,3072]{1,0:T(8,128)(2,1)}, bf16[512,3072]{1,0:T(8,128)(2,1)}) custom-call(bf16[1024,768]{1,0:T(8,128)(2,1)} %bitcast.21, bf16[768,3072]{1,0:T(8,128)(2,1)} %bitcast.29, bf16[3072,768]{1,0:T(8,128)(2,1)} %bitcast.30), custom_call_target="tpu_custom_call" | custom-call | flops 9663676416 | bytes 20000000 | tf_op jit(solution)/shard_map/experts/pallas_call | solution.py:449
  71.0 4.4 %all-to-all-start.1 = ((bf16[128,8,768]{2,1,0:T(8,128)(2,1)}), bf16[128,8,768]{2,1,0:T(8,128)(2,1)S(1)}, u32[]{:S(2)}, u32[]{:S(2)}) async-start(bf16[128,8,768]{2,1,0:T(8,128)(2,1)} %bitcast.23), calls=%async_computation.1 | async-start | bytes 3145728 | tf_op jit(solution)/shard_map/all_to_all | solution.py:472
  75.4 10.7 %weight_grads.1 = (bf16[1,768,3072]{2,1,0:T(8,128)(2,1)}, bf16[1,3072,768]{2,1,0:T(8,128)(2,1)}, f32[8,128]{1,0:T(8,128)S(1)}) custom-call(bf16[1024,768]{1,0:T(8,128)(2,1)} %bitcast.22, bf16[512,3072]{1,0:T(8,128)(2,1)} %get-tuple-element.42.act_ref, bf16[512,3072]{1,0:T(8,128)(2,1)} %get-tuple-element.43.dpre_ref), custom_call_target="tpu_custom_call" | custom-call | flops 4831838208 | bytes 20000000 | tf_op jit(solution)/shard_map/weight_grads/pallas_call | solution.py:473
  86.1 14.3 %all-to-all-done.1 = bf16[128,8,768]{2,1,0:T(8,128)(2,1)S(1)} async-done(((bf16[128,8,768]{2,1,0:T(8,128)(2,1)}), bf16[128,8,768]{2,1,0:T(8,128)(2,1)S(1)}, u32[]{:S(2)}, u32[]{:S(2)}) %all-to-all-start.1) | async-done | bytes 1572896 | tf_op jit(solution)/shard_map/all_to_all | solution.py:472
  100.4 0.0 copy-start.5
  100.4 1.2 copy-done.5
  101.6 0.0 copy-start.3
  101.6 7.1 %post.1 = (bf16[384,768]{1,0:T(8,128)(2,1)}, f32[6,384,128]{2,1,0:T(8,128)S(1)}, f32[6,16,128]{2,1,0:T(8,128)S(1)}, f32[6,16,128]{2,1,0:T(8,128)S(1)}, f32[16,768]{1,0:T(8,128)S(1)}, /*index=5*/f32[16,768]{1,0:T(8,128)S(1)}) custom-call(s32[2]{0:T(128)S(1)} %pad_add_fusion.nv_ref, s32[1,384]{1,0:T(1,128)} %bitcast.28, bf16[1024,768]{1,0:T(8,128)(2,1)} %bitcast.20, ...), custom_call_target="tpu_custom_call" | custom-call | flops 1000000000 | bytes 10000000 | tf_op jit(solution)/shard_map/post/pallas_call | solution.py:500
  108.8 1.0 collective-permute-start.4
  109.8 2.1 %collective-permute-start.2 = (f32[6,16,128]{2,1,0:T(8,128)S(1)}, f32[6,16,128]{2,1,0:T(8,128)S(1)}, u32[]{:S(2)}, u32[]{:S(2)}) collective-permute-start(f32[6,16,128]{2,1,0:T(8,128)S(1)} %get-tuple-element.47), channel_id=1, source_target_pairs={{0,1},{1,2},{2,3},{3,4},{4,5},{5,6},{6,7},{7,8},{8,9},{9,10},{10,1... | collective-permute-start | bytes 147464 | tf_op jit(solution)/shard_map/ppermute | solution.py:388
  111.9 2.2 %collective-permute-start.3 = (f32[6,16,128]{2,1,0:T(8,128)S(1)}, f32[6,16,128]{2,1,0:T(8,128)S(1)}, u32[]{:S(2)}, u32[]{:S(2)}) collective-permute-start(f32[6,16,128]{2,1,0:T(8,128)S(1)} %get-tuple-element.48), channel_id=1, source_target_pairs={{1,0},{2,1},{3,2},{4,3},{5,4},{6,5},{7,6},{8,7},{9,8},{10,9},{11,1... | collective-permute-start | bytes 147464 | tf_op jit(solution)/shard_map/ppermute | solution.py:389
  114.1 0.0 collective-permute-done.4
  114.1 2.0 %collective-permute-start.7 = (f32[16,768]{1,0:T(8,128)S(1)}, f32[16,768]{1,0:T(8,128)S(1)}, u32[]{:S(2)}, u32[]{:S(2)}) collective-permute-start(f32[16,768]{1,0:T(8,128)S(1)} %add.8.tie_ref.own_ref), channel_id=1, source_target_pairs={{0,6},{1,7},{2,4},{3,5},{4,2},{5,3},{6,0},{7,1},{8,14},{9,15},{10,... | collective-permute-start | bytes 147464 | tf_op jit(solution)/shard_map/ppermute | solution.py:556
  116.1 0.2 collective-permute-start.6
  116.3 1.2 collective-permute-start.5
  117.5 0.0 collective-permute-done.2.left_ref
  117.5 0.0 collective-permute-done.3.right_ref
  117.5 0.0 copy-done.3
  117.5 1.5 %conv_back.3.tie_ref.refs_0_ = bf16[384,256]{1,0:T(8,128)(2,1)S(1)} custom-call(s32[2]{0:T(128)S(1)} %pad_add_fusion.nv_ref, f32[6,384,128]{2,1,0:T(8,128)S(1)} %get-tuple-element.46.dconv_ref, f32[6,16,128]{2,1,0:T(8,128)S(1)} %collective-permute-done.2.left_ref, f32[6,16,128]{2,1,0:T(8,128)S(1)} %collective-permute-done.3.right_ref, ...), custom_call_target="tpu_custom_call" | custom-call | flops 1000000000 | bytes 4000000 | tf_op jit(solution)/shard_map/conv_back/pallas_call | solution.py:526
  118.9 0.0 collective-permute-done.7.three_ref
  118.9 2.0 %collective-permute-done.6.two_ref = f32[16,768]{1,0:T(8,128)S(1)} collective-permute-done((f32[16,768]{1,0:T(8,128)S(1)}, f32[16,768]{1,0:T(8,128)S(1)}, u32[]{:S(2)}, u32[]{:S(2)}) %collective-permute-start.6) | collective-permute-done | bytes 49184 | tf_op jit(solution)/shard_map/ppermute | solution.py:556
  120.9 0.0 collective-permute-done.5.one_ref
  121.0 0.5 collective-permute-start.10
  121.4 1.3 collective-permute-start.9
  122.7 1.6 %collective-permute-start.8 = (f32[16,768]{1,0:T(8,128)S(1)}, f32[16,768]{1,0:T(8,128)S(1)}, u32[]{:S(2)}, u32[]{:S(2)}) collective-permute-start(f32[16,768]{1,0:T(8,128)S(1)} %ring_add.3.tie_ref.own_ref), channel_id=1, source_target_pairs={{0,32},{32,0},{64,96},{96,64},{1,33},{33,1},{65,97},{97,65},{2,34}... | collective-permute-start | bytes 147464 | tf_op jit(solution)/shard_map/ppermute | solution.py:556
  124.3 1.5 %conv_back.4.tie_ref.refs_1_ = bf16[384,256]{1,0:T(8,128)(2,1)S(1)} custom-call(s32[2]{0:T(128)S(1)} %pad_add_fusion.nv_ref, f32[6,384,128]{2,1,0:T(8,128)S(1)} %get-tuple-element.46.dconv_ref, f32[6,16,128]{2,1,0:T(8,128)S(1)} %collective-permute-done.2.left_ref, f32[6,16,128]{2,1,0:T(8,128)S(1)} %collective-permute-done.3.right_ref, ...), custom_call_target="tpu_custom_call" | custom-call | flops 1000000000 | bytes 4000000 | tf_op jit(solution)/shard_map/conv_back/pallas_call | solution.py:526
  125.7 0.0 collective-permute-done.10.three_ref
  125.8 0.1 collective-permute-done.9.two_ref
  125.9 0.4 collective-permute-done.8.one_ref
  126.3 0.1 collective-permute-start.13
  126.4 0.8 collective-permute-start.12
  127.2 2.4 %collective-permute-start.11 = (f32[16,768]{1,0:T(8,128)S(1)}, f32[16,768]{1,0:T(8,128)S(1)}, u32[]{:S(2)}, u32[]{:S(2)}) collective-permute-start(f32[16,768]{1,0:T(8,128)S(1)} %ring_add.4.tie_ref.own_ref), channel_id=1, source_target_pairs={{0,8},{1,9},{2,10},{3,11},{4,12},{5,13},{6,14},{7,15},{8,0},{9,1},... | collective-permute-start | bytes 147464 | tf_op jit(solution)/shard_map/ppermute | solution.py:556
  129.6 1.5 %conv_back.5.tie_ref.refs_2_ = bf16[384,256]{1,0:T(8,128)(2,1)S(1)} custom-call(s32[2]{0:T(128)S(1)} %pad_add_fusion.nv_ref, f32[6,384,128]{2,1,0:T(8,128)S(1)} %get-tuple-element.46.dconv_ref, f32[6,16,128]{2,1,0:T(8,128)S(1)} %collective-permute-done.2.left_ref, f32[6,16,128]{2,1,0:T(8,128)S(1)} %collective-permute-done.3.right_ref, ...), custom_call_target="tpu_custom_call" | custom-call | flops 1000000000 | bytes 4000000 | tf_op jit(solution)/shard_map/conv_back/pallas_call | solution.py:526
  131.1 0.0 collective-permute-done.13.three_ref
  131.1 0.0 collective-permute-done.12.two_ref
  131.1 0.5 collective-permute-done.11.one_ref
  131.7 6.2 %collective-permute-start.14 = (f32[16,768]{1,0:T(8,128)S(1)}, f32[16,768]{1,0:T(8,128)S(1)}, u32[]{:S(2)}, u32[]{:S(2)}) collective-permute-start(f32[16,768]{1,0:T(8,128)S(1)} %ring_add.5.part_ref), channel_id=1, source_target_pairs={{0,1},{1,0},{2,3},{3,2},{4,5},{5,4},{6,7},{7,6},{8,9},{9,8},{10,11... | collective-permute-start | bytes 147464 | tf_op jit(solution)/shard_map/ppermute | solution.py:561
  137.8 0.9 collective-permute-done.14.fellow_ref
  138.7 1.4 %finish.1 = (f32[31,768]{1,0:T(8,128)}, f32[768]{0:T(1024)}, bf16[384,768]{1,0:T(8,128)(2,1)}) custom-call(s32[2]{0:T(128)S(1)} %pad_add_fusion.nv_ref, f32[16,768]{1,0:T(8,128)S(1)} %ring_add.5.part_ref, f32[16,768]{1,0:T(8,128)S(1)} %collective-permute-done.14.fellow_ref, bf16[384,256]{1,0:T(8,128)(2,1)S(1)} %conv_back.3.tie_ref.refs_0_, ...), custom_call_target="tpu_custom_call" | custom-call | tf_op jit(solution)/shard_map/finish/pallas_call | solution.py:562
  (4 shorter events, 0.0 us)
Async XLA Ops:
  1.4 13.0 %collective-permute-start.1 = (bf16[16,768]{1,0:T(8,128)(2,1)S(1)}, bf16[16,768]{1,0:T(8,128)(2,1)S(1)}, u32[]{:S(2)}, u32[]{:S(2)}) collective-permute-start(bf16[16,768]{1,0:T(8,128)(2,1)S(1)} %get-tuple-element.56), channel_id=1, source_target_pairs={{1,0},{2,1},{3,2},{4,3},{5,4},{6,5},{7,6},{8,7},{9,8},{10,9},{11,1... | collective-permute-start | bytes 73736 | tf_op jit(solution)/shard_map/ppermute | solution.py:389
  4.7 9.6 %collective-permute-start = (bf16[16,768]{1,0:T(8,128)(2,1)S(1)}, bf16[16,768]{1,0:T(8,128)(2,1)S(1)}, u32[]{:S(2)}, u32[]{:S(2)}) collective-permute-start(bf16[16,768]{1,0:T(8,128)(2,1)S(1)} %get-tuple-element.57), channel_id=1, source_target_pairs={{0,1},{1,2},{2,3},{3,4},{4,5},{5,6},{6,7},{7,8},{8,9},{9,10},{10,1... | collective-permute-start | bytes 73736 | tf_op jit(solution)/shard_map/ppermute | solution.py:388
  14.3 2.0 %copy-start.2 = (f32[6,32,128]{2,1,0:T(8,128)}, f32[6,32,128]{2,1,0:T(8,128)S(1)}, u32[]{:S(2)}) copy-start(f32[6,32,128]{2,1,0:T(8,128)S(1)} %get-tuple-element.36.taps_ref.taps_hbm) | copy-start | bytes 294916
  16.4 36.6 %copy-start = (f32[6,416,128]{2,1,0:T(8,128)}, f32[6,416,128]{2,1,0:T(8,128)S(1)}, u32[]{:S(2)}) copy-start(f32[6,416,128]{2,1,0:T(8,128)S(1)} %get-tuple-element.41.pad_hbm) | copy-start | bytes 3833860
  16.4 36.6 %copy-start.1 = (f32[6,384,128]{2,1,0:T(8,128)}, f32[6,384,128]{2,1,0:T(8,128)S(1)}, u32[]{:S(2)}) copy-start(f32[6,384,128]{2,1,0:T(8,128)S(1)} %get-tuple-element.40.conv_hbm) | copy-start | bytes 3538948
  16.4 36.6 %copy-start.4 = (f32[384,128]{1,0:T(8,128)}, f32[384,128]{1,0:T(8,128)S(1)}, u32[]{:S(2)}) copy-start(f32[384,128]{1,0:T(8,128)S(1)} %get-tuple-element.39.inv_hbm) | copy-start | bytes 589828
  71.0 29.4 %all-to-all-start.1 = ((bf16[128,8,768]{2,1,0:T(8,128)(2,1)}), bf16[128,8,768]{2,1,0:T(8,128)(2,1)S(1)}, u32[]{:S(2)}, u32[]{:S(2)}) async-start(bf16[128,8,768]{2,1,0:T(8,128)(2,1)} %bitcast.23), calls=%async_computation.1 | async-start | bytes 3145728 | tf_op jit(solution)/shard_map/all_to_all | solution.py:472
  100.4 1.2 copy-start.5
  101.6 15.9 %copy-start.3 = (f32[6,32,128]{2,1,0:T(8,128)S(1)}, f32[6,32,128]{2,1,0:T(8,128)}, u32[]{:S(2)}) copy-start(f32[6,32,128]{2,1,0:T(8,128)} %copy-done.2) | copy-start | bytes 294916
  108.8 5.3 %collective-permute-start.4 = (f32[16,768]{1,0:T(8,128)S(1)}, f32[16,768]{1,0:T(8,128)S(1)}, u32[]{:S(2)}, u32[]{:S(2)}) collective-permute-start(f32[16,768]{1,0:T(8,128)S(1)} %get-tuple-element.50), channel_id=1, source_target_pairs={{0,1},{1,0},{2,3},{3,2},{4,5},{5,4},{6,7},{7,6},{8,9},{9,8},{10,11... | collective-permute-start | bytes 147464 | tf_op jit(solution)/shard_map/ppermute | solution.py:552
  109.8 7.7 %collective-permute-start.2 = (f32[6,16,128]{2,1,0:T(8,128)S(1)}, f32[6,16,128]{2,1,0:T(8,128)S(1)}, u32[]{:S(2)}, u32[]{:S(2)}) collective-permute-start(f32[6,16,128]{2,1,0:T(8,128)S(1)} %get-tuple-element.47), channel_id=1, source_target_pairs={{0,1},{1,2},{2,3},{3,4},{4,5},{5,6},{6,7},{7,8},{8,9},{9,10},{10,1... | collective-permute-start | bytes 147464 | tf_op jit(solution)/shard_map/ppermute | solution.py:388
  111.9 5.6 %collective-permute-start.3 = (f32[6,16,128]{2,1,0:T(8,128)S(1)}, f32[6,16,128]{2,1,0:T(8,128)S(1)}, u32[]{:S(2)}, u32[]{:S(2)}) collective-permute-start(f32[6,16,128]{2,1,0:T(8,128)S(1)} %get-tuple-element.48), channel_id=1, source_target_pairs={{1,0},{2,1},{3,2},{4,3},{5,4},{6,5},{7,6},{8,7},{9,8},{10,9},{11,1... | collective-permute-start | bytes 147464 | tf_op jit(solution)/shard_map/ppermute | solution.py:389
  114.1 4.8 %collective-permute-start.7 = (f32[16,768]{1,0:T(8,128)S(1)}, f32[16,768]{1,0:T(8,128)S(1)}, u32[]{:S(2)}, u32[]{:S(2)}) collective-permute-start(f32[16,768]{1,0:T(8,128)S(1)} %add.8.tie_ref.own_ref), channel_id=1, source_target_pairs={{0,6},{1,7},{2,4},{3,5},{4,2},{5,3},{6,0},{7,1},{8,14},{9,15},{10,... | collective-permute-start | bytes 147464 | tf_op jit(solution)/shard_map/ppermute | solution.py:556
  116.1 4.8 %collective-permute-start.6 = (f32[16,768]{1,0:T(8,128)S(1)}, f32[16,768]{1,0:T(8,128)S(1)}, u32[]{:S(2)}, u32[]{:S(2)}) collective-permute-start(f32[16,768]{1,0:T(8,128)S(1)} %add.8.tie_ref.own_ref), channel_id=1, source_target_pairs={{0,4},{1,5},{2,6},{3,7},{4,0},{5,1},{6,2},{7,3},{8,12},{9,13},{10,... | collective-permute-start | bytes 147464 | tf_op jit(solution)/shard_map/ppermute | solution.py:556
  116.3 4.6 %collective-permute-start.5 = (f32[16,768]{1,0:T(8,128)S(1)}, f32[16,768]{1,0:T(8,128)S(1)}, u32[]{:S(2)}, u32[]{:S(2)}) collective-permute-start(f32[16,768]{1,0:T(8,128)S(1)} %add.8.tie_ref.own_ref), channel_id=1, source_target_pairs={{0,2},{1,3},{2,0},{3,1},{4,6},{5,7},{6,4},{7,5},{8,10},{9,11},{10,... | collective-permute-start | bytes 147464 | tf_op jit(solution)/shard_map/ppermute | solution.py:556
  121.0 4.8 %collective-permute-start.10 = (f32[16,768]{1,0:T(8,128)S(1)}, f32[16,768]{1,0:T(8,128)S(1)}, u32[]{:S(2)}, u32[]{:S(2)}) collective-permute-start(f32[16,768]{1,0:T(8,128)S(1)} %ring_add.3.tie_ref.own_ref), channel_id=1, source_target_pairs={{0,96},{32,64},{64,32},{96,0},{1,97},{33,65},{65,33},{97,1},{2,98}... | collective-permute-start | bytes 147464 | tf_op jit(solution)/shard_map/ppermute | solution.py:556
  121.4 4.4 %collective-permute-start.9 = (f32[16,768]{1,0:T(8,128)S(1)}, f32[16,768]{1,0:T(8,128)S(1)}, u32[]{:S(2)}, u32[]{:S(2)}) collective-permute-start(f32[16,768]{1,0:T(8,128)S(1)} %ring_add.3.tie_ref.own_ref), channel_id=1, source_target_pairs={{0,64},{32,96},{64,0},{96,32},{1,65},{33,97},{65,1},{97,33},{2,66}... | collective-permute-start | bytes 147464 | tf_op jit(solution)/shard_map/ppermute | solution.py:556
  122.7 3.6 %collective-permute-start.8 = (f32[16,768]{1,0:T(8,128)S(1)}, f32[16,768]{1,0:T(8,128)S(1)}, u32[]{:S(2)}, u32[]{:S(2)}) collective-permute-start(f32[16,768]{1,0:T(8,128)S(1)} %ring_add.3.tie_ref.own_ref), channel_id=1, source_target_pairs={{0,32},{32,0},{64,96},{96,64},{1,33},{33,1},{65,97},{97,65},{2,34}... | collective-permute-start | bytes 147464 | tf_op jit(solution)/shard_map/ppermute | solution.py:556
  126.3 4.8 %collective-permute-start.13 = (f32[16,768]{1,0:T(8,128)S(1)}, f32[16,768]{1,0:T(8,128)S(1)}, u32[]{:S(2)}, u32[]{:S(2)}) collective-permute-start(f32[16,768]{1,0:T(8,128)S(1)} %ring_add.4.tie_ref.own_ref), channel_id=1, source_target_pairs={{0,24},{1,25},{2,26},{3,27},{4,28},{5,29},{6,30},{7,31},{8,16},{9,... | collective-permute-start | bytes 147464 | tf_op jit(solution)/shard_map/ppermute | solution.py:556
  126.4 4.7 %collective-permute-start.12 = (f32[16,768]{1,0:T(8,128)S(1)}, f32[16,768]{1,0:T(8,128)S(1)}, u32[]{:S(2)}, u32[]{:S(2)}) collective-permute-start(f32[16,768]{1,0:T(8,128)S(1)} %ring_add.4.tie_ref.own_ref), channel_id=1, source_target_pairs={{0,16},{1,17},{2,18},{3,19},{4,20},{5,21},{6,22},{7,23},{8,24},{9,... | collective-permute-start | bytes 147464 | tf_op jit(solution)/shard_map/ppermute | solution.py:556
  127.2 4.4 %collective-permute-start.11 = (f32[16,768]{1,0:T(8,128)S(1)}, f32[16,768]{1,0:T(8,128)S(1)}, u32[]{:S(2)}, u32[]{:S(2)}) collective-permute-start(f32[16,768]{1,0:T(8,128)S(1)} %ring_add.4.tie_ref.own_ref), channel_id=1, source_target_pairs={{0,8},{1,9},{2,10},{3,11},{4,12},{5,13},{6,14},{7,15},{8,0},{9,1},... | collective-permute-start | bytes 147464 | tf_op jit(solution)/shard_map/ppermute | solution.py:556
  131.7 7.0 %collective-permute-start.14 = (f32[16,768]{1,0:T(8,128)S(1)}, f32[16,768]{1,0:T(8,128)S(1)}, u32[]{:S(2)}, u32[]{:S(2)}) collective-permute-start(f32[16,768]{1,0:T(8,128)S(1)} %ring_add.5.part_ref), channel_id=1, source_target_pairs={{0,1},{1,0},{2,3},{3,2},{4,5},{5,4},{6,7},{7,6},{8,9},{9,8},{10,11... | collective-permute-start | bytes 147464 | tf_op jit(solution)/shard_map/ppermute | solution.py:561

commit v3 on v2

--- a/solution.py
+++ b/solution.py
@@ -37,6 +37,10 @@
 
 def limit(mebibytes):
     return pltpu.CompilerParams(vmem_limit_bytes=mebibytes * 1024 * 1024)
+
+
+def vmem(x):
+    return pltpu.with_memory_space_constraint(x, pltpu.VMEM)
 
 
 def hbm(x):
@@ -161,55 +165,62 @@
     return bf16(jnp.where(r == place, 1.0, 0.0)), bf16(jnp.where(r == place + SLOTS, 1.0, 0.0))
 
 
-def unpack(recv_ref, x_ref, g_ref, copies=None):
+def unpack(recv_ref, x_ref, g_ref):
     pick_x, pick_g = picks()
     half, whole = pick_x.shape
     for n in range(x_ref.shape[0] // half):
-        if copies:
-            copies[n].wait()
         part = recv_ref[n * whole : (n + 1) * whole, :]
         x_ref[n * half : (n + 1) * half, :] = bf16(dot(pick_x, part))
         g_ref[n * half : (n + 1) * half, :] = bf16(dot(pick_g, part))
 
 
+def pack(rows, put, n):
+    half = put[0].shape[1]
+    part = bf16(rows[n * half : (n + 1) * half, :])
+    cut = part.shape[1] // 2
+    return bf16(dot(put[0], part[:, :cut]) + dot(put[1], part[:, cut:]))
+
+
+def puts():
+    half, whole = 128, 256
+    q, j = iota((whole, half), 0), iota((whole, half), 1)
+    home = (j // SLOTS) * PAIR + j % SLOTS
+    return bf16(jnp.where(q == home, 1.0, 0.0)), bf16(jnp.where(q == home + SLOTS, 1.0, 0.0))
+
+
 TILE = 512
 
 
 def expert_kernel(
-    recv_hbm, win_hbm, wout_hbm,
-    back_hbm, act_hbm, dpre_hbm,
-    recv_ref, win_ref, wout_ref, x_ref, g_ref, act_ref, dpre_ref, result, d_rows,
-    row_sems, in_sems, out_sems,
+    recv_ref, win_ref, wout_ref,
+    back_hbm, x_hbm, g_hbm, act_hbm, dpre_hbm,
+    x_ref, g_ref, act_ref, dpre_ref, d_rows, back_ref, row_sems, back_sems, out_sems,
 ):
     rows = x_ref.shape[0]
     hidden = win_ref.shape[1]
     tiles = hidden // TILE
     half, whole = 128, 256
     groups = rows // half
-    arrivals, returns, loads, stores = [], [], [], []
+    returns, stores = [], []
     for n in range(groups):
         part = pl.ds(n * whole, whole)
-        arrivals.append(pltpu.make_async_copy(recv_hbm.at[part, :], recv_ref.at[part, :], row_sems.at[0, n]))
-        returns.append(pltpu.make_async_copy(recv_ref.at[part, :], back_hbm.at[part, :], row_sems.at[1, n]))
-        arrivals[n].start()
+        returns.append(pltpu.make_async_copy(back_ref.at[part, :], back_hbm.at[part, :], back_sems.at[n]))
     for n in range(tiles):
         cols = pl.ds(n * TILE, TILE)
-        loads.append((
-            pltpu.make_async_copy(win_hbm.at[:, cols], win_ref.at[:, cols], in_sems.at[0, n]),
-            pltpu.make_async_copy(wout_hbm.at[cols, :], wout_ref.at[cols, :], in_sems.at[1, n]),
-        ))
         stores.append((
             pltpu.make_async_copy(act_ref.at[:, cols], act_hbm.at[:, cols], out_sems.at[0, n]),
             pltpu.make_async_copy(dpre_ref.at[:, cols], dpre_hbm.at[:, cols], out_sems.at[1, n]),
         ))
-        for copy in loads[n]:
-            copy.start()
-    unpack(recv_ref, x_ref, g_ref, arrivals)
+    unpack(recv_ref, x_ref, g_ref)
+    stores.append((
+        pltpu.make_async_copy(x_ref, x_hbm, row_sems.at[0]),
+        pltpu.make_async_copy(g_ref, g_hbm, row_sems.at[1]),
+    ))
+    for copy in stores[tiles]:
+        copy.start()
 
     def front(n):
         cols = slice(n * TILE, (n + 1) * TILE)
-        for copy in loads[n]:
-            copy.wait()
         return (
             dot(x_ref[...], win_ref[:, cols]),
             dot(g_ref[...], wout_ref[cols, :], ((1,), (1,))),
@@ -223,27 +234,16 @@
             ready = front(n + 1)
         gate = 0.5 * jnp.tanh(0.5 * pre) + 0.5
         value = pre * gate
-        act = bf16(value)
         d_pre = bf16(d_act * (gate + value * (1.0 - gate)))
-        act_ref[:, cols] = act
+        act_ref[:, cols] = bf16(value)
         dpre_ref[:, cols] = d_pre
         for copy in stores[n]:
             copy.start()
-        forward = dot(act, wout_ref[cols, :])
         backward = dot(d_pre, win_ref[:, cols], ((1,), (1,)))
-        if n:
-            forward, backward = forward + result[...], backward + d_rows[...]
-        result[...] = forward
-        d_rows[...] = backward
-    q, j = iota((whole, half), 0), iota((whole, half), 1)
-    home = (j // SLOTS) * PAIR + j % SLOTS
-    put_x = bf16(jnp.where(q == home, 1.0, 0.0))
-    put_g = bf16(jnp.where(q == home + SLOTS, 1.0, 0.0))
+        d_rows[...] = backward + d_rows[...] if n else backward
+    put = puts()
     for n in range(groups):
-        part = slice(n * half, (n + 1) * half)
-        recv_ref[n * whole : (n + 1) * whole, :] = bf16(
-            dot(put_x, bf16(result[part, :])) + dot(put_g, bf16(d_rows[part, :]))
-        )
+        back_ref[n * whole : (n + 1) * whole, :] = pack(d_rows, put, n)
         returns[n].start()
     for pair in stores:
         for copy in pair:
@@ -252,21 +252,59 @@
         copy.wait()
 
 
-def grads_kernel(recv_ref, act_ref, dpre_ref, gin_ref, gout_ref, done_ref, x_ref, g_ref):
-    @pl.when(pl.program_id(0) == 0)
-    def _():
-        unpack(recv_ref, x_ref, g_ref)
-
+def rest_kernel(x_ref, g_ref, act_ref, dpre_ref, wout_ref, gin_ref, gout_ref, back_ref, result):
+    n = pl.program_id(0)
     gin_ref[0] = bf16(dot(x_ref[...], dpre_ref[...], ((0,), (0,))))
     gout_ref[0] = bf16(dot(act_ref[...], g_ref[...], ((0,), (0,))))
-    done_ref[...] = jnp.zeros_like(done_ref)
+    forward = dot(act_ref[...], wout_ref[...])
+
+    @pl.when(n == 0)
+    def _():
+        result[...] = forward
+
+    @pl.when(n > 0)
+    def _():
+        result[...] += forward
+
+    @pl.when(n == pl.num_programs(0) - 1)
+    def _():
+        put = puts()
+        half, whole = 128, 256
+        for m in range(result.shape[0] // half):
+            back_ref[m * whole : (m + 1) * whole, :] = pack(result, put, m)
+
+
+def picked_by(key, seats):
+    seat = iota((key.shape[0], seats), 1)
+    return bf16(jnp.where(seat == key, 1.0, 0.0)), bf16(jnp.where(seat == key + SLOTS, 1.0, 0.0))
+
+
+def out_kernel(nv_ref, key_ref, recv_hbm, conv_hbm, tie_ref, out_ref, recv_ref, conv_ref, sems):
+    copies = [
+        pltpu.make_async_copy(src, dst, sems.at[i])
+        for i, (src, dst) in enumerate(((recv_hbm, recv_ref), (conv_hbm, conv_ref)))
+    ]
+    for copy in copies:
+        copy.start()
+    count, width = out_ref.shape
+    picked = picked_by(key_ref[:, 0:1], recv_ref.shape[0])
+    inside = iota((count, LANES), 0) < nv_ref[0]
+    for copy in copies:
+        copy.wait()
+    half = width // 2
+    for n in range(2):
+        back = dot(picked[n], recv_ref[...])
+        for i in range(half // LANES):
+            c = n * (half // LANES) + i
+            rows = back[:, i * LANES : (i + 1) * LANES]
+            out_ref[:, c * LANES : (c + 1) * LANES] = bf16(conv_ref[c] + jnp.where(inside, rows, 0.0))
 
 
 def post_kernel(
-    nv_ref, row_hbm, recv_hbm, cot_hbm, inv_hbm, conv_hbm, taps_hbm, pad_hbm, done_ref,
-    out_ref, dconv_ref, head_ref, tail_ref, mine_ref, other_ref,
+    nv_ref, row_hbm, recv_hbm, cot_hbm, inv_hbm, conv_hbm, taps_hbm, pad_hbm, tie_ref,
+    dconv_ref, head_ref, tail_ref, mine_ref, other_ref, key_ref,
     row_ref, recv_ref, cot_ref, inv_ref, conv_ref, taps_ref, pad_ref,
-    back, dhid, means, sums_ref, sems,
+    dhid, means, sums_ref, sems,
 ):
     copies = [
         pltpu.make_async_copy(src, dst, sems.at[i])
@@ -283,22 +321,20 @@
     chunks = width // LANES
     kernel = sums_ref.shape[0] - 1
     reach = (kernel - 1) // 2
-    here, there = iota((count, count), 0), iota((count, count), 1)
     copies[0].wait()
     row = row_ref[...]
+    here, there = iota((count, count), 0), iota((count, count), 1)
     col = jnp.sum(jnp.where(here == there, f32(row), 0.0), axis=1, keepdims=True).astype(jnp.int32)
     earlier = (col == row) & (there < here)
     slot = jnp.sum(jnp.where(earlier, 1.0, 0.0), axis=1, keepdims=True).astype(jnp.int32)
     key = col * PAIR + slot
-    seats = iota((count, recv_ref.shape[0]), 1)
-    pick_grad = bf16(jnp.where(seats == key + SLOTS, 1.0, 0.0))
-    pick_out = bf16(jnp.where(seats == key, 1.0, 0.0))
+    key_ref[...] = jnp.broadcast_to(key, key_ref.shape)
+    picked = picked_by(key, recv_ref.shape[0])
     copies[1].wait()
-    dhid[...] = dot(pick_grad, recv_ref[...])
-    back[...] = dot(pick_out, recv_ref[...])
+    for n in range(2):
+        dhid[:, n * (width // 2) : (n + 1) * (width // 2)] = dot(picked[n], recv_ref[...])
     for copy in copies[2:]:
         copy.wait()
-    inside = iota((count, LANES), 0) < nv_ref[0]
     inv = inv_ref[...]
     means[...] = jnp.zeros_like(means)
     for c in range(chunks):
@@ -307,7 +343,6 @@
         d_hidden = dhid[:, lanes]
         means[...] += d_hidden * taps_ref[c, kernel : kernel + 1, :] * normed
         sums_ref[kernel : kernel + 1, lanes] = jnp.sum(d_hidden * normed, axis=0, keepdims=True)
-        out_ref[:, lanes] = bf16(conv_ref[c] + jnp.where(inside, back[:, lanes], 0.0))
     mean = jnp.sum(means[...], axis=-1, keepdims=True) * (1.0 / width)
     mean = jnp.broadcast_to(mean, (count, LANES))
     for c in range(chunks):
@@ -364,7 +399,8 @@
             grad_ref[start : start + ROWS, lanes] = bf16(jnp.where(keep, total, 0.0))
 
 
-def add_kernel(tie_ref, own_ref, one_ref, two_ref, three_ref, out_ref):
+def add_kernel(own_ref, one_ref, two_ref, three_ref, *refs):
+    out_ref = refs[-1]
     out_ref[...] = (own_ref[...] + one_ref[...]) + (two_ref[...] + three_ref[...])
 
 
@@ -446,72 +482,71 @@
     )(scalars, left, right, conv, pad, squares, pick, grads, taps)
     recv = lax.all_to_all(send, ("rec", "tm"), split_axis=0, concat_axis=0, tiled=True)
     wide_rows = shape((rows, hidden), jnp.bfloat16)
-    back, act, d_pre = pl.pallas_call(
+    these = shape((rows, width), jnp.bfloat16)
+    halves = shape((2 * rows, width // 2), jnp.bfloat16)
+    tiles = hidden // TILE
+    back, rows_x, rows_g, act, d_pre = pl.pallas_call(
         expert_kernel,
-        out_shape=[pltpu.HBM(v.shape, v.dtype) for v in (buffer, wide_rows, wide_rows)],
-        in_specs=[HBM] * 3,
-        out_specs=[HBM] * 3,
+        out_shape=[pltpu.HBM(v.shape, v.dtype) for v in (halves, these, these, wide_rows, wide_rows)],
+        in_specs=[VMEM] * 3,
+        out_specs=[HBM] * 5,
         scratch_shapes=[
-            pltpu.VMEM((2 * rows, width), jnp.bfloat16),
-            pltpu.VMEM((width, hidden), jnp.bfloat16),
-            pltpu.VMEM((hidden, width), jnp.bfloat16),
             pltpu.VMEM((rows, width), jnp.bfloat16),
             pltpu.VMEM((rows, width), jnp.bfloat16),
             pltpu.VMEM((rows, hidden), jnp.bfloat16),
             pltpu.VMEM((rows, hidden), jnp.bfloat16),
             pltpu.VMEM((rows, width), jnp.float32),
-            pltpu.VMEM((rows, width), jnp.float32),
-            pltpu.SemaphoreType.DMA((2, rows // 128)),
-            pltpu.SemaphoreType.DMA((2, hidden // TILE)),
-            pltpu.SemaphoreType.DMA((2, hidden // TILE)),
-        ],
-        compiler_params=limit(40),
-        cost_estimate=cost(8 * rows * width * hidden, 2 * 10**7),
+            pltpu.VMEM((2 * rows, width // 2), jnp.bfloat16),
+            pltpu.SemaphoreType.DMA((2,)),
+            pltpu.SemaphoreType.DMA((rows // 128,)),
+            pltpu.SemaphoreType.DMA((2, tiles)),
+        ],
+        compiler_params=limit(30),
+        cost_estimate=cost(6 * rows * width * hidden, 2 * 10**7),
         name="experts",
-    )(hbm(recv), win, wout)
+    )(recv, vmem(expert_in[0]), vmem(expert_out[0]))
     home = lax.all_to_all(back, ("rec", "tm"), split_axis=0, concat_axis=0, tiled=True)
-    grad_in, grad_out, done = pl.pallas_call(
-        grads_kernel,
-        grid=(hidden // TILE,),
+    grad_in, grad_out, back = pl.pallas_call(
+        rest_kernel,
+        grid=(tiles,),
         out_shape=[
             shape((1, width, hidden), jnp.bfloat16),
             shape((1, hidden, width), jnp.bfloat16),
-            shape((8, LANES), jnp.float32),
+            pltpu.HBM(halves.shape, halves.dtype),
         ],
         in_specs=[
-            pl.BlockSpec((2 * rows, width), lambda i: (0, 0)),
+            pl.BlockSpec((rows, width), lambda i: (0, 0)),
+            pl.BlockSpec((rows, width), lambda i: (0, 0)),
             pl.BlockSpec((rows, TILE), lambda i: (0, i)),
             pl.BlockSpec((rows, TILE), lambda i: (0, i)),
+            pl.BlockSpec((TILE, width), lambda i: (i, 0)),
         ],
         out_specs=[
             pl.BlockSpec((1, width, TILE), lambda i: (0, 0, i)),
             pl.BlockSpec((1, TILE, width), lambda i: (0, i, 0)),
-            pl.BlockSpec((8, LANES), lambda i: (0, 0)),
-        ],
-        scratch_shapes=[
-            pltpu.VMEM((rows, width), jnp.bfloat16),
-            pltpu.VMEM((rows, width), jnp.bfloat16),
-        ],
+            pl.BlockSpec((2 * rows, width // 2), lambda i: (0, 0)),
+        ],
+        scratch_shapes=[pltpu.VMEM((rows, width), jnp.float32)],
         compiler_params=limit(24),
-        cost_estimate=cost(4 * rows * width * hidden, 2 * 10**7),
+        cost_estimate=cost(6 * rows * width * hidden, 2 * 10**7),
         name="weight_grads",
-    )(hbm(recv), hbm(act), hbm(d_pre))
+    )(hbm(rows_x), hbm(rows_g), hbm(act), hbm(d_pre), wout)
+    home_out = lax.all_to_all(back, ("rec", "tm"), split_axis=0, concat_axis=0, tiled=True)
     edges = shape((chunks, EDGE, LANES), jnp.float32)
-    output, d_conv, head, tail, mine, other = pl.pallas_call(
+    d_conv, head, tail, mine, other, key = pl.pallas_call(
         post_kernel,
-        out_shape=[shape((count, width), jnp.bfloat16), wide, edges, edges, half, half],
+        out_shape=[wide, edges, edges, half, half, shape((count, LANES), jnp.int32)],
         in_specs=[SMEM] + [HBM] * 7 + [ANY],
         out_specs=[VMEM] * 6,
         scratch_shapes=[
             pltpu.VMEM((1, count), jnp.int32),
-            pltpu.VMEM((2 * rows, width), jnp.bfloat16),
+            pltpu.VMEM((2 * rows, width // 2), jnp.bfloat16),
             pltpu.VMEM((count, width), jnp.bfloat16),
             pltpu.VMEM((count, LANES), jnp.float32),
             pltpu.VMEM(wide.shape, jnp.float32),
             pltpu.VMEM((chunks, 32, LANES), jnp.float32),
             pltpu.VMEM(padded.shape, jnp.float32),
             pltpu.VMEM((count, width), jnp.float32),
-            pltpu.VMEM((count, width), jnp.float32),
             pltpu.VMEM((count, LANES), jnp.float32),
             pltpu.VMEM((kernel + 1, width), jnp.float32),
             pltpu.SemaphoreType.DMA((7,)),
@@ -519,7 +554,7 @@
         compiler_params=limit(24),
         cost_estimate=cost(10**9, 10**7),
         name="post",
-    )(scalars, row, hbm(home), cot, hbm(inv), hbm(conv), hbm(taps), hbm(pad), done)
+    )(scalars, row, home, cot, hbm(inv), hbm(conv), hbm(taps), hbm(pad), hbm(back))
     left, right = shifted(tail, head)
 
     def back_part(first, tie):
@@ -537,27 +572,50 @@
             name="conv_back",
         )(scalars, d_conv, left, right, taps, tie)
 
-    def add(part, others, tie):
+    def add(part, others, ties):
         return pl.pallas_call(
             add_kernel,
             out_shape=half,
-            in_specs=[ANY] + [VMEM] * 4,
+            in_specs=[VMEM] * 4 + [ANY] * len(ties),
             out_specs=VMEM,
             compiler_params=limit(4),
             name="ring_add",
-        )(tie, part, *others)
+        )(part, *others, *ties)
 
     n_rec, n_tm = lax.axis_size("rec"), lax.axis_size("tm")
     swap = [(i, i ^ 1) for i in range(n_tm)]
     part = mine + lax.ppermute(other, "tm", swap)
-    pieces = []
-    for axis, size, step in (("tm", n_tm, 2), ("rec", n_rec, 1), ("tm", n_tm, 8)):
+    def out(tie):
+        return pl.pallas_call(
+            out_kernel,
+            out_shape=shape((count, width), jnp.bfloat16),
+            in_specs=[SMEM, VMEM] + [HBM] * 2 + [ANY],
+            out_specs=VMEM,
+            scratch_shapes=[
+                pltpu.VMEM((2 * rows, width // 2), jnp.bfloat16),
+                pltpu.VMEM(wide.shape, jnp.float32),
+                pltpu.SemaphoreType.DMA((2,)),
+            ],
+            compiler_params=limit(16),
+            cost_estimate=cost(10**9, 4 * 10**6),
+            name="out",
+        )(scalars, key, home_out, hbm(conv), tie)
+
+    beside = (
+        lambda tie: [],
+        lambda tie: [back_part(0, tie), back_part(2, tie), back_part(4, tie)],
+        lambda tie: [out(tie)],
+    )
+    done = []
+    for (axis, size, step), work in zip((("tm", n_tm, 2), ("rec", n_rec, 1), ("tm", n_tm, 8)), beside):
         others = [
             lax.ppermute(part, axis, [(i, i ^ (step * flip)) for i in range(size)])
             for flip in (1, 2, 3)
         ]
-        pieces.append(back_part(2 * len(pieces), part))
-        part = add(part, others, pieces[-1])
+        ties = work(part)
+        done += ties
+        part = add(part, others, ties if len(done) <= 3 else [hbm(done[3])])
+    *pieces, output = done
     fellow = lax.ppermute(part, "tm", swap)
     grad_conv, grad_gain, grad_frames = pl.pallas_call(
         functools.partial(finish_kernel, 1.0 / math.sqrt(n_rec * n_tm * count)),

time: 141 us -> 133 us (0.943)
  waiting for transfers between devices: 18.3 us -> 4.33 us
  starting transfers between devices: 32.3 us -> 40.8 us
    all_to_all x1 -> x2, waiting for transfers between devices: 14.3 us -> 2.1 us  [local(): lax.all_to_all(back, ('rec', 'tm'), split_axis=0, concat_axis=0, tiled=True)]
    all_to_all x1 -> x2, starting transfers between devices: 4.38 us -> 12.4 us  [local(): lax.all_to_all(back, ('rec', 'tm'), split_axis=0, concat_axis=0, tiled=True)]
    pallas_call x1, Pallas kernels: 18 us -> 10.2 us  [local(): pl.pallas_call(expert_kernel, out_shape=[pltpu.HBM(v.shape, v.dtype) for...]
    pallas_call x5 -> x6, Pallas kernels: 17.9 us -> 24.5 us  [the longest x1 14.6 us: local(): pl.pallas_call(rest_kernel, grid=(tiles,), out_shape=[shape((1, width, hi...]
    ppermute x9, waiting for transfers between devices: 3.05 us -> 0.08 us  [local(): lax.ppermute(part, axis, [(i, i ^ step * flip) for i in range(size)])]
    ppermute x2, starting transfers between devices: 5.21 us -> 6.82 us  [shifted(): left = lax.ppermute(tail, 'tm', [(i, i + 1) for i in range(n - 1)])]
  transfers between devices with their start and end apart: 16 -> 17, of which waited for: 6 -> 5; matrix products, arithmetic and copies ran while one was open for 0% -> 0% of each run, Pallas kernels for 15% -> 26%
where the time goes in v3:
time: 133 us; the launch traced here: 132 us
  Pallas kernels  48.2 us (36%)
  starting transfers between devices  40.8 us (31%)
  blocking collectives  36.5 us (27%)
  waiting for transfers between devices  4.33 us (3%)
  between operations  1.58 us (1%)
    all_to_all x1, blocking collectives, local(): lax.all_to_all(send, ('rec', 'tm'), split_axis=0, concat_axis=0, tiled=True)  36.5 us
    pallas_call x1, Pallas kernels, local(): pl.pallas_call(rest_kernel, grid=(tiles,), out_shape=[shape((1, width, hi...  14.6 us
    all_to_all x2, starting transfers between devices, local(): lax.all_to_all(back, ('rec', 'tm'), split_axis=0, concat_axis=0, tiled=True)  12.4 us
    pallas_call x1, Pallas kernels, local(): pl.pallas_call(expert_kernel, out_shape=[pltpu.HBM(v.shape, v.dtype) for...  10.2 us
    ppermute x9, starting transfers between devices, local(): lax.ppermute(part, axis, [(i, i ^ step * flip) for i in range(size)])  10.1 us
    ppermute x2, starting transfers between devices, shifted(): left = lax.ppermute(tail, 'tm', [(i, i + 1) for i in range(n - 1)])  6.82 us
    pallas_call x1, Pallas kernels, local(): pl.pallas_call(post_kernel, out_shape=[wide, edges, edges, half, half, sh...  6.24 us
    pallas_call x1, Pallas kernels, local(): pl.pallas_call(pre_kernel, out_shape=[wide, padded, lane, shape((2 * rows...  5.94 us
  transfers between devices with their start and end apart: 17, of which 5 were waited for; matrix products, arithmetic and copies ran while one was open for 0% of the time, Pallas kernels for 26%

profile of v3, /device:TPU:1, one launch (start us, length us, event | category | flops | bytes accessed | tf_op | source)
XLA Modules:
  0.0 132.3 jit_solution(14022686969156296603)
XLA Ops:
  0.6 0.8 slice_bitcast_fusion
  1.4 3.3 %collective-permute-start.1 = (bf16[16,768]{1,0:T(8,128)(2,1)S(1)}, bf16[16,768]{1,0:T(8,128)(2,1)S(1)}, u32[]{:S(2)}, u32[]{:S(2)}) collective-permute-start(bf16[16,768]{1,0:T(8,128)(2,1)S(1)} %get-tuple-element.60), channel_id=1, source_target_pairs={{1,0},{2,1},{3,2},{4,3},{5,4},{6,5},{7,6},{8,7},{9,8},{10,9},{11,1... | collective-permute-start | bytes 73736 | tf_op jit(solution)/shard_map/ppermute | solution.py:425
  4.7 3.1 %collective-permute-start = (bf16[16,768]{1,0:T(8,128)(2,1)S(1)}, bf16[16,768]{1,0:T(8,128)(2,1)S(1)}, u32[]{:S(2)}, u32[]{:S(2)}) collective-permute-start(bf16[16,768]{1,0:T(8,128)(2,1)S(1)} %get-tuple-element.61), channel_id=1, source_target_pairs={{0,1},{1,2},{2,3},{3,4},{4,5},{5,6},{6,7},{7,8},{8,9},{9,10},{10,1... | collective-permute-start | bytes 73736 | tf_op jit(solution)/shard_map/ppermute | solution.py:424
  8.5 0.1 pad_add_fusion.nv_ref
  8.6 0.0 copy-start.6
  8.6 5.9 %pre.1 = (f32[6,384,128]{2,1,0:T(8,128)S(1)}, f32[6,416,128]{2,1,0:T(8,128)S(1)}, f32[384,128]{1,0:T(8,128)S(1)}, bf16[1024,384]{1,0:T(8,128)(2,1)S(1)}, bf16[10...) custom-call(s32[2]{0:T(128)S(1)} %pad_add_fusion.nv_ref, s32[1,384]{1,0:T(1,128)} %bitcast.34, ...), custom_call_target="tpu_custom_call" | custom-call | flops 6000000000 | bytes 20000000 | tf_op jit(solution)/shard_map/pre/pallas_call | solution.py:449
  14.5 0.0 copy-start.2
  14.5 0.0 collective-permute-done.1.right_ref
  14.5 0.0 collective-permute-done.left_ref
  14.5 0.0 copy-start.5
  14.6 1.9 %send.1 = (f32[6,384,128]{2,1,0:T(8,128)S(1)}, f32[6,416,128]{2,1,0:T(8,128)S(1)}, bf16[1024,768]{1,0:T(8,128)(2,1)S(1)}, f32[384,128]{1,0:T(8,128)S(1)}) custom-call(s32[2]{0:T(128)S(1)} %pad_add_fusion.nv_ref, bf16[16,768]{1,0:T(8,128)(2,1)S(1)} %collective-permute-done.left_ref, bf16[16,768]{1,0:T(8,128)(2,1)S(1)} %collective-permute-done.1.right_ref, ...), custom_call_target="tpu_custom_call" | custom-call | flops 1000000000 | bytes 10000000 | tf_op jit(solution)/shard_map/send/pallas_call | solution.py:470
  16.5 0.0 copy-done.2
  16.5 0.0 copy-start
  16.5 0.0 copy-start.1
  16.5 0.0 copy-start.4
  16.5 36.5 %all_to_all.33 = bf16[128,8,768]{2,1,0:T(8,128)(2,1)S(1)} all-to-all(bf16[128,8,768]{2,1,0:T(8,128)(2,1)S(1)} %bitcast.22), channel_id=1, replica_groups=mesh['rec'=4,'tm'=32] {'rec','tm'}, dimensions={0} | all-to-all | bytes 3145728 | tf_op jit(solution)/shard_map/all_to_all | solution.py:483
  53.0 0.0 copy-done
  53.0 0.0 copy-done.1
  53.0 0.0 copy-done.4
  53.0 0.0 copy-done.6
  53.0 0.0 copy-done.5
  53.1 10.2 %experts.1 = (bf16[1024,384]{1,0:T(8,128)(2,1)}, bf16[512,768]{1,0:T(8,128)(2,1)}, bf16[512,768]{1,0:T(8,128)(2,1)}, bf16[512,3072]{1,0:T(8,128)(2,1)}, bf16[512,3072]{1,0:T(8,128)(2,1)}) custom-call(bf16[1024,768]{1,0:T(8,128)(2,1)S(1)} %bitcast.23, bf16[768,3072]{1,0:T(8,128)(2,1)S(1)} %bitcast.25, bf16[3072,768]{1,0:T(8,128)(2,1)S(1)} %bitcast.27), custom_call_target="tpu_custom_call" | custom-call | flops 7247757312 | bytes 20000000 | tf_op jit(solution)/shard_map/experts/pallas_call | solution.py:488
  63.2 4.5 %all-to-all-start.1 = ((bf16[128,8,384]{2,1,0:T(8,128)(2,1)}), bf16[128,8,384]{2,1,0:T(8,128)(2,1)S(1)}, u32[]{:S(2)}, u32[]{:S(2)}) async-start(bf16[128,8,384]{2,1,0:T(8,128)(2,1)} %bitcast.29), calls=%async_computation.1 | async-start | bytes 1572864 | tf_op jit(solution)/shard_map/all_to_all | solution.py:508
  67.8 14.6 %weight_grads.1 = (bf16[1,768,3072]{2,1,0:T(8,128)(2,1)}, bf16[1,3072,768]{2,1,0:T(8,128)(2,1)}, bf16[1024,384]{1,0:T(8,128)(2,1)}) custom-call(bf16[512,768]{1,0:T(8,128)(2,1)} %get-tuple-element.44.x_ref, bf16[512,768]{1,0:T(8,128)(2,1)} %get-tuple-element.45.g_ref, bf16[512,3072]{1,0:T(8,128)(2,1)} %get-tuple-element.46.act_ref, ...), custom_call_target="tpu_custom_call" | custom-call | flops 7247757312 | bytes 20000000 | tf_op jit(solution)/shard_map/weight_grads/pallas_call | solution.py:509
  82.4 2.1 %all-to-all-done.1 = bf16[128,8,384]{2,1,0:T(8,128)(2,1)S(1)} async-done(((bf16[128,8,384]{2,1,0:T(8,128)(2,1)}), bf16[128,8,384]{2,1,0:T(8,128)(2,1)S(1)}, u32[]{:S(2)}, u32[]{:S(2)}) %all-to-all-start.1) | async-done | bytes 786464 | tf_op jit(solution)/shard_map/all_to_all | solution.py:508
  84.5 7.8 %all-to-all-start.2 = ((bf16[128,8,384]{2,1,0:T(8,128)(2,1)}), bf16[128,8,384]{2,1,0:T(8,128)(2,1)S(1)}, u32[]{:S(2)}, u32[]{:S(2)}) async-start(bf16[128,8,384]{2,1,0:T(8,128)(2,1)} %bitcast.28), calls=%async_computation.2 | async-start | bytes 1572864 | tf_op jit(solution)/shard_map/all_to_all | solution.py:534
  92.3 0.0 copy-start.3
  92.3 6.2 %post.1 = (f32[6,384,128]{2,1,0:T(8,128)S(1)}, f32[6,16,128]{2,1,0:T(8,128)S(1)}, f32[6,16,128]{2,1,0:T(8,128)S(1)}, f32[16,768]{1,0:T(8,128)S(1)}, f32[16,768]{1,0:T(8,128)S(1)}, /*index=5*/s32[384,128]{1,0:T(8,128)S(1)}) custom-call(s32[2]{0:T(128)S(1)} %pad_add_fusion.nv_ref, s32[1,384]{1,0:T(1,128)} %bitcast.35, bf16[1024,384]{1,0:T(8,128)(2,1)S(1)} %bitcast.21, ...), custom_call_target="tpu_custom_call" | custom-call | flops 1000000000 | bytes 10000000 | tf_op jit(solution)/shard_map/post/pallas_call | solution.py:536
  98.6 1.1 collective-permute-start.2
  99.7 0.9 collective-permute-done.2
  100.6 2.0 %collective-permute-start.5 = (f32[16,768]{1,0:T(8,128)S(1)}, f32[16,768]{1,0:T(8,128)S(1)}, u32[]{:S(2)}, u32[]{:S(2)}) collective-permute-start(f32[16,768]{1,0:T(8,128)S(1)} %add.8.own_ref), channel_id=1, source_target_pairs={{0,6},{1,7},{2,4},{3,5},{4,2},{5,3},{6,0},{7,1},{8,14},{9,15},{10,... | collective-permute-start | bytes 147464 | tf_op jit(solution)/shard_map/ppermute | solution.py:612
  102.5 0.6 collective-permute-start.4
  103.1 0.7 collective-permute-start.3
  103.8 3.7 %collective-permute-start.9 = (f32[6,16,128]{2,1,0:T(8,128)S(1)}, f32[6,16,128]{2,1,0:T(8,128)S(1)}, u32[]{:S(2)}, u32[]{:S(2)}) collective-permute-start(f32[6,16,128]{2,1,0:T(8,128)S(1)} %get-tuple-element.53), channel_id=1, source_target_pairs={{0,1},{1,2},{2,3},{3,4},{4,5},{5,6},{6,7},{7,8},{8,9},{9,10},{10,1... | collective-permute-start | bytes 147464 | tf_op jit(solution)/shard_map/ppermute | solution.py:424
  107.6 1.9 %collective-permute-start.10 = (f32[6,16,128]{2,1,0:T(8,128)S(1)}, f32[6,16,128]{2,1,0:T(8,128)S(1)}, u32[]{:S(2)}, u32[]{:S(2)}) collective-permute-start(f32[6,16,128]{2,1,0:T(8,128)S(1)} %get-tuple-element.54), channel_id=1, source_target_pairs={{1,0},{2,1},{3,2},{4,3},{5,4},{6,5},{7,6},{8,7},{9,8},{10,9},{11,1... | collective-permute-start | bytes 147464 | tf_op jit(solution)/shard_map/ppermute | solution.py:425
  109.5 0.0 collective-permute-done.5.three_ref
  109.5 0.0 collective-permute-done.4.two_ref
  109.5 0.0 collective-permute-done.3.one_ref
  109.6 2.5 %collective-permute-start.8 = (f32[16,768]{1,0:T(8,128)S(1)}, f32[16,768]{1,0:T(8,128)S(1)}, u32[]{:S(2)}, u32[]{:S(2)}) collective-permute-start(f32[16,768]{1,0:T(8,128)S(1)} %ring_add.3.tie_ref.own_ref), channel_id=1, source_target_pairs={{0,96},{32,64},{64,32},{96,0},{1,97},{33,65},{65,33},{97,1},{2,98}... | collective-permute-start | bytes 147464 | tf_op jit(solution)/shard_map/ppermute | solution.py:612
  112.1 0.5 collective-permute-start.7
  112.6 0.3 collective-permute-start.6
  112.9 0.0 collective-permute-done.9.left_ref
  112.9 0.4 collective-permute-done.10.right_ref
  113.3 0.0 copy-done.3
  113.3 1.4 %conv_back.5.refs_2_ = bf16[384,256]{1,0:T(8,128)(2,1)S(1)} custom-call(s32[2]{0:T(128)S(1)} %pad_add_fusion.nv_ref, f32[6,384,128]{2,1,0:T(8,128)S(1)} %get-tuple-element.52.dconv_ref, f32[6,16,128]{2,1,0:T(8,128)S(1)} %collective-permute-done.9.left_ref, f32[6,16,128]{2,1,0:T(8,128)S(1)} %collective-permute-done.10.right_ref, f32[6,32,128]{2,1,0:T(8,128)S(1)} %copy-done.3, ...), custom_call_target="tpu_custom_call" | custom-call | flops 1000000000 | bytes 4000000 | tf_op jit(solution)/shard_map/conv_back/pallas_call | solution.py:561
  114.7 1.4 %conv_back.4.refs_1_ = bf16[384,256]{1,0:T(8,128)(2,1)S(1)} custom-call(s32[2]{0:T(128)S(1)} %pad_add_fusion.nv_ref, f32[6,384,128]{2,1,0:T(8,128)S(1)} %get-tuple-element.52.dconv_ref, f32[6,16,128]{2,1,0:T(8,128)S(1)} %collective-permute-done.9.left_ref, f32[6,16,128]{2,1,0:T(8,128)S(1)} %collective-permute-done.10.right_ref, f32[6,32,128]{2,1,0:T(8,128)S(1)} %copy-done.3, ...), custom_call_target="tpu_custom_call" | custom-call | flops 1000000000 | bytes 4000000 | tf_op jit(solution)/shard_map/conv_back/pallas_call | solution.py:561
  116.1 1.4 %conv_back.3.refs_0_ = bf16[384,256]{1,0:T(8,128)(2,1)S(1)} custom-call(s32[2]{0:T(128)S(1)} %pad_add_fusion.nv_ref, f32[6,384,128]{2,1,0:T(8,128)S(1)} %get-tuple-element.52.dconv_ref, f32[6,16,128]{2,1,0:T(8,128)S(1)} %collective-permute-done.9.left_ref, f32[6,16,128]{2,1,0:T(8,128)S(1)} %collective-permute-done.10.right_ref, f32[6,32,128]{2,1,0:T(8,128)S(1)} %copy-done.3, ...), custom_call_target="tpu_custom_call" | custom-call | flops 1000000000 | bytes 4000000 | tf_op jit(solution)/shard_map/conv_back/pallas_call | solution.py:561
  117.5 0.0 collective-permute-done.8.three_ref
  117.5 0.0 collective-permute-done.7.two_ref
  117.5 0.0 collective-permute-done.6.one_ref
  117.6 2.9 %collective-permute-start.13 = (f32[16,768]{1,0:T(8,128)S(1)}, f32[16,768]{1,0:T(8,128)S(1)}, u32[]{:S(2)}, u32[]{:S(2)}) collective-permute-start(f32[16,768]{1,0:T(8,128)S(1)} %ring_add.4.tie_ref.own_ref), channel_id=1, source_target_pairs={{0,24},{1,25},{2,26},{3,27},{4,28},{5,29},{6,30},{7,31},{8,16},{9,... | collective-permute-start | bytes 147464 | tf_op jit(solution)/shard_map/ppermute | solution.py:612
  120.4 0.1 collective-permute-start.12
  120.5 0.6 collective-permute-start.11
  121.1 0.0 all-to-all-done.2
  121.1 3.7 %out.1.refs_0_ = bf16[384,768]{1,0:T(8,128)(2,1)} custom-call(s32[2]{0:T(128)S(1)} %pad_add_fusion.nv_ref, s32[384,128]{1,0:T(8,128)S(1)} %get-tuple-element.49.key_ref, bf16[1024,384]{1,0:T(8,128)(2,1)S(1)} %bitcast.24, f32[6,384,128]{2,1,0:T(8,128)} %copy-done.1, f32[16,768]{1,0:T(8,128)S(1)} %ring_add.4.tie_ref.own_ref), custom_call_target="tpu_custom_call" | custom-call | flops 1000000000 | bytes 4000000 | tf_op jit(solution)/shard_map/out/pallas_call | solution.py:589
  124.8 0.0 collective-permute-done.13.three_ref
  124.8 0.1 collective-permute-done.12.two_ref
  124.9 0.0 collective-permute-done.11.one_ref
  124.9 5.1 %collective-permute-start.14 = (f32[16,768]{1,0:T(8,128)S(1)}, f32[16,768]{1,0:T(8,128)S(1)}, u32[]{:S(2)}, u32[]{:S(2)}) collective-permute-start(f32[16,768]{1,0:T(8,128)S(1)} %ring_add.5.part_ref), channel_id=1, source_target_pairs={{0,1},{1,0},{2,3},{3,2},{4,5},{5,4},{6,7},{7,6},{8,9},{9,8},{10,11... | collective-permute-start | bytes 147464 | tf_op jit(solution)/shard_map/ppermute | solution.py:619
  130.0 0.9 collective-permute-done.14.fellow_ref
  130.9 1.4 %finish.1 = (f32[31,768]{1,0:T(8,128)}, f32[768]{0:T(1024)}, bf16[384,768]{1,0:T(8,128)(2,1)}) custom-call(s32[2]{0:T(128)S(1)} %pad_add_fusion.nv_ref, f32[16,768]{1,0:T(8,128)S(1)} %ring_add.5.part_ref, f32[16,768]{1,0:T(8,128)S(1)} %collective-permute-done.14.fellow_ref, bf16[384,256]{1,0:T(8,128)(2,1)S(1)} %conv_back.3.refs_0_, ...), custom_call_target="tpu_custom_call" | custom-call | tf_op jit(solution)/shard_map/finish/pallas_call | solution.py:620
  (4 shorter events, 0.0 us)
Async XLA Ops:
  1.4 13.1 %collective-permute-start.1 = (bf16[16,768]{1,0:T(8,128)(2,1)S(1)}, bf16[16,768]{1,0:T(8,128)(2,1)S(1)}, u32[]{:S(2)}, u32[]{:S(2)}) collective-permute-start(bf16[16,768]{1,0:T(8,128)(2,1)S(1)} %get-tuple-element.60), channel_id=1, source_target_pairs={{1,0},{2,1},{3,2},{4,3},{5,4},{6,5},{7,6},{8,7},{9,8},{10,9},{11,1... | collective-permute-start | bytes 73736 | tf_op jit(solution)/shard_map/ppermute | solution.py:425
  4.7 9.8 %collective-permute-start = (bf16[16,768]{1,0:T(8,128)(2,1)S(1)}, bf16[16,768]{1,0:T(8,128)(2,1)S(1)}, u32[]{:S(2)}, u32[]{:S(2)}) collective-permute-start(bf16[16,768]{1,0:T(8,128)(2,1)S(1)} %get-tuple-element.61), channel_id=1, source_target_pairs={{0,1},{1,2},{2,3},{3,4},{4,5},{5,6},{6,7},{7,8},{8,9},{9,10},{10,1... | collective-permute-start | bytes 73736 | tf_op jit(solution)/shard_map/ppermute | solution.py:424
  8.6 44.5 %copy-start.6 = (bf16[1,3072,768]{2,1,0:T(8,128)(2,1)S(1)}, bf16[1,3072,768]{2,1,0:T(8,128)(2,1)}, u32[]{:S(2)}) copy-start(bf16[1,3072,768]{2,1,0:T(8,128)(2,1)} %param.15) | copy-start | bytes 14155780
  14.5 2.0 %copy-start.2 = (f32[6,32,128]{2,1,0:T(8,128)}, f32[6,32,128]{2,1,0:T(8,128)S(1)}, u32[]{:S(2)}) copy-start(f32[6,32,128]{2,1,0:T(8,128)S(1)} %get-tuple-element.38.taps_ref.taps_hbm) | copy-start | bytes 294916
  14.5 38.5 %copy-start.5 = (bf16[1,768,3072]{2,1,0:T(8,128)(2,1)S(1)}, bf16[1,768,3072]{2,1,0:T(8,128)(2,1)}, u32[]{:S(2)}) copy-start(bf16[1,768,3072]{2,1,0:T(8,128)(2,1)} %param.14) | copy-start | bytes 14155780
  16.5 36.5 %copy-start = (f32[6,416,128]{2,1,0:T(8,128)}, f32[6,416,128]{2,1,0:T(8,128)S(1)}, u32[]{:S(2)}) copy-start(f32[6,416,128]{2,1,0:T(8,128)S(1)} %get-tuple-element.43.pad_hbm) | copy-start | bytes 3833860
  16.5 36.5 %copy-start.1 = (f32[6,384,128]{2,1,0:T(8,128)}, f32[6,384,128]{2,1,0:T(8,128)S(1)}, u32[]{:S(2)}) copy-start(f32[6,384,128]{2,1,0:T(8,128)S(1)} %get-tuple-element.42.conv_hbm) | copy-start | bytes 3538948
  16.5 36.5 %copy-start.4 = (f32[384,128]{1,0:T(8,128)}, f32[384,128]{1,0:T(8,128)S(1)}, u32[]{:S(2)}) copy-start(f32[384,128]{1,0:T(8,128)S(1)} %get-tuple-element.41.inv_hbm) | copy-start | bytes 589828
  63.2 21.2 %all-to-all-start.1 = ((bf16[128,8,384]{2,1,0:T(8,128)(2,1)}), bf16[128,8,384]{2,1,0:T(8,128)(2,1)S(1)}, u32[]{:S(2)}, u32[]{:S(2)}) async-start(bf16[128,8,384]{2,1,0:T(8,128)(2,1)} %bitcast.29), calls=%async_computation.1 | async-start | bytes 1572864 | tf_op jit(solution)/shard_map/all_to_all | solution.py:508
  84.5 36.6 %all-to-all-start.2 = ((bf16[128,8,384]{2,1,0:T(8,128)(2,1)}), bf16[128,8,384]{2,1,0:T(8,128)(2,1)S(1)}, u32[]{:S(2)}, u32[]{:S(2)}) async-start(bf16[128,8,384]{2,1,0:T(8,128)(2,1)} %bitcast.28), calls=%async_computation.2 | async-start | bytes 1572864 | tf_op jit(solution)/shard_map/all_to_all | solution.py:534
  92.3 21.0 %copy-start.3 = (f32[6,32,128]{2,1,0:T(8,128)S(1)}, f32[6,32,128]{2,1,0:T(8,128)}, u32[]{:S(2)}) copy-start(f32[6,32,128]{2,1,0:T(8,128)} %copy-done.2) | copy-start | bytes 294916
  98.6 2.0 %collective-permute-start.2 = (f32[16,768]{1,0:T(8,128)S(1)}, f32[16,768]{1,0:T(8,128)S(1)}, u32[]{:S(2)}, u32[]{:S(2)}) collective-permute-start(f32[16,768]{1,0:T(8,128)S(1)} %get-tuple-element.51), channel_id=1, source_target_pairs={{0,1},{1,0},{2,3},{3,2},{4,5},{5,4},{6,7},{7,6},{8,9},{9,8},{10,11... | collective-permute-start | bytes 147464 | tf_op jit(solution)/shard_map/ppermute | solution.py:587
  100.6 8.9 %collective-permute-start.5 = (f32[16,768]{1,0:T(8,128)S(1)}, f32[16,768]{1,0:T(8,128)S(1)}, u32[]{:S(2)}, u32[]{:S(2)}) collective-permute-start(f32[16,768]{1,0:T(8,128)S(1)} %add.8.own_ref), channel_id=1, source_target_pairs={{0,6},{1,7},{2,4},{3,5},{4,2},{5,3},{6,0},{7,1},{8,14},{9,15},{10,... | collective-permute-start | bytes 147464 | tf_op jit(solution)/shard_map/ppermute | solution.py:612
  102.5 7.0 %collective-permute-start.4 = (f32[16,768]{1,0:T(8,128)S(1)}, f32[16,768]{1,0:T(8,128)S(1)}, u32[]{:S(2)}, u32[]{:S(2)}) collective-permute-start(f32[16,768]{1,0:T(8,128)S(1)} %add.8.own_ref), channel_id=1, source_target_pairs={{0,4},{1,5},{2,6},{3,7},{4,0},{5,1},{6,2},{7,3},{8,12},{9,13},{10,... | collective-permute-start | bytes 147464 | tf_op jit(solution)/shard_map/ppermute | solution.py:612
  103.1 6.4 %collective-permute-start.3 = (f32[16,768]{1,0:T(8,128)S(1)}, f32[16,768]{1,0:T(8,128)S(1)}, u32[]{:S(2)}, u32[]{:S(2)}) collective-permute-start(f32[16,768]{1,0:T(8,128)S(1)} %add.8.own_ref), channel_id=1, source_target_pairs={{0,2},{1,3},{2,0},{3,1},{4,6},{5,7},{6,4},{7,5},{8,10},{9,11},{10,... | collective-permute-start | bytes 147464 | tf_op jit(solution)/shard_map/ppermute | solution.py:612
  103.8 9.1 %collective-permute-start.9 = (f32[6,16,128]{2,1,0:T(8,128)S(1)}, f32[6,16,128]{2,1,0:T(8,128)S(1)}, u32[]{:S(2)}, u32[]{:S(2)}) collective-permute-start(f32[6,16,128]{2,1,0:T(8,128)S(1)} %get-tuple-element.53), channel_id=1, source_target_pairs={{0,1},{1,2},{2,3},{3,4},{4,5},{5,6},{6,7},{7,8},{8,9},{9,10},{10,1... | collective-permute-start | bytes 147464 | tf_op jit(solution)/shard_map/ppermute | solution.py:424
  107.6 5.7 %collective-permute-start.10 = (f32[6,16,128]{2,1,0:T(8,128)S(1)}, f32[6,16,128]{2,1,0:T(8,128)S(1)}, u32[]{:S(2)}, u32[]{:S(2)}) collective-permute-start(f32[6,16,128]{2,1,0:T(8,128)S(1)} %get-tuple-element.54), channel_id=1, source_target_pairs={{1,0},{2,1},{3,2},{4,3},{5,4},{6,5},{7,6},{8,7},{9,8},{10,9},{11,1... | collective-permute-start | bytes 147464 | tf_op jit(solution)/shard_map/ppermute | solution.py:425
  109.6 7.9 %collective-permute-start.8 = (f32[16,768]{1,0:T(8,128)S(1)}, f32[16,768]{1,0:T(8,128)S(1)}, u32[]{:S(2)}, u32[]{:S(2)}) collective-permute-start(f32[16,768]{1,0:T(8,128)S(1)} %ring_add.3.tie_ref.own_ref), channel_id=1, source_target_pairs={{0,96},{32,64},{64,32},{96,0},{1,97},{33,65},{65,33},{97,1},{2,98}... | collective-permute-start | bytes 147464 | tf_op jit(solution)/shard_map/ppermute | solution.py:612
  112.1 5.4 %collective-permute-start.7 = (f32[16,768]{1,0:T(8,128)S(1)}, f32[16,768]{1,0:T(8,128)S(1)}, u32[]{:S(2)}, u32[]{:S(2)}) collective-permute-start(f32[16,768]{1,0:T(8,128)S(1)} %ring_add.3.tie_ref.own_ref), channel_id=1, source_target_pairs={{0,64},{32,96},{64,0},{96,32},{1,65},{33,97},{65,1},{97,33},{2,66}... | collective-permute-start | bytes 147464 | tf_op jit(solution)/shard_map/ppermute | solution.py:612
  112.6 4.9 %collective-permute-start.6 = (f32[16,768]{1,0:T(8,128)S(1)}, f32[16,768]{1,0:T(8,128)S(1)}, u32[]{:S(2)}, u32[]{:S(2)}) collective-permute-start(f32[16,768]{1,0:T(8,128)S(1)} %ring_add.3.tie_ref.own_ref), channel_id=1, source_target_pairs={{0,32},{32,0},{64,96},{96,64},{1,33},{33,1},{65,97},{97,65},{2,34}... | collective-permute-start | bytes 147464 | tf_op jit(solution)/shard_map/ppermute | solution.py:612
  117.6 7.2 %collective-permute-start.13 = (f32[16,768]{1,0:T(8,128)S(1)}, f32[16,768]{1,0:T(8,128)S(1)}, u32[]{:S(2)}, u32[]{:S(2)}) collective-permute-start(f32[16,768]{1,0:T(8,128)S(1)} %ring_add.4.tie_ref.own_ref), channel_id=1, source_target_pairs={{0,24},{1,25},{2,26},{3,27},{4,28},{5,29},{6,30},{7,31},{8,16},{9,... | collective-permute-start | bytes 147464 | tf_op jit(solution)/shard_map/ppermute | solution.py:612
  120.4 4.4 %collective-permute-start.12 = (f32[16,768]{1,0:T(8,128)S(1)}, f32[16,768]{1,0:T(8,128)S(1)}, u32[]{:S(2)}, u32[]{:S(2)}) collective-permute-start(f32[16,768]{1,0:T(8,128)S(1)} %ring_add.4.tie_ref.own_ref), channel_id=1, source_target_pairs={{0,16},{1,17},{2,18},{3,19},{4,20},{5,21},{6,22},{7,23},{8,24},{9,... | collective-permute-start | bytes 147464 | tf_op jit(solution)/shard_map/ppermute | solution.py:612
  120.5 4.3 %collective-permute-start.11 = (f32[16,768]{1,0:T(8,128)S(1)}, f32[16,768]{1,0:T(8,128)S(1)}, u32[]{:S(2)}, u32[]{:S(2)}) collective-permute-start(f32[16,768]{1,0:T(8,128)S(1)} %ring_add.4.tie_ref.own_ref), channel_id=1, source_target_pairs={{0,8},{1,9},{2,10},{3,11},{4,12},{5,13},{6,14},{7,15},{8,0},{9,1},... | collective-permute-start | bytes 147464 | tf_op jit(solution)/shard_map/ppermute | solution.py:612
  124.9 6.0 %collective-permute-start.14 = (f32[16,768]{1,0:T(8,128)S(1)}, f32[16,768]{1,0:T(8,128)S(1)}, u32[]{:S(2)}, u32[]{:S(2)}) collective-permute-start(f32[16,768]{1,0:T(8,128)S(1)} %ring_add.5.part_ref), channel_id=1, source_target_pairs={{0,1},{1,0},{2,3},{3,2},{4,5},{5,4},{6,7},{7,6},{8,9},{9,8},{10,11... | collective-permute-start | bytes 147464 | tf_op jit(solution)/shard_map/ppermute | solution.py:619

commit v4 on v3

--- a/solution.py
+++ b/solution.py
@@ -53,7 +53,7 @@
 
 def pre_kernel(
     nv_ref, row_hbm, x_hbm, cot_hbm, w_hbm, gain_hbm,
-    conv_ref, pad_ref, squares_ref, pick_ref, send_ref, taps_ref,
+    conv_ref, pad_ref, squares_ref, pick_ref, send_ref, taps_ref, first_ref, last_ref,
     row_ref, x_ref, cot_ref, w_ref, gain_ref, grads, sems,
 ):
     count, width = x_ref.shape
@@ -76,6 +76,8 @@
     squares_ref[...] = jnp.zeros_like(squares_ref)
     for copy in copies[:3]:
         copy.wait()
+    first_ref[...] = x_ref[0:EDGE, :]
+    last_ref[...] = x_ref[count - EDGE :, :]
     for c in range(chunks):
         lanes = slice(c * LANES, (c + 1) * LANES)
         pad_ref[c, 0:EDGE, :] = jnp.zeros((EDGE, LANES), jnp.float32)
@@ -445,15 +447,16 @@
     lane = shape((count, LANES), jnp.float32)
     buffer = shape((2 * rows, width), jnp.bfloat16)
     half = shape(((kernel + 1) // 2, width), jnp.float32)
-    left, right = shifted(frames[0, count - EDGE :], frames[0, :EDGE])
-    conv, pad, squares, pick, grads, taps = pl.pallas_call(
+    conv, pad, squares, pick, grads, taps, first, last = pl.pallas_call(
         pre_kernel,
         out_shape=[
             wide, padded, lane, shape((2 * rows, count), jnp.bfloat16), buffer,
             shape((chunks, 32, LANES), jnp.float32),
+            shape((EDGE, width), jnp.bfloat16),
+            shape((EDGE, width), jnp.bfloat16),
         ],
         in_specs=[SMEM] + [HBM] * 5,
-        out_specs=[VMEM] * 6,
+        out_specs=[VMEM] * 8,
         scratch_shapes=[
             pltpu.VMEM((1, count), jnp.int32),
             pltpu.VMEM((count, width), jnp.bfloat16),
@@ -467,6 +470,7 @@
         cost_estimate=cost(6 * 10**9, 2 * 10**7),
         name="pre",
     )(scalars, row, x, cot, conv_weight, norm_gain)
+    left, right = shifted(last, first)
     conv, pad, send, inv = pl.pallas_call(
         send_kernel,
         out_shape=[wide, padded, buffer, lane],

time: 133 us -> 136 us (1.023)
  waiting for transfers between devices: 4.33 us -> 7.54 us
    ppermute x2, waiting for transfers between devices: 0.39 us -> 3.59 us  [shifted(): right = lax.ppermute(head, 'tm', [(i + 1, i) for i in range(n - 1)])]
    ppermute x2, starting transfers between devices: 6.82 us -> 8.23 us  [shifted(): left = lax.ppermute(tail, 'tm', [(i, i + 1) for i in range(n - 1)])]
    ppermute x2, starting transfers between devices: 5.24 us -> 3.84 us  [shifted(): right = lax.ppermute(head, 'tm', [(i + 1, i) for i in range(n - 1)])]
  transfers between devices with their start and end apart: 17 -> 17, of which waited for: 5 -> 6; matrix products, arithmetic and copies ran while one was open for 0% -> 0% of each run, Pallas kernels for 26% -> 21%
where the time goes in v4:
time: 136 us; the launch traced here: 135 us
  Pallas kernels  48.9 us (36%)
  starting transfers between devices  40.7 us (30%)
  blocking collectives  36.6 us (27%)
  waiting for transfers between devices  7.54 us (6%)
  between operations  1.55 us (1%)
    all_to_all x1, blocking collectives, local(): lax.all_to_all(send, ('rec', 'tm'), split_axis=0, concat_axis=0, tiled=True)  36.6 us
    pallas_call x1, Pallas kernels, local(): pl.pallas_call(rest_kernel, grid=(tiles,), out_shape=[shape((1, width, hi...  14.6 us
    all_to_all x2, starting transfers between devices, local(): lax.all_to_all(back, ('rec', 'tm'), split_axis=0, concat_axis=0, tiled=True)  12.3 us
    pallas_call x1, Pallas kernels, local(): pl.pallas_call(expert_kernel, out_shape=[pltpu.HBM(v.shape, v.dtype) for...  10.4 us
    ppermute x9, starting transfers between devices, local(): lax.ppermute(part, axis, [(i, i ^ step * flip) for i in range(size)])  10.1 us
    ppermute x2, starting transfers between devices, shifted(): left = lax.ppermute(tail, 'tm', [(i, i + 1) for i in range(n - 1)])  8.23 us
    pallas_call x1, Pallas kernels, local(): pl.pallas_call(post_kernel, out_shape=[wide, edges, edges, half, half, sh...  6.35 us
    pallas_call x1, Pallas kernels, local(): pl.pallas_call(pre_kernel, out_shape=[wide, padded, lane, shape((2 * rows...  6.04 us
  transfers between devices with their start and end apart: 17, of which 6 were waited for; matrix products, arithmetic and copies ran while one was open for 0% of the time, Pallas kernels for 21%

profile of v4, /device:TPU:1, one launch (start us, length us, event | category | flops | bytes accessed | tf_op | source)
XLA Modules:
  0.0 135.4 jit_solution(6489626202083436240)
XLA Ops:
  1.3 0.1 pad_add_fusion.nv_ref
  1.4 0.0 copy-start.6
  1.4 6.0 %pre.1 = (f32[6,384,128]{2,1,0:T(8,128)S(1)}, f32[6,416,128]{2,1,0:T(8,128)S(1)}, f32[384,128]{1,0:T(8,128)S(1)}, bf16[1024,384]{1,0:T(8,128)(2,1)S(1)}, bf16[10...) custom-call(s32[2]{0:T(128)S(1)} %pad_add_fusion.nv_ref, ...), custom_call_target="tpu_custom_call" | custom-call | flops 6000000000 | bytes 20000000 | tf_op jit(solution)/shard_map/pre/pallas_call | solution.py:450
  7.4 0.0 copy-start.2
  7.4 4.5 %collective-permute-start = (bf16[16,768]{1,0:T(8,128)(2,1)S(1)}, bf16[16,768]{1,0:T(8,128)(2,1)S(1)}, u32[]{:S(2)}, u32[]{:S(2)}) collective-permute-start(bf16[16,768]{1,0:T(8,128)(2,1)S(1)} %get-tuple-element.35), channel_id=1, source_target_pairs={{0,1},{1,2},{2,3},{3,4},{4,5},{5,6},{6,7},{7,8},{8,9},{9,10},{10,1... | collective-permute-start | bytes 73736 | tf_op jit(solution)/shard_map/ppermute | solution.py:426
  11.9 1.9 %collective-permute-start.1 = (bf16[16,768]{1,0:T(8,128)(2,1)S(1)}, bf16[16,768]{1,0:T(8,128)(2,1)S(1)}, u32[]{:S(2)}, u32[]{:S(2)}) collective-permute-start(bf16[16,768]{1,0:T(8,128)(2,1)S(1)} %get-tuple-element.36), channel_id=1, source_target_pairs={{1,0},{2,1},{3,2},{4,3},{5,4},{6,5},{7,6},{8,7},{9,8},{10,9},{11,1... | collective-permute-start | bytes 73736 | tf_op jit(solution)/shard_map/ppermute | solution.py:427
  13.9 0.0 collective-permute-done.left_ref
  13.9 3.2 %collective-permute-done.1.right_ref = bf16[16,768]{1,0:T(8,128)(2,1)S(1)} collective-permute-done((bf16[16,768]{1,0:T(8,128)(2,1)S(1)}, bf16[16,768]{1,0:T(8,128)(2,1)S(1)}, u32[]{:S(2)}, u32[]{:S(2)}) %collective-permute-start.1) | collective-permute-done | bytes 24608 | tf_op jit(solution)/shard_map/ppermute | solution.py:427
  17.1 0.0 copy-start.5
  17.1 2.0 %send.1 = (f32[6,384,128]{2,1,0:T(8,128)S(1)}, f32[6,416,128]{2,1,0:T(8,128)S(1)}, bf16[1024,768]{1,0:T(8,128)(2,1)S(1)}, f32[384,128]{1,0:T(8,128)S(1)}) custom-call(s32[2]{0:T(128)S(1)} %pad_add_fusion.nv_ref, bf16[16,768]{1,0:T(8,128)(2,1)S(1)} %collective-permute-done.left_ref, bf16[16,768]{1,0:T(8,128)(2,1)S(1)} %collective-permute-done.1.right_ref, ...), custom_call_target="tpu_custom_call" | custom-call | flops 1000000000 | bytes 10000000 | tf_op jit(solution)/shard_map/send/pallas_call | solution.py:474
  19.1 0.0 copy-done.2
  19.1 0.0 copy-start
  19.1 0.0 copy-start.1
  19.1 0.0 copy-start.4
  19.1 36.6 %all_to_all.33 = bf16[128,8,768]{2,1,0:T(8,128)(2,1)S(1)} all-to-all(bf16[128,8,768]{2,1,0:T(8,128)(2,1)S(1)} %bitcast.18), channel_id=1, replica_groups=mesh['rec'=4,'tm'=32] {'rec','tm'}, dimensions={0} | all-to-all | bytes 3145728 | tf_op jit(solution)/shard_map/all_to_all | solution.py:487
  55.7 0.0 copy-done
  55.7 0.0 copy-done.1
  55.7 0.0 copy-done.4
  55.7 0.0 copy-done.6
  55.7 0.0 copy-done.5
  55.7 10.4 %experts.1 = (bf16[1024,384]{1,0:T(8,128)(2,1)}, bf16[512,768]{1,0:T(8,128)(2,1)}, bf16[512,768]{1,0:T(8,128)(2,1)}, bf16[512,3072]{1,0:T(8,128)(2,1)}, bf16[512,3072]{1,0:T(8,128)(2,1)}) custom-call(bf16[1024,768]{1,0:T(8,128)(2,1)S(1)} %bitcast.19, bf16[768,3072]{1,0:T(8,128)(2,1)S(1)} %bitcast.21, bf16[3072,768]{1,0:T(8,128)(2,1)S(1)} %bitcast.23), custom_call_target="tpu_custom_call" | custom-call | flops 7247757312 | bytes 20000000 | tf_op jit(solution)/shard_map/experts/pallas_call | solution.py:492
  66.1 4.5 %all-to-all-start.1 = ((bf16[128,8,384]{2,1,0:T(8,128)(2,1)}), bf16[128,8,384]{2,1,0:T(8,128)(2,1)S(1)}, u32[]{:S(2)}, u32[]{:S(2)}) async-start(bf16[128,8,384]{2,1,0:T(8,128)(2,1)} %bitcast.25), calls=%async_computation.1 | async-start | bytes 1572864 | tf_op jit(solution)/shard_map/all_to_all | solution.py:512
  70.7 14.6 %weight_grads.1 = (bf16[1,768,3072]{2,1,0:T(8,128)(2,1)}, bf16[1,3072,768]{2,1,0:T(8,128)(2,1)}, bf16[1024,384]{1,0:T(8,128)(2,1)}) custom-call(bf16[512,768]{1,0:T(8,128)(2,1)} %get-tuple-element.48.x_ref, bf16[512,768]{1,0:T(8,128)(2,1)} %get-tuple-element.49.g_ref, bf16[512,3072]{1,0:T(8,128)(2,1)} %get-tuple-element.50.act_ref, ...), custom_call_target="tpu_custom_call" | custom-call | flops 7247757312 | bytes 20000000 | tf_op jit(solution)/shard_map/weight_grads/pallas_call | solution.py:513
  85.2 2.1 %all-to-all-done.1 = bf16[128,8,384]{2,1,0:T(8,128)(2,1)S(1)} async-done(((bf16[128,8,384]{2,1,0:T(8,128)(2,1)}), bf16[128,8,384]{2,1,0:T(8,128)(2,1)S(1)}, u32[]{:S(2)}, u32[]{:S(2)}) %all-to-all-start.1) | async-done | bytes 786464 | tf_op jit(solution)/shard_map/all_to_all | solution.py:512
  87.3 7.8 %all-to-all-start.2 = ((bf16[128,8,384]{2,1,0:T(8,128)(2,1)}), bf16[128,8,384]{2,1,0:T(8,128)(2,1)S(1)}, u32[]{:S(2)}, u32[]{:S(2)}) async-start(bf16[128,8,384]{2,1,0:T(8,128)(2,1)} %bitcast.24), calls=%async_computation.2 | async-start | bytes 1572864 | tf_op jit(solution)/shard_map/all_to_all | solution.py:538
  95.2 0.0 copy-start.3
  95.2 6.4 %post.1 = (f32[6,384,128]{2,1,0:T(8,128)S(1)}, f32[6,16,128]{2,1,0:T(8,128)S(1)}, f32[6,16,128]{2,1,0:T(8,128)S(1)}, f32[16,768]{1,0:T(8,128)S(1)}, f32[16,768]{1,0:T(8,128)S(1)}, /*index=5*/s32[384,128]{1,0:T(8,128)S(1)}) custom-call(s32[2]{0:T(128)S(1)} %pad_add_fusion.nv_ref, s32[1,384]{1,0:T(1,128)} %bitcast.30, bf16[1024,384]{1,0:T(8,128)(2,1)S(1)} %bitcast.17, ...), custom_call_target="tpu_custom_call" | custom-call | flops 1000000000 | bytes 10000000 | tf_op jit(solution)/shard_map/post/pallas_call | solution.py:540
  101.5 1.1 collective-permute-start.2
  102.7 0.9 collective-permute-done.2
  103.6 2.0 %collective-permute-start.5 = (f32[16,768]{1,0:T(8,128)S(1)}, f32[16,768]{1,0:T(8,128)S(1)}, u32[]{:S(2)}, u32[]{:S(2)}) collective-permute-start(f32[16,768]{1,0:T(8,128)S(1)} %add.8.own_ref), channel_id=1, source_target_pairs={{0,6},{1,7},{2,4},{3,5},{4,2},{5,3},{6,0},{7,1},{8,14},{9,15},{10,... | collective-permute-start | bytes 147464 | tf_op jit(solution)/shard_map/ppermute | solution.py:616
  105.5 0.6 collective-permute-start.4
  106.1 0.7 collective-permute-start.3
  106.8 3.7 %collective-permute-start.9 = (f32[6,16,128]{2,1,0:T(8,128)S(1)}, f32[6,16,128]{2,1,0:T(8,128)S(1)}, u32[]{:S(2)}, u32[]{:S(2)}) collective-permute-start(f32[6,16,128]{2,1,0:T(8,128)S(1)} %get-tuple-element.57), channel_id=1, source_target_pairs={{0,1},{1,2},{2,3},{3,4},{4,5},{5,6},{6,7},{7,8},{8,9},{9,10},{10,1... | collective-permute-start | bytes 147464 | tf_op jit(solution)/shard_map/ppermute | solution.py:426
  110.5 1.9 %collective-permute-start.10 = (f32[6,16,128]{2,1,0:T(8,128)S(1)}, f32[6,16,128]{2,1,0:T(8,128)S(1)}, u32[]{:S(2)}, u32[]{:S(2)}) collective-permute-start(f32[6,16,128]{2,1,0:T(8,128)S(1)} %get-tuple-element.58), channel_id=1, source_target_pairs={{1,0},{2,1},{3,2},{4,3},{5,4},{6,5},{7,6},{8,7},{9,8},{10,9},{11,1... | collective-permute-start | bytes 147464 | tf_op jit(solution)/shard_map/ppermute | solution.py:427
  112.5 0.0 collective-permute-done.5.three_ref
  112.5 0.0 collective-permute-done.4.two_ref
  112.5 0.0 collective-permute-done.3.one_ref
  112.5 2.5 %collective-permute-start.8 = (f32[16,768]{1,0:T(8,128)S(1)}, f32[16,768]{1,0:T(8,128)S(1)}, u32[]{:S(2)}, u32[]{:S(2)}) collective-permute-start(f32[16,768]{1,0:T(8,128)S(1)} %ring_add.3.tie_ref.own_ref), channel_id=1, source_target_pairs={{0,96},{32,64},{64,32},{96,0},{1,97},{33,65},{65,33},{97,1},{2,98}... | collective-permute-start | bytes 147464 | tf_op jit(solution)/shard_map/ppermute | solution.py:616
  115.1 0.5 collective-permute-start.7
  115.6 0.3 collective-permute-start.6
  115.9 0.0 collective-permute-done.9.left_ref
  115.9 0.4 collective-permute-done.10.right_ref
  116.3 0.0 copy-done.3
  116.3 1.5 %conv_back.5.refs_2_ = bf16[384,256]{1,0:T(8,128)(2,1)S(1)} custom-call(s32[2]{0:T(128)S(1)} %pad_add_fusion.nv_ref, f32[6,384,128]{2,1,0:T(8,128)S(1)} %get-tuple-element.56.dconv_ref, f32[6,16,128]{2,1,0:T(8,128)S(1)} %collective-permute-done.9.left_ref, f32[6,16,128]{2,1,0:T(8,128)S(1)} %collective-permute-done.10.right_ref, f32[6,32,128]{2,1,0:T(8,128)S(1)} %copy-done.3, ...), custom_call_target="tpu_custom_call" | custom-call | flops 1000000000 | bytes 4000000 | tf_op jit(solution)/shard_map/conv_back/pallas_call | solution.py:565
  117.7 1.5 %conv_back.4.refs_1_ = bf16[384,256]{1,0:T(8,128)(2,1)S(1)} custom-call(s32[2]{0:T(128)S(1)} %pad_add_fusion.nv_ref, f32[6,384,128]{2,1,0:T(8,128)S(1)} %get-tuple-element.56.dconv_ref, f32[6,16,128]{2,1,0:T(8,128)S(1)} %collective-permute-done.9.left_ref, f32[6,16,128]{2,1,0:T(8,128)S(1)} %collective-permute-done.10.right_ref, f32[6,32,128]{2,1,0:T(8,128)S(1)} %copy-done.3, ...), custom_call_target="tpu_custom_call" | custom-call | flops 1000000000 | bytes 4000000 | tf_op jit(solution)/shard_map/conv_back/pallas_call | solution.py:565
  119.2 1.5 %conv_back.3.refs_0_ = bf16[384,256]{1,0:T(8,128)(2,1)S(1)} custom-call(s32[2]{0:T(128)S(1)} %pad_add_fusion.nv_ref, f32[6,384,128]{2,1,0:T(8,128)S(1)} %get-tuple-element.56.dconv_ref, f32[6,16,128]{2,1,0:T(8,128)S(1)} %collective-permute-done.9.left_ref, f32[6,16,128]{2,1,0:T(8,128)S(1)} %collective-permute-done.10.right_ref, f32[6,32,128]{2,1,0:T(8,128)S(1)} %copy-done.3, ...), custom_call_target="tpu_custom_call" | custom-call | flops 1000000000 | bytes 4000000 | tf_op jit(solution)/shard_map/conv_back/pallas_call | solution.py:565
  120.6 0.0 collective-permute-done.8.three_ref
  120.6 0.0 collective-permute-done.7.two_ref
  120.7 0.0 collective-permute-done.6.one_ref
  120.7 2.9 %collective-permute-start.13 = (f32[16,768]{1,0:T(8,128)S(1)}, f32[16,768]{1,0:T(8,128)S(1)}, u32[]{:S(2)}, u32[]{:S(2)}) collective-permute-start(f32[16,768]{1,0:T(8,128)S(1)} %ring_add.4.tie_ref.own_ref), channel_id=1, source_target_pairs={{0,24},{1,25},{2,26},{3,27},{4,28},{5,29},{6,30},{7,31},{8,16},{9,... | collective-permute-start | bytes 147464 | tf_op jit(solution)/shard_map/ppermute | solution.py:616
  123.5 0.1 collective-permute-start.12
  123.7 0.6 collective-permute-start.11
  124.2 0.0 all-to-all-done.2
  124.2 3.7 %out.1.refs_0_ = bf16[384,768]{1,0:T(8,128)(2,1)} custom-call(s32[2]{0:T(128)S(1)} %pad_add_fusion.nv_ref, s32[384,128]{1,0:T(8,128)S(1)} %get-tuple-element.53.key_ref, bf16[1024,384]{1,0:T(8,128)(2,1)S(1)} %bitcast.20, f32[6,384,128]{2,1,0:T(8,128)} %copy-done.1, f32[16,768]{1,0:T(8,128)S(1)} %ring_add.4.tie_ref.own_ref), custom_call_target="tpu_custom_call" | custom-call | flops 1000000000 | bytes 4000000 | tf_op jit(solution)/shard_map/out/pallas_call | solution.py:593
  127.9 0.0 collective-permute-done.13.three_ref
  127.9 0.1 collective-permute-done.12.two_ref
  128.0 0.0 collective-permute-done.11.one_ref
  128.0 5.0 %collective-permute-start.14 = (f32[16,768]{1,0:T(8,128)S(1)}, f32[16,768]{1,0:T(8,128)S(1)}, u32[]{:S(2)}, u32[]{:S(2)}) collective-permute-start(f32[16,768]{1,0:T(8,128)S(1)} %ring_add.5.part_ref), channel_id=1, source_target_pairs={{0,1},{1,0},{2,3},{3,2},{4,5},{5,4},{6,7},{7,6},{8,9},{9,8},{10,11... | collective-permute-start | bytes 147464 | tf_op jit(solution)/shard_map/ppermute | solution.py:623
  133.0 0.9 collective-permute-done.14.fellow_ref
  133.9 1.4 %finish.1 = (f32[31,768]{1,0:T(8,128)}, f32[768]{0:T(1024)}, bf16[384,768]{1,0:T(8,128)(2,1)}) custom-call(s32[2]{0:T(128)S(1)} %pad_add_fusion.nv_ref, f32[16,768]{1,0:T(8,128)S(1)} %ring_add.5.part_ref, f32[16,768]{1,0:T(8,128)S(1)} %collective-permute-done.14.fellow_ref, bf16[384,256]{1,0:T(8,128)(2,1)S(1)} %conv_back.3.refs_0_, ...), custom_call_target="tpu_custom_call" | custom-call | tf_op jit(solution)/shard_map/finish/pallas_call | solution.py:624
  (4 shorter events, 0.0 us)
Async XLA Ops:
  1.4 54.3 %copy-start.6 = (bf16[1,3072,768]{2,1,0:T(8,128)(2,1)S(1)}, bf16[1,3072,768]{2,1,0:T(8,128)(2,1)}, u32[]{:S(2)}) copy-start(bf16[1,3072,768]{2,1,0:T(8,128)(2,1)} %param.15) | copy-start | bytes 14155780
  7.4 11.7 %copy-start.2 = (f32[6,32,128]{2,1,0:T(8,128)}, f32[6,32,128]{2,1,0:T(8,128)S(1)}, u32[]{:S(2)}) copy-start(f32[6,32,128]{2,1,0:T(8,128)S(1)} %get-tuple-element.42.taps_ref.taps_hbm) | copy-start | bytes 294916
  7.4 6.4 %collective-permute-start = (bf16[16,768]{1,0:T(8,128)(2,1)S(1)}, bf16[16,768]{1,0:T(8,128)(2,1)S(1)}, u32[]{:S(2)}, u32[]{:S(2)}) collective-permute-start(bf16[16,768]{1,0:T(8,128)(2,1)S(1)} %get-tuple-element.35), channel_id=1, source_target_pairs={{0,1},{1,2},{2,3},{3,4},{4,5},{5,6},{6,7},{7,8},{8,9},{9,10},{10,1... | collective-permute-start | bytes 73736 | tf_op jit(solution)/shard_map/ppermute | solution.py:426
  11.9 5.1 %collective-permute-start.1 = (bf16[16,768]{1,0:T(8,128)(2,1)S(1)}, bf16[16,768]{1,0:T(8,128)(2,1)S(1)}, u32[]{:S(2)}, u32[]{:S(2)}) collective-permute-start(bf16[16,768]{1,0:T(8,128)(2,1)S(1)} %get-tuple-element.36), channel_id=1, source_target_pairs={{1,0},{2,1},{3,2},{4,3},{5,4},{6,5},{7,6},{8,7},{9,8},{10,9},{11,1... | collective-permute-start | bytes 73736 | tf_op jit(solution)/shard_map/ppermute | solution.py:427
  17.1 38.6 %copy-start.5 = (bf16[1,768,3072]{2,1,0:T(8,128)(2,1)S(1)}, bf16[1,768,3072]{2,1,0:T(8,128)(2,1)}, u32[]{:S(2)}) copy-start(bf16[1,768,3072]{2,1,0:T(8,128)(2,1)} %param.14) | copy-start | bytes 14155780
  19.1 36.6 %copy-start = (f32[6,416,128]{2,1,0:T(8,128)}, f32[6,416,128]{2,1,0:T(8,128)S(1)}, u32[]{:S(2)}) copy-start(f32[6,416,128]{2,1,0:T(8,128)S(1)} %get-tuple-element.47.pad_hbm) | copy-start | bytes 3833860
  19.1 36.6 %copy-start.1 = (f32[6,384,128]{2,1,0:T(8,128)}, f32[6,384,128]{2,1,0:T(8,128)S(1)}, u32[]{:S(2)}) copy-start(f32[6,384,128]{2,1,0:T(8,128)S(1)} %get-tuple-element.46.conv_hbm) | copy-start | bytes 3538948
  19.1 36.6 %copy-start.4 = (f32[384,128]{1,0:T(8,128)}, f32[384,128]{1,0:T(8,128)S(1)}, u32[]{:S(2)}) copy-start(f32[384,128]{1,0:T(8,128)S(1)} %get-tuple-element.45.inv_hbm) | copy-start | bytes 589828
  66.1 21.2 %all-to-all-start.1 = ((bf16[128,8,384]{2,1,0:T(8,128)(2,1)}), bf16[128,8,384]{2,1,0:T(8,128)(2,1)S(1)}, u32[]{:S(2)}, u32[]{:S(2)}) async-start(bf16[128,8,384]{2,1,0:T(8,128)(2,1)} %bitcast.25), calls=%async_computation.1 | async-start | bytes 1572864 | tf_op jit(solution)/shard_map/all_to_all | solution.py:512
  87.3 36.9 %all-to-all-start.2 = ((bf16[128,8,384]{2,1,0:T(8,128)(2,1)}), bf16[128,8,384]{2,1,0:T(8,128)(2,1)S(1)}, u32[]{:S(2)}, u32[]{:S(2)}) async-start(bf16[128,8,384]{2,1,0:T(8,128)(2,1)} %bitcast.24), calls=%async_computation.2 | async-start | bytes 1572864 | tf_op jit(solution)/shard_map/all_to_all | solution.py:538
  95.2 21.1 %copy-start.3 = (f32[6,32,128]{2,1,0:T(8,128)S(1)}, f32[6,32,128]{2,1,0:T(8,128)}, u32[]{:S(2)}) copy-start(f32[6,32,128]{2,1,0:T(8,128)} %copy-done.2) | copy-start | bytes 294916
  101.5 2.0 %collective-permute-start.2 = (f32[16,768]{1,0:T(8,128)S(1)}, f32[16,768]{1,0:T(8,128)S(1)}, u32[]{:S(2)}, u32[]{:S(2)}) collective-permute-start(f32[16,768]{1,0:T(8,128)S(1)} %get-tuple-element.55), channel_id=1, source_target_pairs={{0,1},{1,0},{2,3},{3,2},{4,5},{5,4},{6,7},{7,6},{8,9},{9,8},{10,11... | collective-permute-start | bytes 147464 | tf_op jit(solution)/shard_map/ppermute | solution.py:591
  103.6 8.9 %collective-permute-start.5 = (f32[16,768]{1,0:T(8,128)S(1)}, f32[16,768]{1,0:T(8,128)S(1)}, u32[]{:S(2)}, u32[]{:S(2)}) collective-permute-start(f32[16,768]{1,0:T(8,128)S(1)} %add.8.own_ref), channel_id=1, source_target_pairs={{0,6},{1,7},{2,4},{3,5},{4,2},{5,3},{6,0},{7,1},{8,14},{9,15},{10,... | collective-permute-start | bytes 147464 | tf_op jit(solution)/shard_map/ppermute | solution.py:616
  105.5 7.0 %collective-permute-start.4 = (f32[16,768]{1,0:T(8,128)S(1)}, f32[16,768]{1,0:T(8,128)S(1)}, u32[]{:S(2)}, u32[]{:S(2)}) collective-permute-start(f32[16,768]{1,0:T(8,128)S(1)} %add.8.own_ref), channel_id=1, source_target_pairs={{0,4},{1,5},{2,6},{3,7},{4,0},{5,1},{6,2},{7,3},{8,12},{9,13},{10,... | collective-permute-start | bytes 147464 | tf_op jit(solution)/shard_map/ppermute | solution.py:616
  106.1 6.4 %collective-permute-start.3 = (f32[16,768]{1,0:T(8,128)S(1)}, f32[16,768]{1,0:T(8,128)S(1)}, u32[]{:S(2)}, u32[]{:S(2)}) collective-permute-start(f32[16,768]{1,0:T(8,128)S(1)} %add.8.own_ref), channel_id=1, source_target_pairs={{0,2},{1,3},{2,0},{3,1},{4,6},{5,7},{6,4},{7,5},{8,10},{9,11},{10,... | collective-permute-start | bytes 147464 | tf_op jit(solution)/shard_map/ppermute | solution.py:616
  106.8 9.1 %collective-permute-start.9 = (f32[6,16,128]{2,1,0:T(8,128)S(1)}, f32[6,16,128]{2,1,0:T(8,128)S(1)}, u32[]{:S(2)}, u32[]{:S(2)}) collective-permute-start(f32[6,16,128]{2,1,0:T(8,128)S(1)} %get-tuple-element.57), channel_id=1, source_target_pairs={{0,1},{1,2},{2,3},{3,4},{4,5},{5,6},{6,7},{7,8},{8,9},{9,10},{10,1... | collective-permute-start | bytes 147464 | tf_op jit(solution)/shard_map/ppermute | solution.py:426
  110.5 5.7 %collective-permute-start.10 = (f32[6,16,128]{2,1,0:T(8,128)S(1)}, f32[6,16,128]{2,1,0:T(8,128)S(1)}, u32[]{:S(2)}, u32[]{:S(2)}) collective-permute-start(f32[6,16,128]{2,1,0:T(8,128)S(1)} %get-tuple-element.58), channel_id=1, source_target_pairs={{1,0},{2,1},{3,2},{4,3},{5,4},{6,5},{7,6},{8,7},{9,8},{10,9},{11,1... | collective-permute-start | bytes 147464 | tf_op jit(solution)/shard_map/ppermute | solution.py:427
  112.5 8.1 %collective-permute-start.8 = (f32[16,768]{1,0:T(8,128)S(1)}, f32[16,768]{1,0:T(8,128)S(1)}, u32[]{:S(2)}, u32[]{:S(2)}) collective-permute-start(f32[16,768]{1,0:T(8,128)S(1)} %ring_add.3.tie_ref.own_ref), channel_id=1, source_target_pairs={{0,96},{32,64},{64,32},{96,0},{1,97},{33,65},{65,33},{97,1},{2,98}... | collective-permute-start | bytes 147464 | tf_op jit(solution)/shard_map/ppermute | solution.py:616
  115.1 5.6 %collective-permute-start.7 = (f32[16,768]{1,0:T(8,128)S(1)}, f32[16,768]{1,0:T(8,128)S(1)}, u32[]{:S(2)}, u32[]{:S(2)}) collective-permute-start(f32[16,768]{1,0:T(8,128)S(1)} %ring_add.3.tie_ref.own_ref), channel_id=1, source_target_pairs={{0,64},{32,96},{64,0},{96,32},{1,65},{33,97},{65,1},{97,33},{2,66}... | collective-permute-start | bytes 147464 | tf_op jit(solution)/shard_map/ppermute | solution.py:616
  115.6 5.1 %collective-permute-start.6 = (f32[16,768]{1,0:T(8,128)S(1)}, f32[16,768]{1,0:T(8,128)S(1)}, u32[]{:S(2)}, u32[]{:S(2)}) collective-permute-start(f32[16,768]{1,0:T(8,128)S(1)} %ring_add.3.tie_ref.own_ref), channel_id=1, source_target_pairs={{0,32},{32,0},{64,96},{96,64},{1,33},{33,1},{65,97},{97,65},{2,34}... | collective-permute-start | bytes 147464 | tf_op jit(solution)/shard_map/ppermute | solution.py:616
  120.7 7.2 %collective-permute-start.13 = (f32[16,768]{1,0:T(8,128)S(1)}, f32[16,768]{1,0:T(8,128)S(1)}, u32[]{:S(2)}, u32[]{:S(2)}) collective-permute-start(f32[16,768]{1,0:T(8,128)S(1)} %ring_add.4.tie_ref.own_ref), channel_id=1, source_target_pairs={{0,24},{1,25},{2,26},{3,27},{4,28},{5,29},{6,30},{7,31},{8,16},{9,... | collective-permute-start | bytes 147464 | tf_op jit(solution)/shard_map/ppermute | solution.py:616
  123.5 4.4 %collective-permute-start.12 = (f32[16,768]{1,0:T(8,128)S(1)}, f32[16,768]{1,0:T(8,128)S(1)}, u32[]{:S(2)}, u32[]{:S(2)}) collective-permute-start(f32[16,768]{1,0:T(8,128)S(1)} %ring_add.4.tie_ref.own_ref), channel_id=1, source_target_pairs={{0,16},{1,17},{2,18},{3,19},{4,20},{5,21},{6,22},{7,23},{8,24},{9,... | collective-permute-start | bytes 147464 | tf_op jit(solution)/shard_map/ppermute | solution.py:616
  123.7 4.3 %collective-permute-start.11 = (f32[16,768]{1,0:T(8,128)S(1)}, f32[16,768]{1,0:T(8,128)S(1)}, u32[]{:S(2)}, u32[]{:S(2)}) collective-permute-start(f32[16,768]{1,0:T(8,128)S(1)} %ring_add.4.tie_ref.own_ref), channel_id=1, source_target_pairs={{0,8},{1,9},{2,10},{3,11},{4,12},{5,13},{6,14},{7,15},{8,0},{9,1},... | collective-permute-start | bytes 147464 | tf_op jit(solution)/shard_map/ppermute | solution.py:616
  128.0 5.9 %collective-permute-start.14 = (f32[16,768]{1,0:T(8,128)S(1)}, f32[16,768]{1,0:T(8,128)S(1)}, u32[]{:S(2)}, u32[]{:S(2)}) collective-permute-start(f32[16,768]{1,0:T(8,128)S(1)} %ring_add.5.part_ref), channel_id=1, source_target_pairs={{0,1},{1,0},{2,3},{3,2},{4,5},{5,4},{6,7},{7,6},{8,9},{9,8},{10,11... | collective-permute-start | bytes 147464 | tf_op jit(solution)/shard_map/ppermute | solution.py:623

commit v5 on v3

--- a/solution.py
+++ b/solution.py
@@ -188,7 +188,7 @@
     return bf16(jnp.where(q == home, 1.0, 0.0)), bf16(jnp.where(q == home + SLOTS, 1.0, 0.0))
 
 
-TILE = 512
+TILE = 768
 
 
 def expert_kernel(

time: 133 us -> 132 us (level)
  no operation moved by 1% of the time
where the time goes in v5:
time: 132 us
  Pallas kernels  47.6 us (36%)
  starting transfers between devices  40.2 us (30%)
  blocking collectives  36.5 us (28%)
  waiting for transfers between devices  4.98 us (4%)
  between operations  1.58 us (1%)
    all_to_all x1, blocking collectives, local(): lax.all_to_all(send, ('rec', 'tm'), split_axis=0, concat_axis=0, tiled=True)  36.5 us
    pallas_call x1, Pallas kernels, local(): pl.pallas_call(rest_kernel, grid=(tiles,), out_shape=[shape((1, width, hi...  13.9 us
    all_to_all x2, starting transfers between devices, local(): lax.all_to_all(back, ('rec', 'tm'), split_axis=0, concat_axis=0, tiled=True)  11.7 us
    pallas_call x1, Pallas kernels, local(): pl.pallas_call(expert_kernel, out_shape=[pltpu.HBM(v.shape, v.dtype) for...  10.2 us
    ppermute x9, starting transfers between devices, local(): lax.ppermute(part, axis, [(i, i ^ step * flip) for i in range(size)])  10.1 us
    ppermute x2, starting transfers between devices, shifted(): left = lax.ppermute(tail, 'tm', [(i, i + 1) for i in range(n - 1)])  6.82 us
    pallas_call x1, Pallas kernels, local(): pl.pallas_call(post_kernel, out_shape=[wide, edges, edges, half, half, sh...  6.24 us
    pallas_call x1, Pallas kernels, local(): pl.pallas_call(pre_kernel, out_shape=[wide, padded, lane, shape((2 * rows...  5.94 us
  transfers between devices with their start and end apart: 17, of which 5 were waited for; matrix products, arithmetic and copies ran while one was open for 0% of the time, Pallas kernels for 26%

profile of v5, /device:TPU:1, one launch (start us, length us, event | category | flops | bytes accessed | tf_op | source)
XLA Modules:
  0.0 131.7 jit_solution(17406203780713495276)
XLA Ops:
  0.6 0.8 slice_bitcast_fusion
  1.4 3.3 %collective-permute-start.1 = (bf16[16,768]{1,0:T(8,128)(2,1)S(1)}, bf16[16,768]{1,0:T(8,128)(2,1)S(1)}, u32[]{:S(2)}, u32[]{:S(2)}) collective-permute-start(bf16[16,768]{1,0:T(8,128)(2,1)S(1)} %get-tuple-element.60), channel_id=1, source_target_pairs={{1,0},{2,1},{3,2},{4,3},{5,4},{6,5},{7,6},{8,7},{9,8},{10,9},{11,1... | collective-permute-start | bytes 73736 | tf_op jit(solution)/shard_map/ppermute | solution.py:425
  4.7 3.1 %collective-permute-start = (bf16[16,768]{1,0:T(8,128)(2,1)S(1)}, bf16[16,768]{1,0:T(8,128)(2,1)S(1)}, u32[]{:S(2)}, u32[]{:S(2)}) collective-permute-start(bf16[16,768]{1,0:T(8,128)(2,1)S(1)} %get-tuple-element.61), channel_id=1, source_target_pairs={{0,1},{1,2},{2,3},{3,4},{4,5},{5,6},{6,7},{7,8},{8,9},{9,10},{10,1... | collective-permute-start | bytes 73736 | tf_op jit(solution)/shard_map/ppermute | solution.py:424
  8.5 0.1 pad_add_fusion.nv_ref
  8.6 0.0 copy-start.6
  8.6 5.9 %pre.1 = (f32[6,384,128]{2,1,0:T(8,128)S(1)}, f32[6,416,128]{2,1,0:T(8,128)S(1)}, f32[384,128]{1,0:T(8,128)S(1)}, bf16[1024,384]{1,0:T(8,128)(2,1)S(1)}, bf16[10...) custom-call(s32[2]{0:T(128)S(1)} %pad_add_fusion.nv_ref, s32[1,384]{1,0:T(1,128)} %bitcast.34, ...), custom_call_target="tpu_custom_call" | custom-call | flops 6000000000 | bytes 20000000 | tf_op jit(solution)/shard_map/pre/pallas_call | solution.py:449
  14.5 0.0 copy-start.2
  14.5 0.0 collective-permute-done.1.right_ref
  14.5 0.0 collective-permute-done.left_ref
  14.5 0.0 copy-start.5
  14.6 1.9 %send.1 = (f32[6,384,128]{2,1,0:T(8,128)S(1)}, f32[6,416,128]{2,1,0:T(8,128)S(1)}, bf16[1024,768]{1,0:T(8,128)(2,1)S(1)}, f32[384,128]{1,0:T(8,128)S(1)}) custom-call(s32[2]{0:T(128)S(1)} %pad_add_fusion.nv_ref, bf16[16,768]{1,0:T(8,128)(2,1)S(1)} %collective-permute-done.left_ref, bf16[16,768]{1,0:T(8,128)(2,1)S(1)} %collective-permute-done.1.right_ref, ...), custom_call_target="tpu_custom_call" | custom-call | flops 1000000000 | bytes 10000000 | tf_op jit(solution)/shard_map/send/pallas_call | solution.py:470
  16.5 0.0 copy-done.2
  16.5 0.0 copy-start
  16.5 0.0 copy-start.1
  16.5 0.0 copy-start.4
  16.5 36.5 %all_to_all.33 = bf16[128,8,768]{2,1,0:T(8,128)(2,1)S(1)} all-to-all(bf16[128,8,768]{2,1,0:T(8,128)(2,1)S(1)} %bitcast.22), channel_id=1, replica_groups=mesh['rec'=4,'tm'=32] {'rec','tm'}, dimensions={0} | all-to-all | bytes 3145728 | tf_op jit(solution)/shard_map/all_to_all | solution.py:483
  53.0 0.0 copy-done
  53.0 0.0 copy-done.1
  53.0 0.0 copy-done.4
  53.0 0.0 copy-done.6
  53.0 0.0 copy-done.5
  53.1 10.2 %experts.1 = (bf16[1024,384]{1,0:T(8,128)(2,1)}, bf16[512,768]{1,0:T(8,128)(2,1)}, bf16[512,768]{1,0:T(8,128)(2,1)}, bf16[512,3072]{1,0:T(8,128)(2,1)}, bf16[512,3072]{1,0:T(8,128)(2,1)}) custom-call(bf16[1024,768]{1,0:T(8,128)(2,1)S(1)} %bitcast.23, bf16[768,3072]{1,0:T(8,128)(2,1)S(1)} %bitcast.25, bf16[3072,768]{1,0:T(8,128)(2,1)S(1)} %bitcast.27), custom_call_target="tpu_custom_call" | custom-call | flops 7247757312 | bytes 20000000 | tf_op jit(solution)/shard_map/experts/pallas_call | solution.py:488
  63.3 4.5 %all-to-all-start.1 = ((bf16[128,8,384]{2,1,0:T(8,128)(2,1)}), bf16[128,8,384]{2,1,0:T(8,128)(2,1)S(1)}, u32[]{:S(2)}, u32[]{:S(2)}) async-start(bf16[128,8,384]{2,1,0:T(8,128)(2,1)} %bitcast.29), calls=%async_computation.1 | async-start | bytes 1572864 | tf_op jit(solution)/shard_map/all_to_all | solution.py:508
  67.8 13.9 %weight_grads.1 = (bf16[1,768,3072]{2,1,0:T(8,128)(2,1)}, bf16[1,3072,768]{2,1,0:T(8,128)(2,1)}, bf16[1024,384]{1,0:T(8,128)(2,1)}) custom-call(bf16[512,768]{1,0:T(8,128)(2,1)} %get-tuple-element.44.x_ref, bf16[512,768]{1,0:T(8,128)(2,1)} %get-tuple-element.45.g_ref, bf16[512,3072]{1,0:T(8,128)(2,1)} %get-tuple-element.46.act_ref, ...), custom_call_target="tpu_custom_call" | custom-call | flops 7247757312 | bytes 20000000 | tf_op jit(solution)/shard_map/weight_grads/pallas_call | solution.py:509
  81.7 2.7 %all-to-all-done.1 = bf16[128,8,384]{2,1,0:T(8,128)(2,1)S(1)} async-done(((bf16[128,8,384]{2,1,0:T(8,128)(2,1)}), bf16[128,8,384]{2,1,0:T(8,128)(2,1)S(1)}, u32[]{:S(2)}, u32[]{:S(2)}) %all-to-all-start.1) | async-done | bytes 786464 | tf_op jit(solution)/shard_map/all_to_all | solution.py:508
  84.5 7.2 %all-to-all-start.2 = ((bf16[128,8,384]{2,1,0:T(8,128)(2,1)}), bf16[128,8,384]{2,1,0:T(8,128)(2,1)S(1)}, u32[]{:S(2)}, u32[]{:S(2)}) async-start(bf16[128,8,384]{2,1,0:T(8,128)(2,1)} %bitcast.28), calls=%async_computation.2 | async-start | bytes 1572864 | tf_op jit(solution)/shard_map/all_to_all | solution.py:534
  91.7 0.0 copy-start.3
  91.7 6.2 %post.1 = (f32[6,384,128]{2,1,0:T(8,128)S(1)}, f32[6,16,128]{2,1,0:T(8,128)S(1)}, f32[6,16,128]{2,1,0:T(8,128)S(1)}, f32[16,768]{1,0:T(8,128)S(1)}, f32[16,768]{1,0:T(8,128)S(1)}, /*index=5*/s32[384,128]{1,0:T(8,128)S(1)}) custom-call(s32[2]{0:T(128)S(1)} %pad_add_fusion.nv_ref, s32[1,384]{1,0:T(1,128)} %bitcast.35, bf16[1024,384]{1,0:T(8,128)(2,1)S(1)} %bitcast.21, ...), custom_call_target="tpu_custom_call" | custom-call | flops 1000000000 | bytes 10000000 | tf_op jit(solution)/shard_map/post/pallas_call | solution.py:536
  97.9 1.1 collective-permute-start.2
  99.1 0.9 collective-permute-done.2
  99.9 2.0 %collective-permute-start.5 = (f32[16,768]{1,0:T(8,128)S(1)}, f32[16,768]{1,0:T(8,128)S(1)}, u32[]{:S(2)}, u32[]{:S(2)}) collective-permute-start(f32[16,768]{1,0:T(8,128)S(1)} %add.8.own_ref), channel_id=1, source_target_pairs={{0,6},{1,7},{2,4},{3,5},{4,2},{5,3},{6,0},{7,1},{8,14},{9,15},{10,... | collective-permute-start | bytes 147464 | tf_op jit(solution)/shard_map/ppermute | solution.py:612
  101.9 0.6 collective-permute-start.4
  102.5 0.7 collective-permute-start.3
  103.2 3.7 %collective-permute-start.9 = (f32[6,16,128]{2,1,0:T(8,128)S(1)}, f32[6,16,128]{2,1,0:T(8,128)S(1)}, u32[]{:S(2)}, u32[]{:S(2)}) collective-permute-start(f32[6,16,128]{2,1,0:T(8,128)S(1)} %get-tuple-element.53), channel_id=1, source_target_pairs={{0,1},{1,2},{2,3},{3,4},{4,5},{5,6},{6,7},{7,8},{8,9},{9,10},{10,1... | collective-permute-start | bytes 147464 | tf_op jit(solution)/shard_map/ppermute | solution.py:424
  106.9 1.9 %collective-permute-start.10 = (f32[6,16,128]{2,1,0:T(8,128)S(1)}, f32[6,16,128]{2,1,0:T(8,128)S(1)}, u32[]{:S(2)}, u32[]{:S(2)}) collective-permute-start(f32[6,16,128]{2,1,0:T(8,128)S(1)} %get-tuple-element.54), channel_id=1, source_target_pairs={{1,0},{2,1},{3,2},{4,3},{5,4},{6,5},{7,6},{8,7},{9,8},{10,9},{11,1... | collective-permute-start | bytes 147464 | tf_op jit(solution)/shard_map/ppermute | solution.py:425
  108.9 0.0 collective-permute-done.5.three_ref
  108.9 0.0 collective-permute-done.4.two_ref
  108.9 0.0 collective-permute-done.3.one_ref
  108.9 2.5 %collective-permute-start.8 = (f32[16,768]{1,0:T(8,128)S(1)}, f32[16,768]{1,0:T(8,128)S(1)}, u32[]{:S(2)}, u32[]{:S(2)}) collective-permute-start(f32[16,768]{1,0:T(8,128)S(1)} %ring_add.3.tie_ref.own_ref), channel_id=1, source_target_pairs={{0,96},{32,64},{64,32},{96,0},{1,97},{33,65},{65,33},{97,1},{2,98}... | collective-permute-start | bytes 147464 | tf_op jit(solution)/shard_map/ppermute | solution.py:612
  111.5 0.5 collective-permute-start.7
  112.0 0.3 collective-permute-start.6
  112.2 0.0 collective-permute-done.9.left_ref
  112.3 0.4 collective-permute-done.10.right_ref
  112.6 0.0 copy-done.3
  112.6 1.4 %conv_back.5.refs_2_ = bf16[384,256]{1,0:T(8,128)(2,1)S(1)} custom-call(s32[2]{0:T(128)S(1)} %pad_add_fusion.nv_ref, f32[6,384,128]{2,1,0:T(8,128)S(1)} %get-tuple-element.52.dconv_ref, f32[6,16,128]{2,1,0:T(8,128)S(1)} %collective-permute-done.9.left_ref, f32[6,16,128]{2,1,0:T(8,128)S(1)} %collective-permute-done.10.right_ref, f32[6,32,128]{2,1,0:T(8,128)S(1)} %copy-done.3, ...), custom_call_target="tpu_custom_call" | custom-call | flops 1000000000 | bytes 4000000 | tf_op jit(solution)/shard_map/conv_back/pallas_call | solution.py:561
  114.0 1.4 %conv_back.4.refs_1_ = bf16[384,256]{1,0:T(8,128)(2,1)S(1)} custom-call(s32[2]{0:T(128)S(1)} %pad_add_fusion.nv_ref, f32[6,384,128]{2,1,0:T(8,128)S(1)} %get-tuple-element.52.dconv_ref, f32[6,16,128]{2,1,0:T(8,128)S(1)} %collective-permute-done.9.left_ref, f32[6,16,128]{2,1,0:T(8,128)S(1)} %collective-permute-done.10.right_ref, f32[6,32,128]{2,1,0:T(8,128)S(1)} %copy-done.3, ...), custom_call_target="tpu_custom_call" | custom-call | flops 1000000000 | bytes 4000000 | tf_op jit(solution)/shard_map/conv_back/pallas_call | solution.py:561
  115.5 1.4 %conv_back.3.refs_0_ = bf16[384,256]{1,0:T(8,128)(2,1)S(1)} custom-call(s32[2]{0:T(128)S(1)} %pad_add_fusion.nv_ref, f32[6,384,128]{2,1,0:T(8,128)S(1)} %get-tuple-element.52.dconv_ref, f32[6,16,128]{2,1,0:T(8,128)S(1)} %collective-permute-done.9.left_ref, f32[6,16,128]{2,1,0:T(8,128)S(1)} %collective-permute-done.10.right_ref, f32[6,32,128]{2,1,0:T(8,128)S(1)} %copy-done.3, ...), custom_call_target="tpu_custom_call" | custom-call | flops 1000000000 | bytes 4000000 | tf_op jit(solution)/shard_map/conv_back/pallas_call | solution.py:561
  116.9 0.0 collective-permute-done.8.three_ref
  116.9 0.0 collective-permute-done.7.two_ref
  116.9 0.0 collective-permute-done.6.one_ref
  116.9 2.9 %collective-permute-start.13 = (f32[16,768]{1,0:T(8,128)S(1)}, f32[16,768]{1,0:T(8,128)S(1)}, u32[]{:S(2)}, u32[]{:S(2)}) collective-permute-start(f32[16,768]{1,0:T(8,128)S(1)} %ring_add.4.tie_ref.own_ref), channel_id=1, source_target_pairs={{0,24},{1,25},{2,26},{3,27},{4,28},{5,29},{6,30},{7,31},{8,16},{9,... | collective-permute-start | bytes 147464 | tf_op jit(solution)/shard_map/ppermute | solution.py:612
  119.8 0.1 collective-permute-start.12
  119.9 0.6 collective-permute-start.11
  120.4 0.0 all-to-all-done.2
  120.4 3.7 %out.1.refs_0_ = bf16[384,768]{1,0:T(8,128)(2,1)} custom-call(s32[2]{0:T(128)S(1)} %pad_add_fusion.nv_ref, s32[384,128]{1,0:T(8,128)S(1)} %get-tuple-element.49.key_ref, bf16[1024,384]{1,0:T(8,128)(2,1)S(1)} %bitcast.24, f32[6,384,128]{2,1,0:T(8,128)} %copy-done.1, f32[16,768]{1,0:T(8,128)S(1)} %ring_add.4.tie_ref.own_ref), custom_call_target="tpu_custom_call" | custom-call | flops 1000000000 | bytes 4000000 | tf_op jit(solution)/shard_map/out/pallas_call | solution.py:589
  124.1 0.0 collective-permute-done.13.three_ref
  124.1 0.1 collective-permute-done.12.two_ref
  124.2 0.0 collective-permute-done.11.one_ref
  124.2 5.1 %collective-permute-start.14 = (f32[16,768]{1,0:T(8,128)S(1)}, f32[16,768]{1,0:T(8,128)S(1)}, u32[]{:S(2)}, u32[]{:S(2)}) collective-permute-start(f32[16,768]{1,0:T(8,128)S(1)} %ring_add.5.part_ref), channel_id=1, source_target_pairs={{0,1},{1,0},{2,3},{3,2},{4,5},{5,4},{6,7},{7,6},{8,9},{9,8},{10,11... | collective-permute-start | bytes 147464 | tf_op jit(solution)/shard_map/ppermute | solution.py:619
  129.4 0.9 collective-permute-done.14.fellow_ref
  130.3 1.4 %finish.1 = (f32[31,768]{1,0:T(8,128)}, f32[768]{0:T(1024)}, bf16[384,768]{1,0:T(8,128)(2,1)}) custom-call(s32[2]{0:T(128)S(1)} %pad_add_fusion.nv_ref, f32[16,768]{1,0:T(8,128)S(1)} %ring_add.5.part_ref, f32[16,768]{1,0:T(8,128)S(1)} %collective-permute-done.14.fellow_ref, bf16[384,256]{1,0:T(8,128)(2,1)S(1)} %conv_back.3.refs_0_, ...), custom_call_target="tpu_custom_call" | custom-call | tf_op jit(solution)/shard_map/finish/pallas_call | solution.py:620
  (4 shorter events, 0.0 us)
Async XLA Ops:
  1.4 13.1 %collective-permute-start.1 = (bf16[16,768]{1,0:T(8,128)(2,1)S(1)}, bf16[16,768]{1,0:T(8,128)(2,1)S(1)}, u32[]{:S(2)}, u32[]{:S(2)}) collective-permute-start(bf16[16,768]{1,0:T(8,128)(2,1)S(1)} %get-tuple-element.60), channel_id=1, source_target_pairs={{1,0},{2,1},{3,2},{4,3},{5,4},{6,5},{7,6},{8,7},{9,8},{10,9},{11,1... | collective-permute-start | bytes 73736 | tf_op jit(solution)/shard_map/ppermute | solution.py:425
  4.7 9.8 %collective-permute-start = (bf16[16,768]{1,0:T(8,128)(2,1)S(1)}, bf16[16,768]{1,0:T(8,128)(2,1)S(1)}, u32[]{:S(2)}, u32[]{:S(2)}) collective-permute-start(bf16[16,768]{1,0:T(8,128)(2,1)S(1)} %get-tuple-element.61), channel_id=1, source_target_pairs={{0,1},{1,2},{2,3},{3,4},{4,5},{5,6},{6,7},{7,8},{8,9},{9,10},{10,1... | collective-permute-start | bytes 73736 | tf_op jit(solution)/shard_map/ppermute | solution.py:424
  8.6 44.5 %copy-start.6 = (bf16[1,3072,768]{2,1,0:T(8,128)(2,1)S(1)}, bf16[1,3072,768]{2,1,0:T(8,128)(2,1)}, u32[]{:S(2)}) copy-start(bf16[1,3072,768]{2,1,0:T(8,128)(2,1)} %param.15) | copy-start | bytes 14155780
  14.5 2.0 %copy-start.2 = (f32[6,32,128]{2,1,0:T(8,128)}, f32[6,32,128]{2,1,0:T(8,128)S(1)}, u32[]{:S(2)}) copy-start(f32[6,32,128]{2,1,0:T(8,128)S(1)} %get-tuple-element.38.taps_ref.taps_hbm) | copy-start | bytes 294916
  14.5 38.5 %copy-start.5 = (bf16[1,768,3072]{2,1,0:T(8,128)(2,1)S(1)}, bf16[1,768,3072]{2,1,0:T(8,128)(2,1)}, u32[]{:S(2)}) copy-start(bf16[1,768,3072]{2,1,0:T(8,128)(2,1)} %param.14) | copy-start | bytes 14155780
  16.5 36.5 %copy-start = (f32[6,416,128]{2,1,0:T(8,128)}, f32[6,416,128]{2,1,0:T(8,128)S(1)}, u32[]{:S(2)}) copy-start(f32[6,416,128]{2,1,0:T(8,128)S(1)} %get-tuple-element.43.pad_hbm) | copy-start | bytes 3833860
  16.5 36.5 %copy-start.1 = (f32[6,384,128]{2,1,0:T(8,128)}, f32[6,384,128]{2,1,0:T(8,128)S(1)}, u32[]{:S(2)}) copy-start(f32[6,384,128]{2,1,0:T(8,128)S(1)} %get-tuple-element.42.conv_hbm) | copy-start | bytes 3538948
  16.5 36.5 %copy-start.4 = (f32[384,128]{1,0:T(8,128)}, f32[384,128]{1,0:T(8,128)S(1)}, u32[]{:S(2)}) copy-start(f32[384,128]{1,0:T(8,128)S(1)} %get-tuple-element.41.inv_hbm) | copy-start | bytes 589828
  63.3 21.2 %all-to-all-start.1 = ((bf16[128,8,384]{2,1,0:T(8,128)(2,1)}), bf16[128,8,384]{2,1,0:T(8,128)(2,1)S(1)}, u32[]{:S(2)}, u32[]{:S(2)}) async-start(bf16[128,8,384]{2,1,0:T(8,128)(2,1)} %bitcast.29), calls=%async_computation.1 | async-start | bytes 1572864 | tf_op jit(solution)/shard_map/all_to_all | solution.py:508
  84.5 36.0 %all-to-all-start.2 = ((bf16[128,8,384]{2,1,0:T(8,128)(2,1)}), bf16[128,8,384]{2,1,0:T(8,128)(2,1)S(1)}, u32[]{:S(2)}, u32[]{:S(2)}) async-start(bf16[128,8,384]{2,1,0:T(8,128)(2,1)} %bitcast.28), calls=%async_computation.2 | async-start | bytes 1572864 | tf_op jit(solution)/shard_map/all_to_all | solution.py:534
  91.7 21.0 %copy-start.3 = (f32[6,32,128]{2,1,0:T(8,128)S(1)}, f32[6,32,128]{2,1,0:T(8,128)}, u32[]{:S(2)}) copy-start(f32[6,32,128]{2,1,0:T(8,128)} %copy-done.2) | copy-start | bytes 294916
  97.9 2.0 %collective-permute-start.2 = (f32[16,768]{1,0:T(8,128)S(1)}, f32[16,768]{1,0:T(8,128)S(1)}, u32[]{:S(2)}, u32[]{:S(2)}) collective-permute-start(f32[16,768]{1,0:T(8,128)S(1)} %get-tuple-element.51), channel_id=1, source_target_pairs={{0,1},{1,0},{2,3},{3,2},{4,5},{5,4},{6,7},{7,6},{8,9},{9,8},{10,11... | collective-permute-start | bytes 147464 | tf_op jit(solution)/shard_map/ppermute | solution.py:587
  99.9 8.9 %collective-permute-start.5 = (f32[16,768]{1,0:T(8,128)S(1)}, f32[16,768]{1,0:T(8,128)S(1)}, u32[]{:S(2)}, u32[]{:S(2)}) collective-permute-start(f32[16,768]{1,0:T(8,128)S(1)} %add.8.own_ref), channel_id=1, source_target_pairs={{0,6},{1,7},{2,4},{3,5},{4,2},{5,3},{6,0},{7,1},{8,14},{9,15},{10,... | collective-permute-start | bytes 147464 | tf_op jit(solution)/shard_map/ppermute | solution.py:612
  101.9 7.0 %collective-permute-start.4 = (f32[16,768]{1,0:T(8,128)S(1)}, f32[16,768]{1,0:T(8,128)S(1)}, u32[]{:S(2)}, u32[]{:S(2)}) collective-permute-start(f32[16,768]{1,0:T(8,128)S(1)} %add.8.own_ref), channel_id=1, source_target_pairs={{0,4},{1,5},{2,6},{3,7},{4,0},{5,1},{6,2},{7,3},{8,12},{9,13},{10,... | collective-permute-start | bytes 147464 | tf_op jit(solution)/shard_map/ppermute | solution.py:612
  102.5 6.4 %collective-permute-start.3 = (f32[16,768]{1,0:T(8,128)S(1)}, f32[16,768]{1,0:T(8,128)S(1)}, u32[]{:S(2)}, u32[]{:S(2)}) collective-permute-start(f32[16,768]{1,0:T(8,128)S(1)} %add.8.own_ref), channel_id=1, source_target_pairs={{0,2},{1,3},{2,0},{3,1},{4,6},{5,7},{6,4},{7,5},{8,10},{9,11},{10,... | collective-permute-start | bytes 147464 | tf_op jit(solution)/shard_map/ppermute | solution.py:612
  103.2 9.1 %collective-permute-start.9 = (f32[6,16,128]{2,1,0:T(8,128)S(1)}, f32[6,16,128]{2,1,0:T(8,128)S(1)}, u32[]{:S(2)}, u32[]{:S(2)}) collective-permute-start(f32[6,16,128]{2,1,0:T(8,128)S(1)} %get-tuple-element.53), channel_id=1, source_target_pairs={{0,1},{1,2},{2,3},{3,4},{4,5},{5,6},{6,7},{7,8},{8,9},{9,10},{10,1... | collective-permute-start | bytes 147464 | tf_op jit(solution)/shard_map/ppermute | solution.py:424
  106.9 5.7 %collective-permute-start.10 = (f32[6,16,128]{2,1,0:T(8,128)S(1)}, f32[6,16,128]{2,1,0:T(8,128)S(1)}, u32[]{:S(2)}, u32[]{:S(2)}) collective-permute-start(f32[6,16,128]{2,1,0:T(8,128)S(1)} %get-tuple-element.54), channel_id=1, source_target_pairs={{1,0},{2,1},{3,2},{4,3},{5,4},{6,5},{7,6},{8,7},{9,8},{10,9},{11,1... | collective-permute-start | bytes 147464 | tf_op jit(solution)/shard_map/ppermute | solution.py:425
  108.9 7.9 %collective-permute-start.8 = (f32[16,768]{1,0:T(8,128)S(1)}, f32[16,768]{1,0:T(8,128)S(1)}, u32[]{:S(2)}, u32[]{:S(2)}) collective-permute-start(f32[16,768]{1,0:T(8,128)S(1)} %ring_add.3.tie_ref.own_ref), channel_id=1, source_target_pairs={{0,96},{32,64},{64,32},{96,0},{1,97},{33,65},{65,33},{97,1},{2,98}... | collective-permute-start | bytes 147464 | tf_op jit(solution)/shard_map/ppermute | solution.py:612
  111.5 5.4 %collective-permute-start.7 = (f32[16,768]{1,0:T(8,128)S(1)}, f32[16,768]{1,0:T(8,128)S(1)}, u32[]{:S(2)}, u32[]{:S(2)}) collective-permute-start(f32[16,768]{1,0:T(8,128)S(1)} %ring_add.3.tie_ref.own_ref), channel_id=1, source_target_pairs={{0,64},{32,96},{64,0},{96,32},{1,65},{33,97},{65,1},{97,33},{2,66}... | collective-permute-start | bytes 147464 | tf_op jit(solution)/shard_map/ppermute | solution.py:612
  112.0 4.9 %collective-permute-start.6 = (f32[16,768]{1,0:T(8,128)S(1)}, f32[16,768]{1,0:T(8,128)S(1)}, u32[]{:S(2)}, u32[]{:S(2)}) collective-permute-start(f32[16,768]{1,0:T(8,128)S(1)} %ring_add.3.tie_ref.own_ref), channel_id=1, source_target_pairs={{0,32},{32,0},{64,96},{96,64},{1,33},{33,1},{65,97},{97,65},{2,34}... | collective-permute-start | bytes 147464 | tf_op jit(solution)/shard_map/ppermute | solution.py:612
  116.9 7.2 %collective-permute-start.13 = (f32[16,768]{1,0:T(8,128)S(1)}, f32[16,768]{1,0:T(8,128)S(1)}, u32[]{:S(2)}, u32[]{:S(2)}) collective-permute-start(f32[16,768]{1,0:T(8,128)S(1)} %ring_add.4.tie_ref.own_ref), channel_id=1, source_target_pairs={{0,24},{1,25},{2,26},{3,27},{4,28},{5,29},{6,30},{7,31},{8,16},{9,... | collective-permute-start | bytes 147464 | tf_op jit(solution)/shard_map/ppermute | solution.py:612
  119.8 4.4 %collective-permute-start.12 = (f32[16,768]{1,0:T(8,128)S(1)}, f32[16,768]{1,0:T(8,128)S(1)}, u32[]{:S(2)}, u32[]{:S(2)}) collective-permute-start(f32[16,768]{1,0:T(8,128)S(1)} %ring_add.4.tie_ref.own_ref), channel_id=1, source_target_pairs={{0,16},{1,17},{2,18},{3,19},{4,20},{5,21},{6,22},{7,23},{8,24},{9,... | collective-permute-start | bytes 147464 | tf_op jit(solution)/shard_map/ppermute | solution.py:612
  119.9 4.3 %collective-permute-start.11 = (f32[16,768]{1,0:T(8,128)S(1)}, f32[16,768]{1,0:T(8,128)S(1)}, u32[]{:S(2)}, u32[]{:S(2)}) collective-permute-start(f32[16,768]{1,0:T(8,128)S(1)} %ring_add.4.tie_ref.own_ref), channel_id=1, source_target_pairs={{0,8},{1,9},{2,10},{3,11},{4,12},{5,13},{6,14},{7,15},{8,0},{9,1},... | collective-permute-start | bytes 147464 | tf_op jit(solution)/shard_map/ppermute | solution.py:612
  124.2 6.0 %collective-permute-start.14 = (f32[16,768]{1,0:T(8,128)S(1)}, f32[16,768]{1,0:T(8,128)S(1)}, u32[]{:S(2)}, u32[]{:S(2)}) collective-permute-start(f32[16,768]{1,0:T(8,128)S(1)} %ring_add.5.part_ref), channel_id=1, source_target_pairs={{0,1},{1,0},{2,3},{3,2},{4,5},{5,4},{6,7},{7,6},{8,9},{9,8},{10,11... | collective-permute-start | bytes 147464 | tf_op jit(solution)/shard_map/ppermute | solution.py:619
